TPU v7x, 32 devices: a whole 2x2x4 slice. The times are simulated.
32 devices in a mesh: dp: 2 (over y), mp: 16 (over z, x, core).
Axes of the slice: x: 2, y: 2, z: 4, core: 2. Of those that a mesh axis runs over, the one named last changes fastest.
Arguments:
- state_action: bfloat16 [16384, 23], P(('dp', 'mp')), may hold values from -6 to 6
- next_state: bfloat16 [16384, 17], P(('dp', 'mp')), may hold values from -6 to 6
- reward: float32 [16384], P(('dp', 'mp')), may hold values from -6 to 6
- done_flags: int32 [16384], P(('dp', 'mp')), may hold values from 0 to 2, as said below
- noise_index: int32 [16384], P(('dp', 'mp')), may hold values from 0 to 255
- noise_table: float32 [256, 6], replicated, may hold values from -4 to 4
- subsets: int32 [16384, 2], P(('dp', 'mp')), may hold values from 0 to 9, all different within a row
- policy_in: bfloat16 [17, 256], replicated, may hold values from -1.5 to 1.5
- policy_mid: bfloat16 [256, 256], replicated, may hold values from -0.375 to 0.375
- policy_out: bfloat16 [256, 12], replicated, may hold values from -0.375 to 0.375
- critic_in: float32 [23, 10240], P(None, ('dp', 'mp')), may hold values from -1.25 to 1.25
- in_first: float32 [23, 10240], P(None, ('dp', 'mp')), may hold values from -0.0009765625 to 0.0009765625
- in_second: float32 [23, 10240], P(None, ('dp', 'mp')), may hold values from 3.90625e-10 to 1.5625e-09
- critic_norms: float32 [4, 10240], P(None, ('dp', 'mp')), as said below
- norm_first: float32 [4, 10240], P(None, ('dp', 'mp')), may hold values from -0.0009765625 to 0.0009765625
- norm_second: float32 [4, 10240], P(None, ('dp', 'mp')), may hold values from 3.90625e-10 to 1.5625e-09
- critic_head: float32 [10240], P(('dp', 'mp')), may hold values from -0.1875 to 0.1875
- head_first: float32 [10240], P(('dp', 'mp')), may hold values from -0.03125 to 0.03125
- head_second: float32 [10240], P(('dp', 'mp')), may hold values from 3.90625e-07 to 1.5625e-06
- critic_hidden: float32 [10, 1024, 1024], P(None, 'mp', 'dp'), may hold values from -0.1875 to 0.1875
- hidden_moment: float32 [10, 1024, 1024], P(None, 'mp', 'dp'), may hold values from -0.009765625 to 0.009765625
- left_stats: float32 [10, 1024, 1024], P(None, 'mp', 'dp'), as said below
- right_stats: float32 [10, 1024, 1024], P(None, 'mp', 'dp'), as said below
- target_in: float32 [23, 10240], P(None, ('dp', 'mp')), may hold values from -1.25 to 1.25
- target_norms: float32 [4, 10240], P(None, ('dp', 'mp')), as said below
- target_head: float32 [10240], P(('dp', 'mp')), may hold values from -0.1875 to 0.1875
- target_hidden: float32 [10, 1024, 1024], P(None, 'mp', 'dp'), may hold values from -0.1875 to 0.1875
Outputs:
- loss_total: float32 [], replicated
- valid_total: float32 [], replicated
- in_moment: float32 [23, 10240], P(None, ('dp', 'mp'))
- in_square: float32 [23, 10240], P(None, ('dp', 'mp'))
- in_updated: float32 [23, 10240], P(None, ('dp', 'mp'))
- norm_moment: float32 [4, 10240], P(None, ('dp', 'mp'))
- norm_square: float32 [4, 10240], P(None, ('dp', 'mp'))
- norm_updated: float32 [4, 10240], P(None, ('dp', 'mp'))
- head_moment: float32 [10240], P(('dp', 'mp'))
- head_square: float32 [10240], P(('dp', 'mp'))
- head_updated: float32 [10240], P(('dp', 'mp'))
- hidden_momentum: float32 [10, 1024, 1024], P(None, 'mp', 'dp')
- left_renewed: float32 [10, 1024, 1024], P(None, 'mp', 'dp')
- right_renewed: float32 [10, 1024, 1024], P(None, 'mp', 'dp')
- hidden_updated: float32 [10, 1024, 1024], P(None, 'mp', 'dp')
Inputs may be any that keep to these rules, and one draw needn't show every extreme that they name: `done_flags`: the first row of each block of 512 rows is never 2. `critic_norms`: rows 0 and 2 are gains, rows 1 and 3 shifts. `target_norms`: rows 0 and 2 are gains, rows 1 and 3 shifts. `left_stats`: zero except the diagonal of each 32 x 32 block, which is positive. `right_stats`: zero except the diagonal of each 32 x 32 block, which is positive.
All inputs are finite; a program needn't handle non-finite values.
Results may differ from a plain program's by a relative error of at most 0.0051.
Values may be sent and summed in bfloat16 or wider, within the bound.
A program may use at most 320 MiB of HBM per device.

v0:
```python
import math

import jax
import jax.numpy as jnp
from jax import lax
from jax.sharding import PartitionSpec as P

ACT = 6
H = 1024
CRIT = 10
BLK = 32
NEWTON = 5
STEP = 10


HIGHEST = lax.Precision.HIGHEST
REWARD_DISCOUNT = 0.99
ENTROPY_TEMP = 0.2
FIRST_DECAY = 0.9
SECOND_DECAY = 0.999
WEIGHT_DECAY = 0.01
RATE_INPUT = 0.1
RATE_NORMS = 0.3
RATE_HEAD = 0.03
RATE_HIDDEN = 0.01
MOMENTUM = 0.9
STAT_DECAY = 0.95


def swish(values):
    return values * jax.nn.sigmoid(values)


def norm_forward(preact, gain, shift):
    centered = preact - jnp.mean(preact, -1, keepdims=True)
    inv_std = lax.rsqrt(jnp.mean(centered * centered, -1, keepdims=True) + 1e-05)
    scaled = centered * inv_std
    return (swish(scaled * gain + shift), (scaled, inv_std))


def norm_backward(grad_out, saved, gain, shift):
    scaled, inv_std = saved
    linear = scaled * gain + shift
    sigma = jax.nn.sigmoid(linear)
    grad_linear = grad_out * sigma * (1.0 + linear * (1.0 - sigma))
    grad_gain = jnp.sum(grad_linear * scaled, 0)
    grad_shift = jnp.sum(grad_linear, 0)
    grad_scaled = grad_linear * gain
    grad_pre = inv_std * (
        grad_scaled
        - jnp.mean(grad_scaled, -1, keepdims=True)
        - scaled * jnp.mean(grad_scaled * scaled, -1, keepdims=True)
    )
    return (grad_pre, grad_gain, grad_shift)


def critic_forward(inputs, weight_in, weight_hidden, gains, head_row):
    count_rows = inputs.shape[0]
    norm_rows = gains.reshape(4, CRIT, H)
    first_pre = jnp.dot(inputs, weight_in, preferred_element_type=jnp.float32).reshape(
        count_rows, CRIT, H
    )
    first_act, first_saved = norm_forward(first_pre, norm_rows[0], norm_rows[1])
    hidden_act = first_act.astype(jnp.bfloat16)
    second_pre = jnp.einsum(
        "rck,ckn->rcn", hidden_act, weight_hidden, preferred_element_type=jnp.float32
    )
    second_act, second_saved = norm_forward(second_pre, norm_rows[2], norm_rows[3])
    q_values = jnp.sum(second_act * head_row.reshape(CRIT, H), -1)
    return (q_values, (first_saved, hidden_act, second_saved, second_act))


def critic_backward(grad_q, inputs, saved, weight_hidden, gains, head_row):
    first_saved, hidden_act, second_saved, second_act = saved
    norm_rows = gains.reshape(4, CRIT, H)
    grad_head = jnp.sum(grad_q[:, :, None] * second_act, 0)
    grad_act = grad_q[:, :, None] * head_row.reshape(CRIT, H)
    second_grad, gain_two, shift_two = norm_backward(
        grad_act, second_saved, norm_rows[2], norm_rows[3]
    )
    second_low = second_grad.astype(jnp.bfloat16)
    grad_hidden = jnp.einsum(
        "rck,rcn->ckn", hidden_act, second_low, preferred_element_type=jnp.float32
    )
    grad_first = jnp.einsum(
        "rcn,ckn->rck", second_low, weight_hidden, preferred_element_type=jnp.float32
    )
    first_grad, gain_one, shift_one = norm_backward(
        grad_first, first_saved, norm_rows[0], norm_rows[1]
    )
    first_low = first_grad.astype(jnp.bfloat16).reshape(inputs.shape[0], CRIT * H)
    grad_in = jnp.einsum("ri,rj->ij", inputs, first_low, preferred_element_type=jnp.float32)
    grad_norms = jnp.stack([gain_one, shift_one, gain_two, shift_two]).reshape(4, CRIT * H)
    return (grad_in, grad_hidden, grad_norms, grad_head.reshape(CRIT * H))


def policy_sample(next_state, noise_rows, policy_in, policy_mid, policy_out):
    layer_one = swish(jnp.dot(next_state, policy_in, preferred_element_type=jnp.float32)).astype(
        jnp.bfloat16
    )
    layer_two = swish(jnp.dot(layer_one, policy_mid, preferred_element_type=jnp.float32)).astype(
        jnp.bfloat16
    )
    output = jnp.dot(layer_two, policy_out, preferred_element_type=jnp.float32)
    means = output[:, :ACT]
    log_std = -5.0 + 3.5 * (jnp.tanh(output[:, ACT:]) + 1.0)
    squashed = means + jnp.exp(log_std) * noise_rows
    action = jnp.tanh(squashed)
    correction = 2.0 * (math.log(2.0) - squashed - jax.nn.softplus(-2.0 * squashed))
    action_log_density = jnp.sum(
        -0.5 * noise_rows * noise_rows - log_std - 0.5 * math.log(2.0 * math.pi) - correction, -1
    )
    return (action.astype(jnp.bfloat16), action_log_density)


def adamw(grad, moment, square, weight, rate):
    moment_new = FIRST_DECAY * moment + (1.0 - FIRST_DECAY) * grad
    square_new = SECOND_DECAY * square + (1.0 - SECOND_DECAY) * grad * grad
    moment_hat = moment_new / (1.0 - FIRST_DECAY**STEP)
    square_hat = square_new / (1.0 - SECOND_DECAY**STEP)
    weight_new = weight - rate * (
        moment_hat / (jnp.sqrt(square_hat) + 1e-08) + WEIGHT_DECAY * weight
    )
    return (moment_new, square_new, weight_new)


def to_blocks(matrix):
    depth, rows_all, cols_all = matrix.shape
    shaped = matrix.reshape(depth, rows_all // BLK, BLK, cols_all // BLK, BLK)
    return shaped.transpose(0, 1, 3, 2, 4)


def from_blocks(blocks):
    depth, row_blocks, col_blocks, side, other = blocks.shape
    return blocks.transpose(0, 1, 3, 2, 4).reshape(depth, row_blocks * side, col_blocks * other)


def matmul(left, right):
    return jnp.einsum("...ij,...jk->...ik", left, right, precision=HIGHEST)


def inverse_root(stat):
    identity = jnp.eye(stat.shape[-1], dtype=jnp.float32)
    scale = jnp.sqrt(jnp.sum(stat * stat, axis=(-2, -1), keepdims=True))
    root = identity * lax.rsqrt(jnp.sqrt(scale))
    scaled = stat / scale
    for sweep in range(NEWTON):
        factor = (5.0 * identity - scaled) * 0.25
        root = matmul(root, factor)
        square_factor = matmul(factor, factor)
        scaled = matmul(matmul(square_factor, square_factor), scaled)
    return root


def shampoo(grad, moment, left, right, weight):
    grad_blocks = to_blocks(grad)
    moment_new = MOMENTUM * to_blocks(moment) + grad_blocks
    left_new = STAT_DECAY * to_blocks(left) + (1.0 - STAT_DECAY) * jnp.einsum(
        "...ij,...kj->...ik", grad_blocks, grad_blocks, precision=HIGHEST
    )
    right_new = STAT_DECAY * to_blocks(right) + (1.0 - STAT_DECAY) * jnp.einsum(
        "...ji,...jk->...ik", grad_blocks, grad_blocks, precision=HIGHEST
    )
    update_direction = matmul(matmul(inverse_root(left_new), moment_new), inverse_root(right_new))
    update_direction = update_direction * lax.rsqrt(
        jnp.mean(update_direction * update_direction, axis=(-2, -1), keepdims=True) + 1e-06
    )
    weight_new = weight - RATE_HIDDEN * (from_blocks(update_direction) + WEIGHT_DECAY * weight)
    return (from_blocks(moment_new), from_blocks(left_new), from_blocks(right_new), weight_new)


def local(
    state_action,
    next_state,
    reward,
    done_flags,
    noise_index,
    noise_table,
    subsets,
    policy_in,
    policy_mid,
    policy_out,
    critic_in,
    in_first,
    in_second,
    critic_norms,
    norm_first,
    norm_second,
    critic_head,
    head_first,
    head_second,
    critic_hidden,
    hidden_moment,
    left_stats,
    right_stats,
    target_in,
    target_norms,
    target_head,
    target_hidden,
):
    gathered = (
        lax.all_gather(critic_in, ("dp", "mp"), axis=1, tiled=True),
        lax.all_gather(critic_norms, ("dp", "mp"), axis=1, tiled=True),
        lax.all_gather(critic_head, ("dp", "mp"), axis=0, tiled=True),
        lax.all_gather(target_in, ("dp", "mp"), axis=1, tiled=True),
        lax.all_gather(target_norms, ("dp", "mp"), axis=1, tiled=True),
        lax.all_gather(target_head, ("dp", "mp"), axis=0, tiled=True),
    )
    full_in, full_norms, full_head, target_full_in, target_full_norms, target_full_head = gathered
    column_pieces = (
        lax.all_gather(critic_hidden.astype(jnp.bfloat16), "dp", axis=2, tiled=True),
        lax.all_gather(target_hidden.astype(jnp.bfloat16), "dp", axis=2, tiled=True),
    )
    whole_hidden = (
        lax.all_gather(column_pieces[0], "mp", axis=1, tiled=True),
        lax.all_gather(column_pieces[1], "mp", axis=1, tiled=True),
    )
    weight_hidden, target_weight_hidden = whole_hidden
    validity = (done_flags != 2).astype(jnp.float32)
    local_count = jnp.sum(validity)
    counted = lax.psum(local_count, ("dp", "mp"))
    one_hot = (noise_index[:, None] == jnp.arange(noise_table.shape[0])[None, :]).astype(
        jnp.float32
    )
    noise_rows = jnp.dot(one_hot, noise_table, precision=HIGHEST)
    action, action_log_density = policy_sample(
        next_state, noise_rows, policy_in, policy_mid, policy_out
    )
    target_inputs = jnp.concatenate([next_state, action], 1)
    q_target, unused_saved = critic_forward(
        target_inputs,
        target_full_in.astype(jnp.bfloat16),
        target_weight_hidden,
        target_full_norms,
        target_full_head,
    )
    picks = jnp.arange(CRIT)[None, :]
    first_critic_choice = jnp.sum(jnp.where(picks == subsets[:, 0:1], q_target, 0.0), -1)
    second_critic_choice = jnp.sum(jnp.where(picks == subsets[:, 1:2], q_target, 0.0), -1)
    bootstrap_value = (done_flags == 0).astype(jnp.float32)
    goal = reward + REWARD_DISCOUNT * bootstrap_value * (
        jnp.minimum(first_critic_choice, second_critic_choice) - ENTROPY_TEMP * action_log_density
    )
    q_values, saved = critic_forward(
        state_action, full_in.astype(jnp.bfloat16), weight_hidden, full_norms, full_head
    )
    errors = q_values - goal[:, None]
    local_loss = jnp.sum(validity[:, None] * errors * errors)
    loss_total = lax.psum(local_loss, ("dp", "mp"))
    grad_q = 2.0 * validity[:, None] * errors * (1.0 / counted)
    grad_in, grad_hidden, grad_norms, grad_head = critic_backward(
        grad_q, state_action, saved, weight_hidden, full_norms, full_head
    )
    own_in, own_norms, own_head = (
        lax.psum_scatter(grad_in, ("dp", "mp"), scatter_dimension=1, tiled=True),
        lax.psum_scatter(grad_norms, ("dp", "mp"), scatter_dimension=1, tiled=True),
        lax.psum_scatter(grad_head, ("dp", "mp"), scatter_dimension=0, tiled=True),
    )
    partial_grad = lax.psum_scatter(grad_hidden, "mp", scatter_dimension=1, tiled=True)
    own_hidden = lax.psum_scatter(partial_grad, "dp", scatter_dimension=2, tiled=True)
    in_moment, in_square, in_updated = adamw(own_in, in_first, in_second, critic_in, RATE_INPUT)
    norm_moment, norm_square, norm_updated = adamw(
        own_norms, norm_first, norm_second, critic_norms, RATE_NORMS
    )
    head_moment, head_square, head_updated = adamw(
        own_head, head_first, head_second, critic_head, RATE_HEAD
    )
    hidden_momentum, left_renewed, right_renewed, hidden_updated = shampoo(
        own_hidden, hidden_moment, left_stats, right_stats, critic_hidden
    )
    return (
        loss_total,
        counted,
        in_moment,
        in_square,
        in_updated,
        norm_moment,
        norm_square,
        norm_updated,
        head_moment,
        head_square,
        head_updated,
        hidden_momentum,
        left_renewed,
        right_renewed,
        hidden_updated,
    )


def solution(mesh):
    return jax.shard_map(
        local,
        mesh=mesh,
        in_specs=(
            P(("dp", "mp"), None),
            P(("dp", "mp"), None),
            P(("dp", "mp")),
            P(("dp", "mp")),
            P(("dp", "mp")),
            P(),
            P(("dp", "mp"), None),
            P(),
            P(),
            P(),
            P(None, ("dp", "mp")),
            P(None, ("dp", "mp")),
            P(None, ("dp", "mp")),
            P(None, ("dp", "mp")),
            P(None, ("dp", "mp")),
            P(None, ("dp", "mp")),
            P(("dp", "mp")),
            P(("dp", "mp")),
            P(("dp", "mp")),
            P(None, "mp", "dp"),
            P(None, "mp", "dp"),
            P(None, "mp", "dp"),
            P(None, "mp", "dp"),
            P(None, ("dp", "mp")),
            P(None, ("dp", "mp")),
            P(("dp", "mp")),
            P(None, "mp", "dp"),
        ),
        out_specs=(
            P(),
            P(),
            P(None, ("dp", "mp")),
            P(None, ("dp", "mp")),
            P(None, ("dp", "mp")),
            P(None, ("dp", "mp")),
            P(None, ("dp", "mp")),
            P(None, ("dp", "mp")),
            P(("dp", "mp")),
            P(("dp", "mp")),
            P(("dp", "mp")),
            P(None, "mp", "dp"),
            P(None, "mp", "dp"),
            P(None, "mp", "dp"),
            P(None, "mp", "dp"),
        ),
        check_vma=False,
    )
```

profile of v0, /device:TPU:9, one launch (start us, length us, event | category | flops | bytes accessed | tf_op | source)
XLA Modules:
  0.0 1616.0 jit_solution(16980032440267643491)
XLA Ops:
  12.0 23.7 %all-gather.13.cloned.1.call-done = bf16[10,64,1024]{2,1,0:T(8,128)(2,1)} async-done(((bf16[10,64,512]{2,1,0:T(8,128)(2,1)}), bf16[10,64,1024]{2,1,0:T(8,128)(2,1)}) %all-gather.13.cloned.1.call-update) | async-done | bytes 1310736 | tf_op jit(solution)/shard_map/all_gather | solution.py:212
  35.7 26.3 %all-gather.9.cloned.1.call-done = bf16[10,64,1024]{2,1,0:T(8,128)(2,1)} async-done(((bf16[10,64,512]{2,1,0:T(8,128)(2,1)}), bf16[10,64,1024]{2,1,0:T(8,128)(2,1)}) %all-gather.9.cloned.1.call-update) | async-done | bytes 1310736 | tf_op jit(solution)/shard_map/all_gather | solution.py:211
  64.5 41.3 %all-reduce.6 = (f32[10240]{0:T(1024)S(1)}, f32[10240]{0:T(1024)S(1)}, f32[]{:T(128)}) all-reduce(f32[10240]{0:T(1024)S(1)} %dynamic-update-slice, f32[10240]{0:T(1024)S(1)} %dynamic-update-slice.1, f32[]{:T(128)} %convert_reduce_fusion), channel_id=1, replica_groups=mesh['dp'=2,'mp'=16] {'dp','mp'}, use_global_device_ids=true, to_apply=%add | all-reduce | flops 20481 | bytes 163848
  107.1 39.9 %all-gather.3 = f32[32,320,4]{1,2,0:T(4,128)S(1)} all-gather(f32[1,320,4]{1,2,0:T(4,128)S(1)} %bitcast.240), channel_id=1, replica_groups=mesh['dp'=2,'mp'=16] {'dp','mp'}, dimensions={0}, use_global_device_ids=true | all-gather | bytes 168960 | tf_op jit(solution)/shard_map/all_gather | solution.py:206
  147.1 37.7 %all-gather.1 = f32[32,320,4]{1,2,0:T(4,128)S(1)} all-gather(f32[1,320,4]{1,2,0:T(4,128)S(1)} %bitcast.237), channel_id=1, replica_groups=mesh['dp'=2,'mp'=16] {'dp','mp'}, dimensions={0}, use_global_device_ids=true | all-gather | bytes 168960 | tf_op jit(solution)/shard_map/all_gather | solution.py:203
  188.5 42.5 %all-gather = bf16[32,320,23]{1,2,0:T(8,128)(2,1)S(1)} all-gather(bf16[1,320,23]{1,2,0:T(8,128)(2,1)S(1)} %bitcast_convert_fusion.1), channel_id=1, replica_groups=mesh['dp'=2,'mp'=16] {'dp','mp'}, dimensions={0}, use_global_device_ids=true | all-gather | bytes 485760 | tf_op jit(solution)/shard_map/all_gather | solution.py:202
  231.8 41.2 %all-gather.2 = bf16[32,320,23]{1,2,0:T(8,128)(2,1)S(1)} all-gather(bf16[1,320,23]{1,2,0:T(8,128)(2,1)S(1)} %bitcast_convert_fusion), channel_id=1, replica_groups=mesh['dp'=2,'mp'=16] {'dp','mp'}, dimensions={0}, use_global_device_ids=true | all-gather | bytes 485760 | tf_op jit(solution)/shard_map/all_gather | solution.py:205
  275.5 8.9 fusion.90
  284.4 20.8 %copy.97 = f32[512,10,1024]{2,0,1:T(8,128)} copy(f32[512,10,1024]{0,2,1:T(8,128)} %bitcast.197) | data formatting | bytes 41943040 | tf_op jit(solution)/shard_map/reshape | solution.py:60
  313.2 8.6 fusion.137
  321.8 20.8 %copy.93 = f32[512,10,1024]{2,0,1:T(8,128)} copy(f32[512,10,1024]{0,2,1:T(8,128)} %bitcast.199) | data formatting | bytes 41943040 | tf_op jit(solution)/shard_map/reshape | solution.py:60
  351.2 8.9 multiply_reduce_fusion.7
  367.0 8.9 multiply_convert_fusion.17
  375.9 28.2 %bitcast_reduce_fusion = (f32[512,10]{0,1:T(8,128)S(1)}, f32[10,512,1024]{2,1,0:T(8,128)}) fusion(bf16[10,1024,1024]{2,1,0:T(8,128)(2,1)} %all-gather.15.cloned.1.call-done, f32[512,10,1024]{2,0,1:T(8,128)} %copy.97, f32[10,1024]{1,0:T(8,128)S(1)} %add.239, f32[10,1024]{1,0:T(8,128)S(1)} %mul.604, f32[512,10]{0,1:T(8,128)S(1)} %add_rsqrt_fusion.1, ...), kind=kOutput, calls=%fused_computation.3 | convolution fusion | flops 10789841920 | bytes 63057920 | tf_op jit(solution)/shard_map/rck,ckn->rcn/dot_general | solution.py:65
  412.7 28.2 %bitcast_reduce_fusion.1 = (f32[512,10]{0,1:T(8,128)S(1)}, f32[10,512,1024]{2,1,0:T(8,128)}) fusion(bf16[10,1024,1024]{2,1,0:T(8,128)(2,1)} %all-gather.11.cloned.1.call-done, f32[512,10,1024]{2,0,1:T(8,128)} %copy.93, f32[10,1024]{1,0:T(8,128)S(1)} %add.222, f32[10,1024]{1,0:T(8,128)S(1)} %mul.580, f32[512,10]{0,1:T(8,128)S(1)} %add_rsqrt_fusion.3, ...), kind=kOutput, calls=%fused_computation.5 | convolution fusion | flops 10789841920 | bytes 63057920 | tf_op jit(solution)/shard_map/rck,ckn->rcn/dot_general | solution.py:65
  441.0 11.1 multiply_reduce_fusion.9
  452.3 12.7 multiply_reduce_fusion.5
  465.2 11.3 multiply_reduce_fusion.8
  477.1 21.9 %multiply_reduce_fusion.1 = (f32[10,1024]{1,0:T(8,128)S(1)}, f32[10,1024]{1,0:T(8,128)S(1)}, f32[512,10]{0,1:T(8,128)S(1)}, f32[512,10]{0,1:T(8,128)S(1)}, f32[10,1024]{1,0:T(8,128)}) fusion(f32[10,512,1024]{2,1,0:T(8,128)S(1)} %bitcast.196, f32[512,10]{0,1:T(8,128)S(1)} %add_rsqrt_fusion.2, f32[512,10]{0,1:T(8,128)S(1)} %broadcast_multiply_fusion.9, ...), kind=kLoop, calls=%fused_computation.7 | loop fusion | flops 115302400 | bytes 42291200 | tf_op jit(solution)/shard_map/reduce_sum | solution.py:46
  499.1 29.5 %fusion.129 = f32[10,1024,1024]{2,1,0:T(8,128)} fusion(f32[10,512,1024]{2,1,0:T(8,128)} %get-tuple-element.65, f32[512,10]{0,1:T(8,128)S(1)} %broadcast_multiply_fusion.5, f32[512,10]{0,1:T(8,128)S(1)} %broadcast_multiply_fusion.6, f32[10,1024]{1,0:T(8,128)S(1)} %copy-done.10, f32[512,10]{0,1:T(8,128)S(1)} %add_rsqrt_fusion.2, ...), kind=kOutput, calls=%fused_computation.235 | convolution fusion | flops 10837032960 | bytes 73625600 | tf_op jit(solution)/shard_map/rck,rcn->ckn/dot_general | solution.py:82
  528.8 47.5 %multiply_reduce_fusion.2 = (f32[10,1024]{1,0:T(8,128)S(1)}, f32[512,10]{0,1:T(8,128)S(1)}, f32[512,10]{0,1:T(8,128)S(1)}, f32[10,1024]{1,0:T(8,128)S(1)}, f32[512,10,1024]{2,0,1:T(8,128)}) fusion(f32[512,10,1024]{2,0,1:T(8,128)} %copy.93, f32[512,10]{0,1:T(8,128)S(1)} %add_rsqrt_fusion.3, f32[512,10]{0,1:T(8,128)S(1)} %broadcast_multiply_fusion.10, ...), kind=kOutput, calls=%fused_computation.8 | convolution fusion | flops 10936616960 | bytes 84357120 | tf_op jit(solution)/shard_map/rcn,ckn->rck/dot_general | solution.py:85
  576.3 22.6 %multiply_convert_fusion = bf16[512,10,1024]{2,0,1:T(8,128)(2,1)} fusion(f32[512,10,1024]{2,0,1:T(8,128)} %get-tuple-element.68, f32[512,10,1024]{2,0,1:T(8,128)} %copy.93, f32[512,10]{0,1:T(8,128)S(1)} %broadcast_multiply_fusion.3, f32[512,10]{0,1:T(8,128)S(1)} %broadcast_multiply_fusion.4, f32[10,1024]{1,0:T(8,128)S(1)} %mul.580, ...), kind=kLoop, calls=%fused_computation.9 | loop fusion | flops 41943040 | bytes 52551680 | tf_op jit(solution)/shard_map/convert_element_type | solution.py:91
  598.9 14.2 copy.99
  626.7 301.3 %reduce-scatter.9.cloned.1.call-done = f32[10,64,1024]{2,1,0:T(8,128)} async-done(((f32[10,1024,1024]{2,1,0:T(8,128)}), f32[10,64,1024]{2,1,0:T(8,128)}) %reduce-scatter.9.cloned.1.call-update) | async-done | bytes 2621456 | tf_op jit(solution)/shard_map/reduce_scatter | solution.py:259
  936.3 41.7 %all-reduce.3 = (f32[]{:T(128)}, f32[10240]{0:T(1024)S(1)}) all-reduce(f32[]{:T(128)} %get-tuple-element.57, f32[10240]{0:T(1024)S(1)} %reshape.243), channel_id=1, replica_groups=mesh['dp'=2,'mp'=16] {'dp','mp'}, use_global_device_ids=true, to_apply=%region_14.15 | all-reduce | flops 10241 | bytes 81928 | tf_op jit(solution)/shard_map/psum | solution.py:249
  978.6 80.5 %reduce-scatter.15.cloned.1.call-done = f32[320,4]{1,0:T(8,128)} async-done(((f32[10240,4]{1,0:T(8,128)}), f32[320,4]{1,0:T(8,128)}) %reduce-scatter.15.cloned.1.call-update) | async-done | bytes 5136
  1060.8 140.0 %reduce-scatter.13.cloned.1.call-done = f32[320,23]{1,0:T(8,128)} async-done(((f32[10240,23]{1,0:T(8,128)}), f32[320,23]{1,0:T(8,128)}) %reduce-scatter.13.cloned.1.call-update) | async-done | bytes 29456
  1202.5 49.8 %reduce-scatter.11.cloned.1.call-done = f32[10,64,512]{2,1,0:T(8,128)} async-done(((f32[10,64,1024]{2,1,0:T(8,128)}), f32[10,64,512]{2,1,0:T(8,128)}) %reduce-scatter.11.cloned.1.call-update) | async-done | bytes 1310736 | tf_op jit(solution)/shard_map/reduce_scatter | solution.py:260
  1261.6 19.6 %bitcast_add_fusion.4 = (f32[10,2,32,16,32]{4,2,3,1,0:T(8,128)S(1)}, f32[10,2,16,32,32]{4,3,2,1,0:T(8,128)}) fusion(f32[10,2,32,16,32]{4,3,2,1,0:T(8,128)} %mul.701, f32[10,2,32,16,32]{4,3,2,1,0:T(8,128)} %reshape.244, f32[10,2,16,32,32]{4,2,3,1,0:T(8,128)} %bitcast.201), kind=kOutput, calls=%fused_computation.42 | convolution fusion | flops 126484480 | bytes 6553600 | tf_op jit(solution)/shard_map/...ji,...jk->...ik/dot_general | solution.py:161
  1414.0 11.7 bitcast_add_fusion.5
  1552.9 9.1 fusion.146
  1577.7 10.1 fusion.9
  (294 shorter events, 378.7 us)
Async XLA Ops:
  7.2 266.6 %copy-start = (bf16[256,256]{1,0:T(8,128)(2,1)S(1)}, bf16[256,256]{1,0:T(8,128)(2,1)}, u32[]{:S(2)}) copy-start(bf16[256,256]{1,0:T(8,128)(2,1)} %param.35) | copy-start | bytes 393220
  7.2 55.0 %copy-start.28 = (s32[512]{0:T(512)S(1)}, s32[512]{0:T(512)}, u32[]{:S(2)}) copy-start(s32[512]{0:T(512)} %param.30) | copy-start | bytes 6148
  7.2 56.1 %copy-start.30 = (f32[320]{0:T(512)S(1)}, f32[320]{0:T(512)}, u32[]{:S(2)}) copy-start(f32[320]{0:T(512)} %param.43) | copy-start | bytes 3844
  7.2 56.4 %copy-start.36 = (f32[320]{0:T(512)S(1)}, f32[320]{0:T(512)}, u32[]{:S(2)}) copy-start(f32[320]{0:T(512)} %param.52) | copy-start | bytes 3844
  7.2 99.8 %copy-start.32 = (f32[4,320]{1,0:T(4,128)S(1)}, f32[4,320]{1,0:T(4,128)}, u32[]{:S(2)}) copy-start(f32[4,320]{1,0:T(4,128)} %param.51) | copy-start | bytes 15364
  7.2 139.9 %copy-start.22 = (f32[4,320]{1,0:T(4,128)S(1)}, f32[4,320]{1,0:T(4,128)}, u32[]{:S(2)}) copy-start(f32[4,320]{1,0:T(4,128)} %param.40) | copy-start | bytes 15364
  7.3 28.4 %all-gather.13.cloned.1.call-start = ((), (), s32[]{:S(2)}) async-start(), calls=%async_computation.6 | async-start | bytes 1966080 | tf_op jit(solution)/shard_map/all_gather | solution.py:212
  9.6 178.9 %copy-start.15 = (f32[23,320]{1,0:T(8,128)S(1)}, f32[23,320]{1,0:T(8,128)}, u32[]{:S(2)}) copy-start(f32[23,320]{1,0:T(8,128)} %param.37) | copy-start | bytes 88324
  9.6 52.5 %all-gather.9.cloned.1.call-start = ((), (), s32[]{:S(2)}) async-start(), calls=%async_computation.4 | async-start | bytes 1966080 | tf_op jit(solution)/shard_map/all_gather | solution.py:211
  11.9 219.9 %copy-start.19 = (f32[23,320]{1,0:T(8,128)S(1)}, f32[23,320]{1,0:T(8,128)}, u32[]{:S(2)}) copy-start(f32[23,320]{1,0:T(8,128)} %param.50) | copy-start | bytes 88324
  11.9 364.0 %all-gather.15.cloned.1.call-start = ((), (), s32[]{:S(2)}) async-start(), calls=%async_computation.7 | async-start | bytes 22282240 | tf_op jit(solution)/shard_map/all_gather | solution.py:216
  35.7 377.1 %all-gather.11.cloned.1.call-start = ((), (), s32[]{:S(2)}) async-start(), calls=%async_computation.5 | async-start | bytes 22282240 | tf_op jit(solution)/shard_map/all_gather | solution.py:215
  62.1 211.8 %copy-start.24 = (bf16[512,17]{0,1:T(8,128)(2,1)S(1)}, bf16[512,17]{0,1:T(8,128)(2,1)}, u32[]{:S(2)}) copy-start(bf16[512,17]{0,1:T(8,128)(2,1)} %param.28) | copy-start | bytes 52228
  62.1 211.8 %copy-start.41 = (bf16[17,256]{1,0:T(8,128)(2,1)S(1)}, bf16[17,256]{1,0:T(8,128)(2,1)}, u32[]{:S(2)}) copy-start(bf16[17,256]{1,0:T(8,128)(2,1)} %param.34) | copy-start | bytes 26116
  62.1 866.0 %reduce-scatter.9.cloned.1.call-start = ((), (), s32[]{:S(2)}) async-start(), calls=%async_computation.8 | async-start | bytes 44564480 | tf_op jit(solution)/shard_map/reduce_scatter | solution.py:259
  188.5 85.8 %copy-start.25 = (bf16[256,12]{0,1:T(8,128)(2,1)S(1)}, bf16[256,12]{0,1:T(8,128)(2,1)}, u32[]{:S(2)}) copy-start(bf16[256,12]{0,1:T(8,128)(2,1)} %param.36) | copy-start | bytes 18436
  231.1 43.4 %copy-start.42 = (f32[256,6]{0,1:T(8,128)S(1)}, f32[256,6]{0,1:T(8,128)}, u32[]{:S(2)}) copy-start(f32[256,6]{0,1:T(8,128)} %param.32) | copy-start | bytes 18436
  231.1 43.4 %copy-start.43 = (s32[512]{0:T(512)S(1)}, s32[512]{0:T(512)}, u32[]{:S(2)}) copy-start(s32[512]{0:T(512)} %param.31) | copy-start | bytes 6148
  465.2 33.8 %slice-start.23 = ((s8[10485760]{0:T(1024)(128)(4,1)}), s8[4194304]{0:T(1024)(128)(4,1)S(1)}, s32[]{:S(2)}) async-start(s8[10485760]{0:T(1024)(128)(4,1)} %bitcast.223), calls=%async_computation.35 | async-start | bytes 8388608
  528.6 530.6 %reduce-scatter.15.cloned.1.call-start = ((), (), s32[]{:S(2)}) async-start(), calls=%async_computation.11 | async-start | bytes 5406720
  616.5 584.3 %reduce-scatter.13.cloned.1.call-start = ((), (), s32[]{:S(2)}) async-start(), calls=%async_computation.10 | async-start | bytes 5406720
  626.7 301.5 %copy-start.7 = (f32[10,64,512]{2,1,0:T(8,128)S(1)}, f32[10,64,512]{2,1,0:T(8,128)}, u32[]{:S(2)}) copy-start(f32[10,64,512]{2,1,0:T(8,128)} %param.49) | copy-start | bytes 3932164
  626.7 625.6 %reduce-scatter.11.cloned.1.call-start = ((), (), s32[]{:S(2)}) async-start(), calls=%async_computation.9 | async-start | bytes 3932160 | tf_op jit(solution)/shard_map/reduce_scatter | solution.py:260
  931.4 46.5 %copy-start.31 = (f32[320]{0:T(512)S(1)}, f32[320]{0:T(512)}, u32[]{:S(2)}) copy-start(f32[320]{0:T(512)} %param.43) | copy-start | bytes 3844
  931.4 46.5 %copy-start.39 = (f32[320]{0:T(512)S(1)}, f32[320]{0:T(512)}, u32[]{:S(2)}) copy-start(f32[320]{0:T(512)} %param.45) | copy-start | bytes 3844
  931.4 46.5 %copy-start.40 = (f32[320]{0:T(512)S(1)}, f32[320]{0:T(512)}, u32[]{:S(2)}) copy-start(f32[320]{0:T(512)} %param.44) | copy-start | bytes 3844
  931.4 128.7 %copy-start.23 = (f32[4,320]{1,0:T(4,128)S(1)}, f32[4,320]{1,0:T(4,128)}, u32[]{:S(2)}) copy-start(f32[4,320]{1,0:T(4,128)} %param.40) | copy-start | bytes 15364
  931.5 128.7 %copy-start.33 = (f32[4,320]{1,0:T(4,128)S(1)}, f32[4,320]{1,0:T(4,128)}, u32[]{:S(2)}) copy-start(f32[4,320]{1,0:T(4,128)} %param.42) | copy-start | bytes 15364
  931.5 128.7 %copy-start.34 = (f32[4,320]{1,0:T(4,128)S(1)}, f32[4,320]{1,0:T(4,128)}, u32[]{:S(2)}) copy-start(f32[4,320]{1,0:T(4,128)} %param.41) | copy-start | bytes 15364
  931.5 270.3 %copy-start.16 = (f32[23,320]{1,0:T(8,128)S(1)}, f32[23,320]{1,0:T(8,128)}, u32[]{:S(2)}) copy-start(f32[23,320]{1,0:T(8,128)} %param.37) | copy-start | bytes 88324
  931.5 270.3 %copy-start.20 = (f32[23,320]{1,0:T(8,128)S(1)}, f32[23,320]{1,0:T(8,128)}, u32[]{:S(2)}) copy-start(f32[23,320]{1,0:T(8,128)} %param.39) | copy-start | bytes 88324
  931.5 270.3 %copy-start.21 = (f32[23,320]{1,0:T(8,128)S(1)}, f32[23,320]{1,0:T(8,128)}, u32[]{:S(2)}) copy-start(f32[23,320]{1,0:T(8,128)} %param.38) | copy-start | bytes 88324
  (46 other events, 568.5 us)
Sparse Core Ops, SparseCore 0:
  10.2 25.4 all-gather.12
  37.8 24.2 all-gather.8
  63.6 111.9 all-gather.14
  177.1 116.0 all-gather.10
  528.7 399.3 reduce-scatter.8
  930.2 128.8 reduce-scatter.14
  1061.4 139.3 reduce-scatter.12
  1203.0 49.2 reduce-scatter.10
where the time goes:
time: 1630 us; the launch traced here: 1620 us
  waiting for transfers between devices  622 us (38%)
  matrix products  449 us (28%)
  blocking collectives  244 us (15%)
  other arithmetic  161 us (10%)
  local copies, waits for them, and re-layouts  123 us (8%)
  between operations  16.5 us (1%)
    reduce_scatter x1, waiting for transfers between devices, local(): lax.psum_scatter(grad_hidden, 'mp', scatter_dimension=1, tiled=True)  301 us
    dot_general x36, matrix products, matmul(): return jnp.einsum('...ij,...jk->...ik', left, right, precision=HIGHEST)  258 us
    unnamed x10, waiting for transfers between devices  221 us
    dot_general x2, matrix products, critic_forward(): jnp.einsum('rck,ckn->rcn', hidden_act, weight_hidden, preferred_element_t...  56.4 us
    reduce_scatter x1, waiting for transfers between devices, local(): lax.psum_scatter(partial_grad, 'dp', scatter_dimension=2, tiled=True)  49.8 us
    dot_general x1, matrix products, critic_backward(): jnp.einsum('rcn,ckn->rck', second_low, weight_hidden, preferred_element_t...  47.5 us
    all_gather x1, blocking collectives, local(): lax.all_gather(critic_in, ('dp', 'mp'), axis=1, tiled=True)  42.5 us
    reshape x2, local copies, waits for them, and re-layouts, critic_forward(): jnp.dot(inputs, weight_in, preferred_element_type=jnp.float32)  41.7 us
  transfers between devices with their start and end apart: 8, of which 6 were waited for; matrix products, arithmetic and copies ran while one was open for 16% of the time, Pallas kernels for 0%

commit v1 on v0

v1 whole, which is shorter than its diff:
```python
import functools
import math

import jax
import jax.numpy as jnp
from jax import lax
from jax.experimental import pallas as pl
from jax.experimental.pallas import tpu as pltpu
from jax.sharding import PartitionSpec as P

ACT = 6
OBS = 17
IN = 23
H = 1024
CRIT = 10
BLK = 32
NEWTON = 5
STEP = 10
REWARD_DISCOUNT = 0.99
ENTROPY_TEMP = 0.2
FIRST_DECAY = 0.9
SECOND_DECAY = 0.999
WEIGHT_DECAY = 0.01
RATE_INPUT = 0.1
RATE_NORMS = 0.3
RATE_HEAD = 0.03
RATE_HIDDEN = 0.01
MOMENTUM = 0.9
STAT_DECAY = 0.95

F32, BF16, I32 = jnp.float32, jnp.bfloat16, jnp.int32
MESH = pl.DeviceIdType.MESH
LANES = 128
HALF = 64
TILE = 256
L_TGT = 23
L_BASE = 46
L_BOOT = 49
L_S0 = 50
L_S1 = 51
L_VALID = 52
L_CNT = 53
VMEM_LIMIT = 60 * 1024 * 1024


def nn(a, b):
    return jnp.dot(a, b, preferred_element_type=F32)


def nt(a, b):
    return lax.dot_general(a, b, (((1,), (1,)), ((), ())), preferred_element_type=F32)


def tn(a, b):
    return lax.dot_general(a, b, (((0,), (0,)), ((), ())), preferred_element_type=F32)


def iota(shape, dim):
    return lax.broadcasted_iota(I32, shape, dim)


def split2(x):
    high = x.astype(BF16)
    return high, (x - high.astype(F32)).astype(BF16)


def split3(x):
    high = x.astype(BF16)
    rest = x - high.astype(F32)
    mid = rest.astype(BF16)
    return high, mid, (rest - mid.astype(F32)).astype(BF16)


def swish(values):
    return values * jax.nn.sigmoid(values)


class Plan:
    def __init__(self, mesh):
        self.n_dp, self.n_mp = mesh.shape["dp"], mesh.shape["mp"]
        self.n = self.n_dp * self.n_mp
        self.groups = self.n // CRIT
        self.workers = self.groups * CRIT
        self.turns = -(-self.n // self.groups)

    def rank(self, dp, mp):
        size = 4 * self.n_dp
        layer = mp // 4
        inner = dp * 4 + (mp % 4 + 2 * (dp % 2)) % 4
        return layer * size + inner + (layer % 2) * (size - 1 - 2 * inner)

    def place(self, k):
        size = 4 * self.n_dp
        layer, inner = k // size, k % size
        inner = inner + (layer % 2) * (size - 1 - 2 * inner)
        dp = inner // 4
        return dp, layer * 4 + (inner % 4 + 2 * (dp % 2)) % 4

    def device(self, s):
        return s // self.n_mp, s % self.n_mp

    def pairs(self, rows):
        per = -(-rows // self.groups)
        return -(-per // 32) * 16

    def cap(self, rows):
        return -(-(self.n * -(-rows // self.groups)) // TILE) * TILE


def chunks_of(columns):
    width = math.gcd(math.gcd(columns, H), HALF)
    return width, columns // width, H // width


def assemble(chunks_ref, width, shift):
    groups = []
    lane = iota((32, LANES), 1)
    for g in range(H // LANES):
        block = jnp.zeros((32, LANES), F32)
        for i in range(LANES // width):
            chunk = chunks_ref[g * (LANES // width) + i]
            turn = (i * width - shift) % LANES
            moved = pltpu.roll(chunk, turn, 1) if turn else chunk
            block = jnp.where(lane // width == i, moved, block)
        groups.append(block)
    return jnp.concatenate(groups, 1)


def all_barrier(plan, dp, mp):
    barrier = pltpu.get_barrier_semaphore()

    def tell(s, _):
        sdp, smp = s // plan.n_mp, s % plan.n_mp

        @pl.when(jnp.logical_or(sdp != dp, smp != mp))
        def _():
            pl.semaphore_signal(barrier, inc=1, device_id=(sdp, smp), device_id_type=MESH)

        return 0

    lax.fori_loop(0, plan.n, tell, 0)
    pl.semaphore_wait(barrier, plan.n - 1)


def dispatch_kernel(
    plan,
    crit_ref,
    targ_ref,
    crit_small,
    targ_small,
    sa_ref,
    ns_ref,
    rows_ref,
    subs_ref,
    table_ref,
    pin_ref,
    pmid_ref,
    pout_ref,
    wt_ref,
    wc_ref,
    x_ref,
    p_ref,
    low,
    msg,
    wide,
    chunk,
    send_w,
    recv_w,
    pass_w,
    send_x,
    recv_x,
    send_p,
    recv_p,
):
    dp, mp = lax.axis_index("dp"), lax.axis_index("mp")
    me = plan.rank(dp, mp)
    index = dp * plan.n_mp + mp
    groups, workers = plan.groups, plan.workers
    critic, group = me // groups, me % groups
    rw, cw = crit_ref.shape[1], crit_ref.shape[2]
    rows = sa_ref.shape[0]
    columns = crit_small[0].shape[1]
    width, mine, per = chunks_of(columns)
    nets = (wt_ref, wc_ref)

    def to_low(c, _):
        low[0, c] = targ_ref[c].astype(BF16)
        low[1, c] = crit_ref[c].astype(BF16)
        return 0

    lax.fori_loop(0, CRIT, to_low, 0)
    all_barrier(plan, dp, mp)

    def w_slot(t, s):
        sdp, smp = plan.device(s)
        return nets[t].at[pl.ds(pl.multiple_of(smp * rw, rw), rw), pl.ds(pl.multiple_of(sdp * cw, cw), cw)]

    def to_worker(src, dst, send, recv, k):
        return pltpu.make_async_remote_copy(
            src_ref=src, dst_ref=dst, send_sem=send, recv_sem=recv, device_id=plan.place(k), device_id_type=MESH
        )

    def first_hop(t, c):
        k = c * groups + index % groups
        return k, to_worker(low.at[t, c], w_slot(t, index), send_w.at[t, c], recv_w.at[t, index], k)

    def send_weights(t):
        def one(i, _):
            c = (critic + i) % CRIT
            k, copy = first_hop(t, c)

            @pl.when(k == me)
            def _():
                pltpu.make_async_copy(low.at[t, c], w_slot(t, index), recv_w.at[t, index]).start()

            @pl.when(k != me)
            def _():
                copy.start()

            return 0

        lax.fori_loop(0, CRIT, one, 0)

    send_weights(0)
    send_weights(1)

    wide[...] = jnp.zeros_like(wide)
    for t, parts in enumerate((targ_small, crit_small)):
        wide[t, 0:IN, 0:columns] = parts[0][...]
        wide[t, IN : IN + 4, 0:columns] = parts[1][...]
        wide[t, IN + 4 : IN + 5, 0:columns] = parts[2][...]
    for j in range(mine):
        start, offset = j * width // LANES * LANES, j * width % LANES
        both = [wide[t, :, start : start + LANES] for t in range(2)]
        turned = [pltpu.roll(v, turn, 1) if turn else v for v, turn in zip(both, ((-offset) % LANES, (HALF - offset) % LANES))]
        chunk[j] = jnp.where(iota((32, LANES), 1) < HALF, turned[0], turned[1])

    def small_hop(j, r):
        g = index * mine + j
        k = (g // per) * groups + r
        return k, to_worker(chunk.at[j], p_ref.at[g % per], send_p.at[j, r], recv_p.at[g % per], k)

    def send_small(i, _):
        j, r = i // groups, i % groups
        k, copy = small_hop(j, r)

        @pl.when(k == me)
        def _():
            slot = (index * mine + j) % per
            pltpu.make_async_copy(chunk.at[j], p_ref.at[slot], recv_p.at[slot]).start()

        @pl.when(k != me)
        def _():
            copy.start()

        return 0

    lax.fori_loop(0, mine * groups, send_small, 0)

    lane = iota((rows, LANES), 1)
    place = lambda height, offset: (iota((height, LANES), 1) == iota((height, LANES), 0) + offset).astype(F32).astype(BF16)
    hidden = swish(nn(ns_ref[...], pin_ref[...])).astype(BF16)
    hidden = swish(nn(hidden, pmid_ref[...])).astype(BF16)
    pout = pout_ref[...]
    spread = lambda offset: nn(
        pout, (iota((2 * ACT, LANES), 0) == iota((2 * ACT, LANES), 1) + offset).astype(F32).astype(BF16)
    ).astype(BF16)
    keep = lane < ACT
    means = nn(hidden, spread(0))
    raw = nn(hidden, spread(ACT))
    facts = rows_ref[...]
    across = jnp.transpose(facts)
    picked = (iota((rows, table_ref.shape[0]), 1) == across[:, 2:3].astype(I32)).astype(F32).astype(BF16)
    noise = jnp.zeros((rows, LANES), F32)
    for part in split3(table_ref[...]):
        noise = noise + nn(picked, nn(part, place(ACT, 0)).astype(BF16))
    log_std = -5.0 + 3.5 * (jnp.tanh(raw) + 1.0)
    squashed = means + jnp.exp(log_std) * noise
    action = jnp.tanh(squashed).astype(BF16)
    twice = -2.0 * squashed
    softplus = jnp.maximum(twice, 0.0) + jnp.log(1.0 + jnp.exp(-jnp.abs(twice)))
    correction = 2.0 * (math.log(2.0) - squashed - softplus)
    density = jnp.sum(
        jnp.where(keep, -0.5 * noise * noise - log_std - 0.5 * math.log(2.0 * math.pi) - correction, 0.0), -1, keepdims=True
    )
    done = across[:, 1:2]
    boot = (done == 0.0).astype(F32)
    base = across[:, 0:1] - (REWARD_DISCOUNT * ENTROPY_TEMP) * boot * density
    high, mid, rest = split3(base)
    subs = subs_ref[...].astype(F32)
    on = lambda k, value: jnp.where(lane == k, value, 0.0)
    features = (
        nn(sa_ref[...], place(IN, 0))
        + nn(ns_ref[...], place(OBS, L_TGT))
        + nn(jnp.where(keep, action.astype(F32), 0.0).astype(BF16), place(LANES, L_TGT + OBS))
        + on(L_BASE, high.astype(F32))
        + on(L_BASE + 1, mid.astype(F32))
        + on(L_BASE + 2, rest.astype(F32))
        + on(L_BOOT, boot)
        + on(L_S0, subs[:, 0:1])
        + on(L_S1, subs[:, 1:2])
        + on(L_VALID, 1.0)
    ).astype(BF16)

    pairs = msg.shape[1]
    valid = (facts[1:2, :] != 2.0).astype(F32)
    before = (iota((rows, rows), 0) < iota((rows, rows), 1)).astype(F32).astype(BF16)
    order = nn(jnp.broadcast_to(valid, (8, rows)).astype(BF16), before)[0:1, :]
    order = jnp.where(valid > 0.0, order, -1.0)
    count = jnp.sum(valid, -1, keepdims=True)
    count_half = jnp.floor(count * 0.5)
    mlane = iota((pairs, LANES), 1)
    tail = jnp.where(mlane == L_CNT, count_half, 0.0) + jnp.where(mlane == L_CNT + 1, count - 2.0 * count_half, 0.0)

    def deal(r, _):
        slot = iota((pairs, rows), 0) * (2 * groups) + r
        halves = []
        for h in range(2):
            hot = (order == (slot + h * groups).astype(F32)).astype(F32).astype(BF16)
            halves.append(nn(hot, features))
        msg[r] = (halves[0] + pltpu.roll(halves[1], HALF, 1) + tail).astype(BF16)
        return 0

    lax.fori_loop(0, groups, deal, 0)

    def row_hop(k):
        return to_worker(msg.at[k % groups], x_ref.at[index], send_x.at[k], recv_x.at[index], k)

    def send_rows(i, _):
        k = (me + i) % workers

        @pl.when(k == me)
        def _():
            pltpu.make_async_copy(msg.at[group], x_ref.at[index], recv_x.at[index]).start()

        @pl.when(k != me)
        def _():
            row_hop(k).start()

        return 0

    lax.fori_loop(0, workers, send_rows, 0)

    def pass_on(t, turn, i):
        s = group + groups * turn
        k = critic * groups + (group + 1 + i) % groups
        return to_worker(w_slot(t, s), w_slot(t, s), pass_w.at[t, turn, i], recv_w.at[t, s], k)

    def arrived_w(t, s):
        pltpu.make_async_copy(low.at[t, 0], w_slot(t, s), recv_w.at[t, s]).wait()

    turns = (plan.n - group + groups - 1) // groups

    @pl.when(me < workers)
    def _():
        for t in range(2):

            def relay(turn, _):
                arrived_w(t, group + groups * turn)

                def one(i, _):
                    pass_on(t, turn, i).start()
                    return 0

                lax.fori_loop(0, groups - 1, one, 0)
                return 0

            lax.fori_loop(0, turns, relay, 0)

        def arrived(s, _):
            @pl.when(s % groups != group)
            def _():
                arrived_w(0, s)
                arrived_w(1, s)

            pltpu.make_async_copy(msg.at[0], x_ref.at[s], recv_x.at[s]).wait()
            return 0

        lax.fori_loop(0, plan.n, arrived, 0)

        def arrived_small(j, _):
            pltpu.make_async_copy(chunk.at[0], p_ref.at[j], recv_p.at[j]).wait()
            return 0

        lax.fori_loop(0, per, arrived_small, 0)
        for t in range(2):

            def passed(turn, _):
                def one(i, _):
                    pass_on(t, turn, i).wait_send()
                    return 0

                lax.fori_loop(0, groups - 1, one, 0)
                return 0

            lax.fori_loop(0, turns, passed, 0)

    def sent_weights(c, _):
        for t in range(2):
            k, copy = first_hop(t, c)

            @pl.when(k != me)
            def _():
                copy.wait_send()

        return 0

    lax.fori_loop(0, CRIT, sent_weights, 0)

    def sent_small(i, _):
        k, copy = small_hop(i // groups, i % groups)

        @pl.when(k != me)
        def _():
            copy.wait_send()

        return 0

    lax.fori_loop(0, mine * groups, sent_small, 0)

    def sent_rows(k, _):
        @pl.when(k != me)
        def _():
            row_hop(k).wait_send()

        return 0

    lax.fori_loop(0, workers, sent_rows, 0)


def dispatch(plan, critic_hidden, target_hidden, critic_small, target_small, rows_args, policy):
    rows = rows_args[0].shape[0]
    pairs = plan.pairs(rows)
    columns = critic_small[0].shape[1]
    _width, mine, per = chunks_of(columns)
    vmem = pl.BlockSpec(memory_space=pltpu.VMEM)
    anywhere = pl.BlockSpec(memory_space=pl.ANY)
    dma = pltpu.SemaphoreType.DMA
    return pl.pallas_call(
        functools.partial(dispatch_kernel, plan),
        out_shape=(
            jax.ShapeDtypeStruct((H, H), BF16),
            jax.ShapeDtypeStruct((H, H), BF16),
            jax.ShapeDtypeStruct((plan.n, pairs, LANES), BF16),
            jax.ShapeDtypeStruct((per, 32, LANES), F32),
        ),
        in_specs=[vmem, vmem, (vmem,) * 3, (vmem,) * 3] + [vmem] * 8,
        out_specs=(anywhere,) * 4,
        scratch_shapes=[
            pltpu.VMEM((2,) + critic_hidden.shape, BF16),
            pltpu.VMEM((plan.groups, pairs, LANES), BF16),
            pltpu.VMEM((2, 32, -(-columns // LANES) * LANES), F32),
            pltpu.VMEM((mine, 32, LANES), F32),
            dma((2, CRIT)),
            dma((2, plan.n)),
            dma((2, plan.turns, plan.groups - 1)),
            dma((plan.workers,)),
            dma((plan.n,)),
            dma((mine, plan.groups)),
            dma((per,)),
        ],
        compiler_params=pltpu.CompilerParams(collective_id=0, has_side_effects=True, vmem_limit_bytes=VMEM_LIMIT),
        name="dispatch",
    )(critic_hidden, target_hidden, critic_small, target_small, *rows_args, *policy)


def norm_parts(pre):
    centered = pre - jnp.sum(pre, -1, keepdims=True) * (1.0 / H)
    inv = lax.rsqrt(jnp.sum(centered * centered, -1, keepdims=True) * (1.0 / H) + 1e-05)
    return centered * inv, inv


def swish_parts(half):
    t = jnp.tanh(half)
    product = half * t
    return half + product, (1.0 + t) * (1.0 + (half - product))


def low_input(params):
    return jnp.where(iota((32, H), 0) < IN, params, 0.0).astype(BF16)


def tile_span(t):
    return pl.ds(pl.multiple_of(t * TILE, TILE), TILE)


def target_kernel(
    plan, width, role_ref, x_ref, w_ref, p_ref, xc_ref, q_ref, info_ref, rows_f, picked, value, hot, win, par, cnt_v, cnt_s, base_s, sem
):
    critic, group, active = role_ref[0], role_ref[1], role_ref[2]
    groups, n = plan.groups, plan.n
    pairs = x_ref.shape[1]
    first = x_ref[:, 0, :].astype(F32)
    lane = iota(first.shape, 1)
    counts = 2.0 * jnp.sum(jnp.where(lane == L_CNT, first, 0.0), -1, keepdims=True) + jnp.sum(
        jnp.where(lane == L_CNT + 1, first, 0.0), -1, keepdims=True
    )
    counts = jnp.where(active > 0, jnp.broadcast_to(counts, first.shape), 0.0)
    mine = jnp.floor((counts + (groups - 1 - group).astype(F32)) * (1.0 / groups) + 0.5 / groups)
    earlier = (iota((n, n), 1) < iota((n, n), 0)).astype(F32).astype(BF16)
    starts = nn(earlier, mine.astype(BF16))
    total = jnp.sum(counts, 0, keepdims=True)
    cnt_v[0:n, :] = mine.astype(I32)
    cnt_v[n : 2 * n, :] = starts.astype(I32)
    cnt_v[2 * n : 2 * n + 8, :] = jnp.broadcast_to(total, (8, LANES)).astype(I32)
    copy = pltpu.make_async_copy(cnt_v, cnt_s, sem)
    copy.start()
    par[...] = assemble(p_ref, width, 0)
    win[...] = jnp.zeros_like(win)
    win[0:32, :] = low_input(par[...])
    copy.wait()
    number = cnt_s[n - 1, 0] + cnt_s[2 * n - 1, 0]
    tiles = (number + TILE - 1) // TILE
    info_ref[0] = number
    info_ref[1] = cnt_s[2 * n, 0]

    def compact(s, _):
        block = x_ref[s].astype(F32)
        have, start = cnt_s[s, 0], cnt_s[n + s, 0]
        rows_f[pl.ds(start, pairs), :] = block
        rows_f[pl.ds(start + (have + 1) // 2, pairs), :] = pltpu.roll(block, HALF, 1)
        return 0

    @pl.when(active > 0)
    def _():
        lax.fori_loop(0, n, compact, 0)

    rows_f[pl.ds(number, TILE), :] = jnp.zeros((TILE, LANES), F32)

    until = (iota((TILE, TILE), 1) < iota((TILE, TILE), 0)).astype(F32).astype(BF16)
    place = iota((TILE, TILE), 1).astype(F32)
    this = critic.astype(F32)

    def choose(t, base):
        wide = rows_f[tile_span(t), :]
        x = wide.astype(BF16)
        xc_ref[tile_span(t), :] = x
        wanted = jnp.logical_or(wide[:, L_S0 : L_S0 + 1] == this, wide[:, L_S1 : L_S1 + 1] == this)
        wanted = jnp.where(jnp.logical_and(wanted, wide[:, L_BOOT : L_BOOT + 1] > 0.0), 1.0, 0.0)
        order = nn(until, jnp.broadcast_to(wanted, (TILE, LANES)).astype(BF16))[:, 0:1]
        chosen = (jnp.where(wanted > 0.0, order, -1.0) == place).astype(F32).astype(BF16)
        hot[t] = chosen
        picked[pl.ds(base, TILE), :] = tn(chosen, x)
        base_s[t] = base
        return base + jnp.sum(wanted).astype(I32)

    chosen_rows = lax.fori_loop(0, tiles, choose, 0)
    picked[pl.ds(chosen_rows, TILE), :] = jnp.zeros((TILE, LANES), F32)
    chosen_tiles = (chosen_rows + TILE - 1) // TILE
    half = jnp.where(iota((32, 1), 0) < IN + 4, 0.5, 1.0)
    par[...] = par[...] * half
    gain1, shift1, gain2, shift2, head = (par[IN + k : IN + k + 1, :] for k in range(5))

    def tile(t, _):
        x = pltpu.roll(picked[tile_span(t), :], LANES - L_TGT, 1).astype(BF16)
        z, _unused = norm_parts(nn(x, win[...]))
        y = z * gain1 + shift1
        act = (y + y * jnp.tanh(y)).astype(BF16)
        z, _unused = norm_parts(nn(act, w_ref[...]))
        y = z * gain2 + shift2
        q = jnp.sum((y + y * jnp.tanh(y)) * head, -1, keepdims=True)
        value[tile_span(t), :] = jnp.broadcast_to(q, (TILE, LANES))
        return 0

    lax.fori_loop(0, chosen_tiles, tile, 0)
    value[tile_span(chosen_tiles), :] = jnp.zeros((TILE, LANES), F32)

    def spread(t, _):
        lane = iota((TILE, LANES), 1)
        high, mid, rest = (v.astype(F32) for v in split3(value[pl.ds(base_s[t], TILE), :]))
        parts = jnp.where(lane == 0, high, jnp.where(lane == 1, mid, jnp.where(lane == 2, rest, 0.0)))
        q = jnp.broadcast_to(jnp.sum(nn(hot[t], parts.astype(BF16)), -1, keepdims=True), (TILE, LANES))
        for h in range(TILE // LANES):
            flat = jnp.transpose(q[h * LANES : (h + 1) * LANES, :])
            q_ref[pl.ds(t * (TILE // LANES) + h, 1), :] = flat[0:1, :]
        return 0

    lax.fori_loop(0, tiles, spread, 0)


def target_values(plan, rows, width, role, x, weights, params):
    capacity = plan.cap(rows)
    vmem = pl.BlockSpec(memory_space=pltpu.VMEM)
    smem = pl.BlockSpec(memory_space=pltpu.SMEM)
    return pl.pallas_call(
        functools.partial(target_kernel, plan, width),
        out_shape=(
            jax.ShapeDtypeStruct((capacity, LANES), BF16),
            jax.ShapeDtypeStruct((capacity // LANES, LANES), F32),
            jax.ShapeDtypeStruct((2,), I32),
        ),
        in_specs=[smem, vmem, vmem, vmem],
        out_specs=(vmem, vmem, smem),
        scratch_shapes=[
            pltpu.VMEM((capacity + TILE + x.shape[1], LANES), F32),
            pltpu.VMEM((capacity + TILE, LANES), F32),
            pltpu.VMEM((capacity + TILE, LANES), F32),
            pltpu.VMEM((capacity // TILE, TILE, TILE), BF16),
            pltpu.VMEM((LANES, H), BF16),
            pltpu.VMEM((32, H), F32),
            pltpu.VMEM((2 * plan.n + 8, LANES), I32),
            pltpu.SMEM((2 * plan.n + 8, LANES), I32),
            pltpu.SMEM((capacity // TILE,), I32),
            pltpu.SemaphoreType.DMA,
        ],
        compiler_params=pltpu.CompilerParams(vmem_limit_bytes=VMEM_LIMIT),
        name="target_values",
    )(role, x, weights, params)


def share_kernel(plan, q_ref, all_ref, send, recv):
    dp, mp = lax.axis_index("dp"), lax.axis_index("mp")
    me = plan.rank(dp, mp)
    groups = plan.groups
    critic, group = me // groups, me % groups
    barrier = pltpu.get_barrier_semaphore()

    @pl.when(me < plan.workers)
    def _():
        def peer(i):
            other = (critic + i) % CRIT
            return other, plan.place(other * groups + group)

        def tell(i, _):
            pl.semaphore_signal(barrier, inc=1, device_id=peer(i)[1], device_id_type=MESH)
            return 0

        lax.fori_loop(1, CRIT, tell, 0)
        pl.semaphore_wait(barrier, CRIT - 1)
        all_ref[critic] = q_ref[...]

        def copy(i):
            other, device = peer(i)
            return pltpu.make_async_remote_copy(
                src_ref=q_ref,
                dst_ref=all_ref.at[critic],
                send_sem=send.at[other],
                recv_sem=recv.at[critic],
                device_id=device,
                device_id_type=MESH,
            )

        def start(i, _):
            copy(i).start()
            return 0

        lax.fori_loop(1, CRIT, start, 0)

        def finish(i, _):
            copy(i).wait_send()
            other = peer(i)[0]
            pltpu.make_async_copy(q_ref, all_ref.at[other], recv.at[other]).wait()
            return 0

        lax.fori_loop(1, CRIT, finish, 0)


def share_values(plan, q):
    vmem = pl.BlockSpec(memory_space=pltpu.VMEM)
    return pl.pallas_call(
        functools.partial(share_kernel, plan),
        out_shape=jax.ShapeDtypeStruct((CRIT,) + q.shape, F32),
        in_specs=[vmem],
        out_specs=vmem,
        scratch_shapes=[pltpu.SemaphoreType.DMA((CRIT,)), pltpu.SemaphoreType.DMA((CRIT,))],
        compiler_params=pltpu.CompilerParams(collective_id=1, has_side_effects=True, vmem_limit_bytes=VMEM_LIMIT),
        name="share_values",
    )(q)


def critic_kernel(
    plan, width, info_ref, xc_ref, q_ref, w_ref, p_ref, grad_ref, small_ref, sums_ref, z_one, slope, act, low, fact, par, win, picks, acc
):
    number = info_ref[0]
    scale = 2.0 / jnp.maximum(info_ref[1], 1).astype(F32)
    tiles = (number + TILE - 1) // TILE
    par[...] = assemble(p_ref, width, HALF)
    win[...] = jnp.zeros_like(win)
    win[0:32, :] = low_input(par[...])
    grad_ref[...] = jnp.zeros_like(grad_ref)
    acc[...] = jnp.zeros_like(acc)
    picks[...] = jnp.zeros_like(picks)
    sums_ref[...] = jnp.zeros_like(sums_ref)
    gain1, shift1, gain2, shift2, head = (par[IN + k : IN + k + 1, :] for k in range(5))

    def fold(k, value):
        acc[32 + k * 8 : 40 + k * 8, :] += jnp.sum(value.reshape(TILE // 8, 8, H), 0)

    def tile(t, _):
        x = xc_ref[tile_span(t), :]
        wide = x.astype(F32)
        for h in range(TILE // LANES):
            picks[0:CRIT, :] = q_ref[:, pl.ds(t * (TILE // LANES) + h, 1), :].reshape(CRIT, LANES)
            table = jnp.transpose(picks[...])
            part = wide[h * LANES : (h + 1) * LANES, :]
            critic = iota(table.shape, 1).astype(F32)
            one = jnp.sum(jnp.where(critic == part[:, L_S0 : L_S0 + 1], table, 0.0), -1, keepdims=True)
            two = jnp.sum(jnp.where(critic == part[:, L_S1 : L_S1 + 1], table, 0.0), -1, keepdims=True)
            base = part[:, L_BASE : L_BASE + 1] + part[:, L_BASE + 1 : L_BASE + 2] + part[:, L_BASE + 2 : L_BASE + 3]
            goal = base + jnp.where(part[:, L_BOOT : L_BOOT + 1] > 0.0, REWARD_DISCOUNT * jnp.minimum(one, two), 0.0)
            fact[h * LANES : (h + 1) * LANES, 0:1] = goal
        z, inv_one = norm_parts(nn(x, win[...]))
        z_one[...] = z
        value, twice = swish_parts(z * (0.5 * gain1) + 0.5 * shift1)
        slope[...] = 0.5 * twice
        act[...] = value.astype(BF16)
        z, inv = norm_parts(nn(act[...], w_ref[...]))
        value, twice = swish_parts(z * (0.5 * gain2) + 0.5 * shift2)
        q = jnp.sum(value * head, -1, keepdims=True)
        error = (q - fact[:, 0:1]) * wide[:, L_VALID : L_VALID + 1]
        sums_ref[0:1, :] += jnp.broadcast_to(jnp.sum(error * error, 0, keepdims=True), (1, LANES))
        dq = error * scale
        fold(4, dq * value)
        dy = dq * (twice * (0.5 * head))
        fold(3, dy)
        fold(2, dy * z)
        dz = dy * gain2
        mean = jnp.sum(dz, -1, keepdims=True) * (1.0 / H)
        along = jnp.sum(dz * z, -1, keepdims=True) * (1.0 / H)
        low[...] = (inv * (dz - mean - z * along)).astype(BF16)
        down = nt(low[...], w_ref[...])
        grad_ref[...] += tn(act[...], low[...])
        z = z_one[...]
        dy = down * slope[...]
        fold(1, dy)
        fold(0, dy * z)
        dz = dy * gain1
        mean = jnp.sum(dz, -1, keepdims=True) * (1.0 / H)
        along = jnp.sum(dz * z, -1, keepdims=True) * (1.0 / H)
        acc[0:32, :] += tn(x[:, 0:32], (inv_one * (dz - mean - z * along)).astype(BF16))
        return 0

    lax.fori_loop(0, tiles, tile, 0)
    sums_ref[1:2, :] = jnp.broadcast_to(info_ref[1].astype(F32), (1, LANES))
    for k in range(5):
        acc[IN + k : IN + k + 1, :] = jnp.sum(acc[32 + k * 8 : 40 + k * 8, :], 0, keepdims=True)
    for i in range(H // width):
        start, offset = i * width // LANES * LANES, i * width % LANES
        block = acc[0:32, start : start + LANES]
        small_ref[i] = pltpu.roll(block, LANES - offset, 1) if offset else block


def critic_step(plan, width, info, xc, q_all, weights, params):
    vmem = pl.BlockSpec(memory_space=pltpu.VMEM)
    smem = pl.BlockSpec(memory_space=pltpu.SMEM)
    return pl.pallas_call(
        functools.partial(critic_kernel, plan, width),
        out_shape=(
            jax.ShapeDtypeStruct((H, H), F32),
            jax.ShapeDtypeStruct((H // width, 32, LANES), F32),
            jax.ShapeDtypeStruct((8, LANES), F32),
        ),
        in_specs=[smem] + [vmem] * 4,
        out_specs=(vmem,) * 3,
        scratch_shapes=[
            pltpu.VMEM((TILE, H), F32),
            pltpu.VMEM((TILE, H), F32),
            pltpu.VMEM((TILE, H), BF16),
            pltpu.VMEM((TILE, H), BF16),
            pltpu.VMEM((TILE, LANES), F32),
            pltpu.VMEM((32, H), F32),
            pltpu.VMEM((LANES, H), BF16),
            pltpu.VMEM((16, LANES), F32),
            pltpu.VMEM((72, H), F32),
        ],
        compiler_params=pltpu.CompilerParams(vmem_limit_bytes=VMEM_LIMIT),
        name="critic_step",
    )(info, xc, q_all, weights, params)


PRECISE = 2


LAG = 2


def shampoo_kernel(
    plan,
    g_ref,
    small_ref,
    sums_ref,
    mom_ref,
    left_ref,
    right_ref,
    w_ref,
    mo_ref,
    lo_ref,
    ro_ref,
    wo_ref,
    own_ref,
    out_ref,
    parts,
    pieces,
    given,
    shares,
    totals,
    send_one,
    recv_one,
    send_two,
    recv_two,
    send_s,
    recv_s,
    send_t,
    recv_t,
):
    dp, mp = lax.axis_index("dp"), lax.axis_index("mp")
    me = plan.rank(dp, mp)
    index = dp * plan.n_mp + mp
    groups, workers, n, turns = plan.groups, plan.workers, plan.n, plan.turns
    critic, group = me // groups, me % groups
    rw, cw = mom_ref.shape[1], mom_ref.shape[2]
    mine, per = shares.shape[1], small_ref.shape[0]
    columns = own_ref.shape[1]
    chunk_width = H // per
    all_barrier(plan, dp, mp)

    def to_device(src, dst, send, recv, device):
        return pltpu.make_async_remote_copy(
            src_ref=src, dst_ref=dst, send_sem=send, recv_sem=recv, device_id=device, device_id_type=MESH
        )

    def block(s):
        sdp, smp = plan.device(s)
        return pl.ds(pl.multiple_of(smp * rw, rw), rw), pl.ds(pl.multiple_of(sdp * cw, cw), cw)

    def turn_of(step):
        return (step + critic) % turns

    def first_hop(step, i):
        other = (group + 1 + i) % groups
        turn = turn_of(step)
        s = other + groups * turn
        copy = to_device(
            g_ref.at[block(s)],
            parts.at[groups - 2 - i, turn],
            send_one.at[step, i],
            recv_one.at[groups - 2 - i, turn],
            plan.place(critic * groups + other),
        )
        return s, copy

    def second_hop(turn):
        s = group + groups * turn
        return s, to_device(pieces.at[turn], given.at[critic], send_two.at[turn], recv_two.at[critic], plan.device(s))

    def small_hop(q):
        g = critic * per + q
        s = g // mine
        return s, to_device(
            small_ref.at[q], shares.at[group, g % mine], send_s.at[q], recv_s.at[group, g % mine], plan.device(s)
        )

    def total_hop(s):
        return to_device(sums_ref, totals.at[me], send_t.at[s], recv_t.at[me], plan.device(s))

    @pl.when(me < workers)
    def _():
        def start(step, _):
            def one(i, _):
                s, copy = first_hop(step, i)

                @pl.when(s < n)
                def _():
                    copy.start()

                return 0

            lax.fori_loop(0, groups - 1, one, 0)
            return 0

        lax.fori_loop(0, turns, start, 0)

        def start_small(q, _):
            s, copy = small_hop(q)

            @pl.when(s == index)
            def _():
                slot = (critic * per + q) % mine
                pltpu.make_async_copy(small_ref.at[q], shares.at[group, slot], recv_s.at[group, slot]).start()

            @pl.when(s != index)
            def _():
                copy.start()

            return 0

        lax.fori_loop(0, per, start_small, 0)
        totals[me] = sums_ref[...]

        def start_total(i, _):
            total_hop((index + i) % n).start()
            return 0

        lax.fori_loop(1, n, start_total, 0)

    def add_up(step):
        turn = turn_of(step)
        s, copy = second_hop(turn)

        @pl.when(s < n)
        def _():
            for i in range(groups - 1):
                pltpu.make_async_copy(pieces.at[0], parts.at[i, turn], recv_one.at[i, turn]).wait()
            value = g_ref[block(s)]
            for i in range(groups - 1):
                value = value + parts[i, turn]
            pieces[turn] = value

            @pl.when(s == index)
            def _():
                pltpu.make_async_copy(pieces.at[turn], given.at[critic], recv_two.at[critic]).start()

            @pl.when(s != index)
            def _():
                copy.start()

    width = min(256, cw)
    many = width // BLK
    nr, nc = rw // BLK, cw // width
    subs = [(i, j) for i in range(nr) for j in range(nc)]
    mask = (iota((width, width), 0) // BLK == iota((width, width), 1) // BLK).astype(F32).astype(BF16)
    eye = (iota((BLK, width), 0) == iota((BLK, width), 1) % BLK).astype(F32)
    eye_low = eye.astype(BF16)

    def diag(x):
        return jnp.concatenate([x] * many, 0) * mask

    def precise(a, b):
        ah, al = split2(a)
        bh, bl = split2(b)
        both = nn(jnp.concatenate([ah, al], 0), diag(bh))
        return both[:BLK] + both[BLK:] + nn(ah, diag(bl))

    def block_sums(s):
        high, rest = split2(s)
        return nn(high, mask) + nn(rest, mask)

    def place(c, i, j):
        return (c, slice(i * BLK, (i + 1) * BLK), slice(j * width, (j + 1) * width))

    def blocked(i):
        c = (index // groups + 2 * CRIT - i) % CRIT
        pltpu.make_async_copy(pieces.at[0], given.at[c], recv_two.at[c]).wait()
        sums = []
        for i, j in subs:
            at = place(c, i, j)
            grad = given[at]
            mo_ref[at] = MOMENTUM * mom_ref[at] + grad
            low = grad.astype(BF16)
            wide = diag(low)
            left = STAT_DECAY * left_ref[at] + (1.0 - STAT_DECAY) * nt(low, wide)
            flip = nt(eye_low, wide).astype(BF16)
            right = STAT_DECAY * right_ref[at] + (1.0 - STAT_DECAY) * nn(flip, wide)
            lo_ref[at] = left
            ro_ref[at] = right
            for stat in (left, right):
                sums.append(jnp.sum((stat * stat).reshape(BLK // 8, 8, width), 0))
        total = block_sums(jnp.concatenate(sums, 0))
        chains = []
        for k, (i, j) in enumerate(subs):
            for side, ref in enumerate((lo_ref, ro_ref)):
                spot = (2 * k + side) * 8
                inv = lax.rsqrt(jnp.sum(total[spot : spot + 8], 0, keepdims=True))
                rest = (eye - ref[place(c, i, j)] * inv) * 0.25
                chains.append([rest, eye + rest, jnp.sqrt(jnp.sqrt(inv))])
        for it in range(NEWTON - 1):
            full = it < PRECISE
            work = []
            for ch in chains:
                high, rest = split2(ch[0])
                wide = diag(high)
                wide_rest = diag(rest) if full else None
                lhs = [high] + ([rest] if full else []) + ([ch[1].astype(BF16)] if it > 0 else [])
                out = nn(jnp.concatenate(lhs, 0), wide)
                power = out[:BLK]
                if full:
                    power = power + out[BLK : 2 * BLK] + nn(high, wide_rest)
                if it > 0:
                    ch[1] = ch[1] + out[-BLK:]
                work.append([wide, wide_rest, power])
            for factor in (3.75, 5.0, 2.5):
                for ch, wk in zip(chains, work):
                    high, rest = split2(factor * ch[0] + wk[2])
                    if full:
                        out = nn(jnp.concatenate([high, rest], 0), wk[0])
                        wk[2] = out[:BLK] + out[BLK:] + nn(high, wk[1])
                    else:
                        wk[2] = nn(high, wk[0])
            for ch, wk in zip(chains, work):
                ch[0] = wk[2]
        for ch in chains:
            ch[1] = ch[1] + nn(ch[1].astype(BF16), diag(ch[0].astype(BF16)))
        for k, (i, j) in enumerate(subs):
            at = place(c, i, j)
            lc, rc = chains[2 * k], chains[2 * k + 1]
            step = precise(precise(lc[1], mo_ref[at]), rc[1]) * (lc[2] * rc[2])
            squares = block_sums(jnp.sum((step * step).reshape(BLK // 8, 8, width), 0))
            square = jnp.sum(squares, 0, keepdims=True) * (1.0 / (BLK * BLK))
            old = w_ref[at]
            wo_ref[at] = old - RATE_HIDDEN * (step * lax.rsqrt(square + 1e-06) + WEIGHT_DECAY * old)

    def round_(i, _):
        @pl.when(jnp.logical_and(me < workers, i < turns))
        def _():
            add_up(i)

        @pl.when(jnp.logical_and(i >= LAG, i < CRIT + LAG))
        def _():
            blocked(i - LAG)

        return 0

    lax.fori_loop(0, max(turns, CRIT + LAG), round_, 0)

    def arrived_small(i, _):
        pltpu.make_async_copy(small_ref.at[0], shares.at[i // mine, i % mine], recv_s.at[i // mine, i % mine]).wait()
        return 0

    lax.fori_loop(0, groups * mine, arrived_small, 0)
    for g in range(columns // LANES):
        part = jnp.zeros((32, LANES), F32)
        for j in range(mine):
            if j * chunk_width // LANES == g:
                value = shares[0, j]
                for r in range(1, groups):
                    value = value + shares[r, j]
                turn = j * chunk_width % LANES
                moved = pltpu.roll(value, turn, 1) if turn else value
                part = jnp.where(iota((32, LANES), 1) // chunk_width == turn // chunk_width, moved, part)
        own_ref[:, g * LANES : (g + 1) * LANES] = part

    def arrived_total(k, _):
        @pl.when(k != me)
        def _():
            pltpu.make_async_copy(sums_ref, totals.at[k], recv_t.at[k]).wait()

        return 0

    lax.fori_loop(0, workers, arrived_total, 0)
    out_ref[0:1, :] = jnp.sum(totals[:, 0, :], 0, keepdims=True)
    out_ref[1:2, :] = totals[0, 1:2, :]
    out_ref[2:8, :] = jnp.zeros((6, LANES), F32)

    @pl.when(me < workers)
    def _():
        def finish(step, _):
            def one(i, _):
                s, copy = first_hop(step, i)

                @pl.when(s < n)
                def _():
                    copy.wait_send()

                return 0

            lax.fori_loop(0, groups - 1, one, 0)
            s, copy = second_hop(step)

            @pl.when(jnp.logical_and(s < n, s != index))
            def _():
                copy.wait_send()

            return 0

        lax.fori_loop(0, turns, finish, 0)

        def finish_small(q, _):
            s, copy = small_hop(q)

            @pl.when(s != index)
            def _():
                copy.wait_send()

            return 0

        lax.fori_loop(0, per, finish_small, 0)

        def finish_total(i, _):
            total_hop((index + i) % n).wait_send()
            return 0

        lax.fori_loop(1, n, finish_total, 0)


def shampoo(plan, columns, grad, small, sums, moment, left, right, weight):
    vmem = pl.BlockSpec(memory_space=pltpu.VMEM)
    shape = jax.ShapeDtypeStruct(moment.shape, F32)
    _width, mine, per = chunks_of(columns)
    piece = moment.shape[1:]
    dma = pltpu.SemaphoreType.DMA
    return pl.pallas_call(
        functools.partial(shampoo_kernel, plan),
        out_shape=(shape,) * 4
        + (jax.ShapeDtypeStruct((32, -(-columns // LANES) * LANES), F32), jax.ShapeDtypeStruct((8, LANES), F32)),
        in_specs=[vmem] * 7,
        out_specs=(vmem,) * 6,
        scratch_shapes=[
            pltpu.VMEM((plan.groups - 1, plan.turns) + piece, F32),
            pltpu.VMEM((plan.turns,) + piece, F32),
            pltpu.VMEM((CRIT,) + piece, F32),
            pltpu.VMEM((plan.groups, mine, 32, LANES), F32),
            pltpu.VMEM((plan.workers, 8, LANES), F32),
            dma((plan.turns, plan.groups - 1)),
            dma((plan.groups - 1, plan.turns)),
            dma((plan.turns,)),
            dma((CRIT,)),
            dma((per,)),
            dma((plan.groups, mine)),
            dma((plan.n,)),
            dma((plan.workers,)),
        ],
        compiler_params=pltpu.CompilerParams(collective_id=2, has_side_effects=True, vmem_limit_bytes=VMEM_LIMIT),
        name="shampoo",
    )(grad, small, sums, moment, left, right, weight)


def adamw(grad, moment, square, weight, rate):
    moment_new = FIRST_DECAY * moment + (1.0 - FIRST_DECAY) * grad
    square_new = SECOND_DECAY * square + (1.0 - SECOND_DECAY) * grad * grad
    moment_hat = moment_new / (1.0 - FIRST_DECAY**STEP)
    square_hat = square_new / (1.0 - SECOND_DECAY**STEP)
    weight_new = weight - rate * (moment_hat / (jnp.sqrt(square_hat) + 1e-08) + WEIGHT_DECAY * weight)
    return (moment_new, square_new, weight_new)


def local(
    plan,
    state_action,
    next_state,
    reward,
    done_flags,
    noise_index,
    noise_table,
    subsets,
    policy_in,
    policy_mid,
    policy_out,
    critic_in,
    in_first,
    in_second,
    critic_norms,
    norm_first,
    norm_second,
    critic_head,
    head_first,
    head_second,
    critic_hidden,
    hidden_moment,
    left_stats,
    right_stats,
    target_in,
    target_norms,
    target_head,
    target_hidden,
):
    me = plan.rank(lax.axis_index("dp"), lax.axis_index("mp"))
    critic, group = me // plan.groups, me % plan.groups
    role = jnp.stack([critic, group, (me < plan.workers).astype(I32)])
    rows, columns = state_action.shape[0], critic_in.shape[1]
    width = chunks_of(columns)[0]
    facts = jnp.stack([reward, done_flags.astype(F32), noise_index.astype(F32)])
    facts = jnp.pad(facts, ((0, 5), (0, 0)))
    w_target, w_critic, x, params = dispatch(
        plan,
        critic_hidden,
        target_hidden,
        (critic_in, critic_norms, critic_head[None]),
        (target_in, target_norms, target_head[None]),
        (state_action, next_state, facts, subsets),
        (noise_table, policy_in, policy_mid, policy_out),
    )
    xc, q, info = target_values(plan, rows, width, role, x, w_target, params)
    q_all = share_values(plan, q)
    grad_hidden, grad_small, sums = critic_step(plan, width, info, xc, q_all, w_critic, params)
    hidden_momentum, left_renewed, right_renewed, hidden_updated, own, totals = shampoo(
        plan, columns, grad_hidden, grad_small, sums, hidden_moment, left_stats, right_stats, critic_hidden
    )
    own = own[:, :columns]
    loss_total, counted = totals[0, 0], totals[1, 0]
    in_moment, in_square, in_updated = adamw(own[:IN], in_first, in_second, critic_in, RATE_INPUT)
    norm_moment, norm_square, norm_updated = adamw(own[IN : IN + 4], norm_first, norm_second, critic_norms, RATE_NORMS)
    head_moment, head_square, head_updated = adamw(own[IN + 4], head_first, head_second, critic_head, RATE_HEAD)
    return (
        loss_total,
        counted,
        in_moment,
        in_square,
        in_updated,
        norm_moment,
        norm_square,
        norm_updated,
        head_moment,
        head_square,
        head_updated,
        hidden_momentum,
        left_renewed,
        right_renewed,
        hidden_updated,
    )


def solution(mesh):
    both = ("dp", "mp")
    rows, columns, flat, hidden = P(both, None), P(None, both), P(both), P(None, "mp", "dp")
    return jax.shard_map(
        functools.partial(local, Plan(mesh)),
        mesh=mesh,
        in_specs=(
            (rows, rows, flat, flat, flat, P(), rows, P(), P(), P())
            + (columns,) * 6
            + (flat,) * 3
            + (hidden,) * 4
            + (columns, columns, flat, hidden)
        ),
        out_specs=(P(), P()) + (columns,) * 6 + (flat,) * 3 + (hidden,) * 4,
        check_vma=False,
    )
```

time: 1630 us -> 435 us (0.27)
  waiting for transfers between devices: 622 us -> 0 us
  matrix products: 449 us -> 0 us
  Pallas kernels: 0 us -> 408 us
  blocking collectives: 244 us -> 0 us
  other arithmetic: 161 us -> 6.65 us
  local copies, waits for them, and re-layouts: 123 us -> 19.2 us
    dot_general x48 -> x0, matrix products: 449 us -> none  [the longest x36 258 us: matmul(): return jnp.einsum('...ij,...jk->...ik', left, right, precision=HIGHEST)]
    pallas_call x0 -> x5, Pallas kernels: none -> 408 us  [the longest x1 230 us: shampoo(): pl.pallas_call(functools.partial(shampoo_kernel, plan), out_shape=(shape,...]
    reduce_scatter x2 -> x0, waiting for transfers between devices: 351 us -> none  [the longest x1 301 us: local(): lax.psum_scatter(grad_hidden, 'mp', scatter_dimension=1, tiled=True)]
    unnamed x10 -> x0, waiting for transfers between devices: 221 us -> none
    all_gather x4 -> x0, blocking collectives: 161 us -> none  [the longest x1 42.5 us: local(): lax.all_gather(critic_in, ('dp', 'mp'), axis=1, tiled=True)]
    reduce_sum x13 -> x0, other arithmetic: 107 us -> none  [the longest x4 31.4 us: norm_forward(): jnp.mean(centered * centered, -1, keepdims=True) + 1e-05]
    reshape x7 -> x0, local copies, waits for them, and re-layouts: 59.6 us -> none  [the longest x2 41.7 us: critic_forward(): jnp.dot(inputs, weight_in, preferred_element_type=jnp.float32)]
    all_gather x4 -> x0, waiting for transfers between devices: 50 us -> none  [the longest x1 26.3 us: local(): lax.all_gather(critic_hidden.astype(jnp.bfloat16), 'dp', axis=2, tiled=True)]
  transfers between devices with their start and end apart: 8 -> 0, of which waited for: 6 -> 0; matrix products, arithmetic and copies ran while one was open for 16% -> 0% of each run, Pallas kernels for 0% -> 0%
where the time goes in v1:
time: 435 us; the launch traced here: 434 us
  Pallas kernels  408 us (94%)
  local copies, waits for them, and re-layouts  19.2 us (4%)
  other arithmetic  6.65 us (2%)
    pallas_call x1, Pallas kernels, shampoo(): pl.pallas_call(functools.partial(shampoo_kernel, plan), out_shape=(shape,...  230 us
    pallas_call x1, Pallas kernels, dispatch(): pl.pallas_call(functools.partial(dispatch_kernel, plan), out_shape=(jax.S...  75.4 us
    pallas_call x1, Pallas kernels, critic_step(): pl.pallas_call(functools.partial(critic_kernel, plan, width), out_shape=(...  49.4 us
    pallas_call x1, Pallas kernels, share_values(): pl.pallas_call(functools.partial(share_kernel, plan), out_shape=jax.Shape...  30.9 us
    pallas_call x1, Pallas kernels, target_values(): pl.pallas_call(functools.partial(target_kernel, plan, width), out_shape=(...  22.3 us
    unnamed x33, local copies, waits for them, and re-layouts  14.8 us

profile of v1, /device:TPU:9, one launch (start us, length us, event | category | flops | bytes accessed | tf_op | source)
XLA Modules:
  0.0 434.4 jit_solution(14454202173842300088)
XLA Ops:
  0.7 0.6 pad_add_fusion.role_ref
  1.3 1.2 broadcast_in_dim.7.targ_small_2_
  2.6 1.2 broadcast_in_dim.6.crit_small_2_
  3.8 0.7 convert_element_type.9
  4.5 0.7 convert_element_type.10
  5.2 1.3 select_maximum_fusion.rows_ref
  6.5 1.4 copy.46.pout_ref
  7.9 1.5 copy.42.sa_ref
  9.4 1.5 copy.43.ns_ref
  11.0 1.5 copy.45.table_ref
  12.4 1.5 copy.44.subs_ref
  14.0 75.4 %dispatch.1 = (bf16[1024,1024]{1,0:T(8,128)(2,1)}, bf16[1024,1024]{1,0:T(8,128)(2,1)}, bf16[32,96,128]{2,1,0:T(8,128)(2,1)}, f32[16,32,128]{2,1,0:T(8,128)}) custom-call(f32[10,64,512]{2,1,0:T(8,128)} %w_ref.1, f32[10,64,512]{2,1,0:T(8,128)} %targ_ref.1, f32[23,320]{1,0:T(8,128)} %crit_small_0_.1, f32[4,320]{1,0:T(4,128)} %crit_small_1_.1, ...), custom_call_target="tpu_custom_call" | custom-call | tf_op jit(solution)/shard_map/dispatch/pallas_call | solution.py:439
  89.4 22.3 %target_values.1 = (bf16[5632,128]{1,0:T(8,128)(2,1)}, f32[44,128]{1,0:T(8,128)}, s32[2]{0:T(128)}) custom-call(s32[3]{0:T(128)} %pad_add_fusion.role_ref, bf16[32,96,128]{2,1,0:T(8,128)(2,1)} %get-tuple-element.31.x_ref, bf16[1024,1024]{1,0:T(8,128)(2,1)} %get-tuple-element.32.w_ref, f32[16,32,128]{2,1,0:T(8,128)} %get-tuple-element.33.p_ref), custom_call_target="tpu_custom_call" | custom-call | tf_op jit(solution)/shard_map/target_values/pallas_call | solution.py:585
  111.7 30.9 %share_values.1.q_ref = f32[10,44,128]{2,1,0:T(8,128)} custom-call(f32[44,128]{1,0:T(8,128)} %get-tuple-element.36.q_ref), custom_call_target="tpu_custom_call" | custom-call | tf_op jit(solution)/shard_map/share_values/pallas_call | solution.py:660
  142.6 49.4 %critic_step.1 = (f32[1024,1024]{1,0:T(8,128)}, f32[16,32,128]{2,1,0:T(8,128)}, f32[8,128]{1,0:T(8,128)}) custom-call(s32[2]{0:T(128)} %get-tuple-element.34.info_ref, bf16[5632,128]{1,0:T(8,128)(2,1)} %get-tuple-element.35.xc_ref, f32[10,44,128]{2,1,0:T(8,128)} %share_values.1.q_ref, bf16[1024,1024]{1,0:T(8,128)(2,1)} %get-tuple-element.37.w_ref, ...), custom_call_target="tpu_custom_call" | custom-call | tf_op jit(solution)/shard_map/critic_step/pallas_call | solution.py:746
  192.0 0.0 copy-start.6
  192.0 0.0 copy-start.8
  192.0 0.0 copy-start.9
  192.0 0.0 copy-start.3
  192.0 0.0 copy-start.5
  192.0 229.7 %shampoo.1 = (f32[10,64,512]{2,1,0:T(8,128)}, f32[10,64,512]{2,1,0:T(8,128)}, f32[10,64,512]{2,1,0:T(8,128)}, f32[10,64,512]{2,1,0:T(8,128)}, f32[32,384]{1,0:T(8,128)}, /*index=5*/f32[8,128]{1,0:T(8,128)}) custom-call(f32[1024,1024]{1,0:T(8,128)} %get-tuple-element.38.g_ref, f32[16,32,128]{2,1,0:T(8,128)} %get-tuple-element.39.small_ref, ...), custom_call_target="tpu_custom_call" | custom-call | tf_op jit(solution)/shard_map/shampoo/pallas_call | solution.py:1091
  421.7 1.3 fusion.6
  423.0 0.7 slice_reduce_fusion
  423.7 0.6 multiply_subtract_fusion.2
  424.3 1.4 multiply_subtract_fusion.1
  425.7 1.4 multiply_subtract_fusion
  427.1 2.6 copy.51
  429.7 1.1 copy.52
  430.8 0.7 copy-done.1
  431.5 1.1 copy.53
  432.6 0.7 copy-done
  433.3 1.1 copy.54
  (17 shorter events, 0.0 us)
Async XLA Ops:
  192.0 231.7 %copy-start.7 = (f32[320]{0:T(512)S(1)}, f32[320]{0:T(512)}, u32[]{:S(2)}) copy-start(f32[320]{0:T(512)} %param.43) | copy-start | bytes 3844
  192.0 231.7 %copy-start.10 = (f32[320]{0:T(512)S(1)}, f32[320]{0:T(512)}, u32[]{:S(2)}) copy-start(f32[320]{0:T(512)} %param.45) | copy-start | bytes 3844
  192.0 231.8 %copy-start.11 = (f32[320]{0:T(512)S(1)}, f32[320]{0:T(512)}, u32[]{:S(2)}) copy-start(f32[320]{0:T(512)} %param.44) | copy-start | bytes 3844
  192.0 232.4 %copy-start.6 = (f32[4,320]{1,0:T(4,128)S(1)}, f32[4,320]{1,0:T(4,128)}, u32[]{:S(2)}) copy-start(f32[4,320]{1,0:T(4,128)} %crit_small_1_.1) | copy-start | bytes 15364
  192.0 232.4 %copy-start.8 = (f32[4,320]{1,0:T(4,128)S(1)}, f32[4,320]{1,0:T(4,128)}, u32[]{:S(2)}) copy-start(f32[4,320]{1,0:T(4,128)} %param.42) | copy-start | bytes 15364
  192.0 232.3 %copy-start.9 = (f32[4,320]{1,0:T(4,128)S(1)}, f32[4,320]{1,0:T(4,128)}, u32[]{:S(2)}) copy-start(f32[4,320]{1,0:T(4,128)} %param.41) | copy-start | bytes 15364
  192.0 233.7 %copy-start.3 = (f32[23,320]{1,0:T(8,128)S(1)}, f32[23,320]{1,0:T(8,128)}, u32[]{:S(2)}) copy-start(f32[23,320]{1,0:T(8,128)} %crit_small_0_.1) | copy-start | bytes 88324
  192.0 233.7 %copy-start.4 = (f32[23,320]{1,0:T(8,128)S(1)}, f32[23,320]{1,0:T(8,128)}, u32[]{:S(2)}) copy-start(f32[23,320]{1,0:T(8,128)} %param.39) | copy-start | bytes 88324
  192.0 233.7 %copy-start.5 = (f32[23,320]{1,0:T(8,128)S(1)}, f32[23,320]{1,0:T(8,128)}, u32[]{:S(2)}) copy-start(f32[23,320]{1,0:T(8,128)} %param.38) | copy-start | bytes 88324
  427.1 2.6 copy-start.2
  429.7 1.8 copy-start.1
  431.5 1.8 copy-start

commit v2 on v1

--- a/solution.py
+++ b/solution.py
@@ -87,12 +87,24 @@
         size = 4 * self.n_dp
         layer = mp // 4
         inner = dp * 4 + (mp % 4 + 2 * (dp % 2)) % 4
-        return layer * size + inner + (layer % 2) * (size - 1 - 2 * inner)
+        if self.n != 32:
+            return layer * size + inner
+        far, near = layer // 2, jnp.logical_or(layer == 1, layer == 2)
+        six = 24 + 3 * far + jnp.where(near, 2, 0)
+        seven = jnp.where(near, 30 + far, 25 + 3 * far)
+        return jnp.where(inner < 6, 6 * layer + inner, jnp.where(inner == 6, six, seven))
 
     def place(self, k):
         size = 4 * self.n_dp
-        layer, inner = k // size, k % size
-        inner = inner + (layer % 2) * (size - 1 - 2 * inner)
+        if self.n != 32:
+            layer, inner = k // size, k % size
+        else:
+            extra = jnp.maximum(k - 24, 0)
+            which, j = extra // 3, extra % 3
+            layer = jnp.where(which == 0, j // 2, jnp.where(which == 1, 3 - j // 2, 1 + j))
+            inner = jnp.where(which == 2, 7, 6 + j % 2)
+            layer = jnp.where(k < 24, k // 6, layer)
+            inner = jnp.where(k < 24, k % 6, inner)
         dp = inner // 4
         return dp, layer * 4 + (inner % 4 + 2 * (dp % 2)) % 4
 
@@ -148,10 +160,10 @@
     targ_ref,
     crit_small,
     targ_small,
+    head_ref,
     sa_ref,
     ns_ref,
     rows_ref,
-    subs_ref,
     table_ref,
     pin_ref,
     pmid_ref,
@@ -178,7 +190,7 @@
     groups, workers = plan.groups, plan.workers
     critic, group = me // groups, me % groups
     rw, cw = crit_ref.shape[1], crit_ref.shape[2]
-    rows = sa_ref.shape[0]
+    rows = sa_ref.shape[1]
     columns = crit_small[0].shape[1]
     width, mine, per = chunks_of(columns)
     nets = (wt_ref, wc_ref)
@@ -228,7 +240,7 @@
     for t, parts in enumerate((targ_small, crit_small)):
         wide[t, 0:IN, 0:columns] = parts[0][...]
         wide[t, IN : IN + 4, 0:columns] = parts[1][...]
-        wide[t, IN + 4 : IN + 5, 0:columns] = parts[2][...]
+        wide[t, IN + 4 : IN + 5, 0:columns] = head_ref[t : t + 1, :]
     for j in range(mine):
         start, offset = j * width // LANES * LANES, j * width % LANES
         both = [wide[t, :, start : start + LANES] for t in range(2)]
@@ -259,10 +271,10 @@
 
     lane = iota((rows, LANES), 1)
     place = lambda height, offset: (iota((height, LANES), 1) == iota((height, LANES), 0) + offset).astype(F32).astype(BF16)
-    hidden = swish(nn(ns_ref[...], pin_ref[...])).astype(BF16)
+    hidden = swish(tn(ns_ref[...], pin_ref[...])).astype(BF16)
     hidden = swish(nn(hidden, pmid_ref[...])).astype(BF16)
     pout = pout_ref[...]
-    spread = lambda offset: nn(
+    spread = lambda offset: tn(
         pout, (iota((2 * ACT, LANES), 0) == iota((2 * ACT, LANES), 1) + offset).astype(F32).astype(BF16)
     ).astype(BF16)
     keep = lane < ACT
@@ -270,10 +282,10 @@
     raw = nn(hidden, spread(ACT))
     facts = rows_ref[...]
     across = jnp.transpose(facts)
-    picked = (iota((rows, table_ref.shape[0]), 1) == across[:, 2:3].astype(I32)).astype(F32).astype(BF16)
+    picked = (iota((rows, table_ref.shape[1]), 1) == across[:, 2:3].astype(I32)).astype(F32).astype(BF16)
     noise = jnp.zeros((rows, LANES), F32)
     for part in split3(table_ref[...]):
-        noise = noise + nn(picked, nn(part, place(ACT, 0)).astype(BF16))
+        noise = noise + nn(picked, tn(part, place(ACT, 0)).astype(BF16))
     log_std = -5.0 + 3.5 * (jnp.tanh(raw) + 1.0)
     squashed = means + jnp.exp(log_std) * noise
     action = jnp.tanh(squashed).astype(BF16)
@@ -287,18 +299,17 @@
     boot = (done == 0.0).astype(F32)
     base = across[:, 0:1] - (REWARD_DISCOUNT * ENTROPY_TEMP) * boot * density
     high, mid, rest = split3(base)
-    subs = subs_ref[...].astype(F32)
     on = lambda k, value: jnp.where(lane == k, value, 0.0)
     features = (
-        nn(sa_ref[...], place(IN, 0))
-        + nn(ns_ref[...], place(OBS, L_TGT))
+        tn(sa_ref[...], place(IN, 0))
+        + tn(ns_ref[...], place(OBS, L_TGT))
         + nn(jnp.where(keep, action.astype(F32), 0.0).astype(BF16), place(LANES, L_TGT + OBS))
         + on(L_BASE, high.astype(F32))
         + on(L_BASE + 1, mid.astype(F32))
         + on(L_BASE + 2, rest.astype(F32))
         + on(L_BOOT, boot)
-        + on(L_S0, subs[:, 0:1])
-        + on(L_S1, subs[:, 1:2])
+        + on(L_S0, across[:, 3:4])
+        + on(L_S1, across[:, 4:5])
         + on(L_VALID, 1.0)
     ).astype(BF16)
 
@@ -428,8 +439,8 @@
     lax.fori_loop(0, workers, sent_rows, 0)
 
 
-def dispatch(plan, critic_hidden, target_hidden, critic_small, target_small, rows_args, policy):
-    rows = rows_args[0].shape[0]
+def dispatch(plan, critic_hidden, target_hidden, critic_small, target_small, heads, rows_args, policy):
+    rows = rows_args[0].shape[1]
     pairs = plan.pairs(rows)
     columns = critic_small[0].shape[1]
     _width, mine, per = chunks_of(columns)
@@ -444,7 +455,7 @@
             jax.ShapeDtypeStruct((plan.n, pairs, LANES), BF16),
             jax.ShapeDtypeStruct((per, 32, LANES), F32),
         ),
-        in_specs=[vmem, vmem, (vmem,) * 3, (vmem,) * 3] + [vmem] * 8,
+        in_specs=[vmem, vmem, (vmem,) * 2, (vmem,) * 2] + [vmem] * 8,
         out_specs=(anywhere,) * 4,
         scratch_shapes=[
             pltpu.VMEM((2,) + critic_hidden.shape, BF16),
@@ -461,7 +472,7 @@
         ],
         compiler_params=pltpu.CompilerParams(collective_id=0, has_side_effects=True, vmem_limit_bytes=VMEM_LIMIT),
         name="dispatch",
-    )(critic_hidden, target_hidden, critic_small, target_small, *rows_args, *policy)
+    )(critic_hidden, target_hidden, critic_small, target_small, heads, *rows_args, *policy)
 
 
 def norm_parts(pre):
@@ -772,6 +783,7 @@
 
 
 LAG = 2
+AHEAD = 3
 
 
 def shampoo_kernel(
@@ -853,23 +865,19 @@
     def total_hop(s):
         return to_device(sums_ref, totals.at[me], send_t.at[s], recv_t.at[me], plan.device(s))
 
-    @pl.when(me < workers)
-    def _():
-        def start(step, _):
-            def one(i, _):
-                s, copy = first_hop(step, i)
-
-                @pl.when(s < n)
-                def _():
-                    copy.start()
-
-                return 0
-
-            lax.fori_loop(0, groups - 1, one, 0)
+    def start_first(step):
+        def one(i, _):
+            s, copy = first_hop(step, i)
+
+            @pl.when(s < n)
+            def _():
+                copy.start()
+
             return 0
 
-        lax.fori_loop(0, turns, start, 0)
-
+        lax.fori_loop(0, groups - 1, one, 0)
+
+    def start_rest():
         def start_small(q, _):
             s, copy = small_hop(q)
 
@@ -892,6 +900,11 @@
             return 0
 
         lax.fori_loop(1, n, start_total, 0)
+
+    @pl.when(me < workers)
+    def _():
+        for step in range(AHEAD):
+            start_first(step)
 
     def add_up(step):
         turn = turn_of(step)
@@ -938,8 +951,7 @@
     def place(c, i, j):
         return (c, slice(i * BLK, (i + 1) * BLK), slice(j * width, (j + 1) * width))
 
-    def blocked(i):
-        c = (index // groups + 2 * CRIT - i) % CRIT
+    def blocked(c):
         pltpu.make_async_copy(pieces.at[0], given.at[c], recv_two.at[c]).wait()
         sums = []
         for i, j in subs:
@@ -1002,15 +1014,25 @@
     def round_(i, _):
         @pl.when(jnp.logical_and(me < workers, i < turns))
         def _():
+            @pl.when(i + AHEAD < turns)
+            def _():
+                start_first(i + AHEAD)
+
+            @pl.when(i == LAG)
+            def _():
+                start_rest()
+
             add_up(i)
 
-        @pl.when(jnp.logical_and(i >= LAG, i < CRIT + LAG))
+        c = (index // groups + 2 * turns + LAG - i) % turns
+
+        @pl.when(jnp.logical_and(i >= LAG, c < CRIT))
         def _():
-            blocked(i - LAG)
-
-        return 0
-
-    lax.fori_loop(0, max(turns, CRIT + LAG), round_, 0)
+            blocked(c)
+
+        return 0
+
+    lax.fori_loop(0, turns + LAG, round_, 0)
 
     def arrived_small(i, _):
         pltpu.make_async_copy(small_ref.at[0], shares.at[i // mine, i % mine], recv_s.at[i // mine, i % mine]).wait()
@@ -1158,16 +1180,18 @@
     role = jnp.stack([critic, group, (me < plan.workers).astype(I32)])
     rows, columns = state_action.shape[0], critic_in.shape[1]
     width = chunks_of(columns)[0]
-    facts = jnp.stack([reward, done_flags.astype(F32), noise_index.astype(F32)])
-    facts = jnp.pad(facts, ((0, 5), (0, 0)))
+    facts = jnp.concatenate(
+        [reward[None], jnp.stack([done_flags, noise_index, subsets[:, 0], subsets[:, 1]]).astype(F32), jnp.zeros((3, rows), F32)], 0
+    )
     w_target, w_critic, x, params = dispatch(
         plan,
         critic_hidden,
         target_hidden,
-        (critic_in, critic_norms, critic_head[None]),
-        (target_in, target_norms, target_head[None]),
-        (state_action, next_state, facts, subsets),
-        (noise_table, policy_in, policy_mid, policy_out),
+        (critic_in, critic_norms),
+        (target_in, target_norms),
+        jnp.stack([target_head, critic_head]),
+        (state_action.T, next_state.T, facts),
+        (noise_table.T, policy_in, policy_mid, policy_out.T),
     )
     xc, q, info = target_values(plan, rows, width, role, x, w_target, params)
     q_all = share_values(plan, q)

time: 435 us -> 286 us (0.66); the launches traced: 434 us -> 281 us
  Pallas kernels: 408 us -> 262 us
  local copies, waits for them, and re-layouts: 19.2 us -> 11.5 us
    pallas_call x1, Pallas kernels: 230 us -> 96.8 us  [shampoo(): pl.pallas_call(functools.partial(shampoo_kernel, plan), out_shape=(shape,...]
    pallas_call x1, Pallas kernels: 30.9 us -> 22 us  [share_values(): pl.pallas_call(functools.partial(share_kernel, plan), out_shape=jax.Shape...]
    unnamed x33 -> x28, local copies, waits for them, and re-layouts: 14.8 us -> 7.25 us
where the time goes in v2:
time: 286 us; the launch traced here: 281 us
  Pallas kernels  262 us (92%)
  local copies, waits for them, and re-layouts  11.5 us (4%)
  other arithmetic  6.64 us (2%)
    pallas_call x1, Pallas kernels, shampoo(): pl.pallas_call(functools.partial(shampoo_kernel, plan), out_shape=(shape,...  96.8 us
    pallas_call x1, Pallas kernels, dispatch(): pl.pallas_call(functools.partial(dispatch_kernel, plan), out_shape=(jax.S...  71.1 us
    pallas_call x1, Pallas kernels, critic_step(): pl.pallas_call(functools.partial(critic_kernel, plan, width), out_shape=(...  49.4 us
    pallas_call x1, Pallas kernels, target_values(): pl.pallas_call(functools.partial(target_kernel, plan, width), out_shape=(...  22.3 us
    pallas_call x1, Pallas kernels, share_values(): pl.pallas_call(functools.partial(share_kernel, plan), out_shape=jax.Shape...  22 us
    unnamed x28, local copies, waits for them, and re-layouts  7.25 us

profile of v2, /device:TPU:9, one launch (start us, length us, event | category | flops | bytes accessed | tf_op | source)
XLA Modules:
  0.0 280.6 jit_solution(1200999679019659045)
XLA Ops:
  0.8 0.6 pad_add_fusion.role_ref
  1.4 0.1 pad.2.clone
  1.4 0.7 stack.38
  2.1 0.7 stack.39
  2.8 0.6 pad_maximum_fusion.head_ref
  3.4 0.8 slice_bitcast_fusion.1
  4.1 0.7 add_convert_fusion
  4.9 1.4 maximum_maximum_fusion.rows_ref
  6.2 71.1 %dispatch.1 = (bf16[1024,1024]{1,0:T(8,128)(2,1)}, bf16[1024,1024]{1,0:T(8,128)(2,1)}, bf16[32,96,128]{2,1,0:T(8,128)(2,1)}, f32[16,32,128]{2,1,0:T(8,128)}) custom-call(f32[10,64,512]{2,1,0:T(8,128)} %w_ref.1, f32[10,64,512]{2,1,0:T(8,128)} %targ_ref.1, f32[23,320]{1,0:T(8,128)} %crit_small_0_.1, f32[4,320]{1,0:T(4,128)} %crit_small_1_.1, ...), custom_call_target="tpu_custom_call" | custom-call | tf_op jit(solution)/shard_map/dispatch/pallas_call | solution.py:450
  77.4 22.3 %target_values.1 = (bf16[5632,128]{1,0:T(8,128)(2,1)}, f32[44,128]{1,0:T(8,128)}, s32[2]{0:T(128)}) custom-call(s32[3]{0:T(128)} %pad_add_fusion.role_ref, bf16[32,96,128]{2,1,0:T(8,128)(2,1)} %get-tuple-element.31.x_ref, bf16[1024,1024]{1,0:T(8,128)(2,1)} %get-tuple-element.32.w_ref, f32[16,32,128]{2,1,0:T(8,128)} %get-tuple-element.33.p_ref), custom_call_target="tpu_custom_call" | custom-call | tf_op jit(solution)/shard_map/target_values/pallas_call | solution.py:596
  99.7 22.0 %share_values.1.q_ref = f32[10,44,128]{2,1,0:T(8,128)} custom-call(f32[44,128]{1,0:T(8,128)} %get-tuple-element.36.q_ref), custom_call_target="tpu_custom_call" | custom-call | tf_op jit(solution)/shard_map/share_values/pallas_call | solution.py:671
  121.7 49.4 %critic_step.1 = (f32[1024,1024]{1,0:T(8,128)}, f32[16,32,128]{2,1,0:T(8,128)}, f32[8,128]{1,0:T(8,128)}) custom-call(s32[2]{0:T(128)} %get-tuple-element.34.info_ref, bf16[5632,128]{1,0:T(8,128)(2,1)} %get-tuple-element.35.xc_ref, f32[10,44,128]{2,1,0:T(8,128)} %share_values.1.q_ref, bf16[1024,1024]{1,0:T(8,128)(2,1)} %get-tuple-element.37.w_ref, ...), custom_call_target="tpu_custom_call" | custom-call | tf_op jit(solution)/shard_map/critic_step/pallas_call | solution.py:757
  171.0 0.0 copy-start.6
  171.1 0.0 copy-start.8
  171.1 0.0 copy-start.9
  171.1 0.0 copy-start.3
  171.1 0.0 copy-start.4
  171.1 0.0 copy-start.5
  171.1 96.8 %shampoo.1 = (f32[10,64,512]{2,1,0:T(8,128)}, f32[10,64,512]{2,1,0:T(8,128)}, f32[10,64,512]{2,1,0:T(8,128)}, f32[10,64,512]{2,1,0:T(8,128)}, f32[32,384]{1,0:T(8,128)}, /*index=5*/f32[8,128]{1,0:T(8,128)}) custom-call(f32[1024,1024]{1,0:T(8,128)} %get-tuple-element.38.g_ref, f32[16,32,128]{2,1,0:T(8,128)} %get-tuple-element.39.small_ref, ...), custom_call_target="tpu_custom_call" | custom-call | tf_op jit(solution)/shard_map/shampoo/pallas_call | solution.py:1113
  267.9 1.3 fusion.6
  269.2 0.7 slice_reduce_fusion
  269.9 0.0 copy-done.7
  269.9 0.0 copy-done.10
  269.9 0.6 multiply_subtract_fusion.2
  270.6 1.4 multiply_subtract_fusion.1
  271.9 1.4 multiply_subtract_fusion
  273.4 2.6 copy.46
  275.9 1.1 copy.47
  277.0 0.7 copy-done.1
  277.7 1.1 copy.48
  278.8 0.7 copy-done
  279.5 1.1 copy.49
  (15 shorter events, 0.0 us)
Async XLA Ops:
  171.0 98.9 %copy-start.7 = (f32[320]{0:T(512)S(1)}, f32[320]{0:T(512)}, u32[]{:S(2)}) copy-start(f32[320]{0:T(512)} %param.43) | copy-start | bytes 3844
  171.0 98.9 %copy-start.10 = (f32[320]{0:T(512)S(1)}, f32[320]{0:T(512)}, u32[]{:S(2)}) copy-start(f32[320]{0:T(512)} %param.45) | copy-start | bytes 3844
  171.0 98.9 %copy-start.11 = (f32[320]{0:T(512)S(1)}, f32[320]{0:T(512)}, u32[]{:S(2)}) copy-start(f32[320]{0:T(512)} %param.44) | copy-start | bytes 3844
  171.0 99.5 %copy-start.6 = (f32[4,320]{1,0:T(4,128)S(1)}, f32[4,320]{1,0:T(4,128)}, u32[]{:S(2)}) copy-start(f32[4,320]{1,0:T(4,128)} %crit_small_1_.1) | copy-start | bytes 15364
  171.1 99.5 %copy-start.8 = (f32[4,320]{1,0:T(4,128)S(1)}, f32[4,320]{1,0:T(4,128)}, u32[]{:S(2)}) copy-start(f32[4,320]{1,0:T(4,128)} %param.42) | copy-start | bytes 15364
  171.1 99.5 %copy-start.9 = (f32[4,320]{1,0:T(4,128)S(1)}, f32[4,320]{1,0:T(4,128)}, u32[]{:S(2)}) copy-start(f32[4,320]{1,0:T(4,128)} %param.41) | copy-start | bytes 15364
  171.1 100.8 %copy-start.3 = (f32[23,320]{1,0:T(8,128)S(1)}, f32[23,320]{1,0:T(8,128)}, u32[]{:S(2)}) copy-start(f32[23,320]{1,0:T(8,128)} %crit_small_0_.1) | copy-start | bytes 88324
  171.1 100.8 %copy-start.4 = (f32[23,320]{1,0:T(8,128)S(1)}, f32[23,320]{1,0:T(8,128)}, u32[]{:S(2)}) copy-start(f32[23,320]{1,0:T(8,128)} %param.39) | copy-start | bytes 88324
  171.1 100.8 %copy-start.5 = (f32[23,320]{1,0:T(8,128)S(1)}, f32[23,320]{1,0:T(8,128)}, u32[]{:S(2)}) copy-start(f32[23,320]{1,0:T(8,128)} %param.38) | copy-start | bytes 88324
  273.4 2.6 copy-start.2
  275.9 1.8 copy-start.1
  277.7 1.8 copy-start

commit v3 on v2

--- a/solution.py
+++ b/solution.py
@@ -110,6 +110,22 @@
 
     def device(self, s):
         return s // self.n_mp, s % self.n_mp
+
+    @property
+    def sets(self):
+        return 4 if self.n == 32 else CRIT // 2
+
+    def extra(self, q, group):
+        if self.n != 32:
+            return jnp.int32(-1)
+        low = jnp.where(group < 2, q == 0, q == 1)
+        high = jnp.where(group < 2, q == 3, q == 2)
+        return jnp.where(low, 8, jnp.where(high, 9, -1))
+
+    def shift(self, k):
+        at = lambda c, r: sum(int(v) * m for v, m in zip(self.place(jnp.int32(c * self.groups + r)), (self.n_mp, 1)))
+        with jax.ensure_compile_time_eval():
+            return [(at(c, r), at(c, (r + k) % self.groups)) for c in range(CRIT) for r in range(self.groups)]
 
     def pairs(self, rows):
         per = -(-rows // self.groups)
@@ -179,10 +195,13 @@
     send_w,
     recv_w,
     pass_w,
+    recv_c,
     send_x,
     recv_x,
+    pass_x,
     send_p,
     recv_p,
+    pass_p,
 ):
     dp, mp = lax.axis_index("dp"), lax.axis_index("mp")
     me = plan.rank(dp, mp)
@@ -193,7 +212,6 @@
     rows = sa_ref.shape[1]
     columns = crit_small[0].shape[1]
     width, mine, per = chunks_of(columns)
-    nets = (wt_ref, wc_ref)
 
     def to_low(c, _):
         low[0, c] = targ_ref[c].astype(BF16)
@@ -203,27 +221,31 @@
     lax.fori_loop(0, CRIT, to_low, 0)
     all_barrier(plan, dp, mp)
 
-    def w_slot(t, s):
+    def w_slot(s):
         sdp, smp = plan.device(s)
-        return nets[t].at[pl.ds(pl.multiple_of(smp * rw, rw), rw), pl.ds(pl.multiple_of(sdp * cw, cw), cw)]
+        return wt_ref.at[pl.ds(pl.multiple_of(smp * rw, rw), rw), pl.ds(pl.multiple_of(sdp * cw, cw), cw)]
 
     def to_worker(src, dst, send, recv, k):
         return pltpu.make_async_remote_copy(
             src_ref=src, dst_ref=dst, send_sem=send, recv_sem=recv, device_id=plan.place(k), device_id_type=MESH
         )
 
+    turn = index // groups
+
     def first_hop(t, c):
         k = c * groups + index % groups
-        return k, to_worker(low.at[t, c], w_slot(t, index), send_w.at[t, c], recv_w.at[t, index], k)
+        dst = w_slot(index) if t == 0 else wc_ref.at[turn]
+        recv = recv_w.at[index] if t == 0 else recv_c.at[turn]
+        return k, dst, recv, to_worker(low.at[t, c], dst, send_w.at[t, c], recv, k)
 
     def send_weights(t):
         def one(i, _):
             c = (critic + i) % CRIT
-            k, copy = first_hop(t, c)
+            k, dst, recv, copy = first_hop(t, c)
 
             @pl.when(k == me)
             def _():
-                pltpu.make_async_copy(low.at[t, c], w_slot(t, index), recv_w.at[t, index]).start()
+                pltpu.make_async_copy(low.at[t, c], dst, recv).start()
 
             @pl.when(k != me)
             def _():
@@ -234,7 +256,6 @@
         lax.fori_loop(0, CRIT, one, 0)
 
     send_weights(0)
-    send_weights(1)
 
     wide[...] = jnp.zeros_like(wide)
     for t, parts in enumerate((targ_small, crit_small)):
@@ -247,18 +268,16 @@
         turned = [pltpu.roll(v, turn, 1) if turn else v for v, turn in zip(both, ((-offset) % LANES, (HALF - offset) % LANES))]
         chunk[j] = jnp.where(iota((32, LANES), 1) < HALF, turned[0], turned[1])
 
-    def small_hop(j, r):
+    def small_hop(j):
         g = index * mine + j
-        k = (g // per) * groups + r
-        return k, to_worker(chunk.at[j], p_ref.at[g % per], send_p.at[j, r], recv_p.at[g % per], k)
-
-    def send_small(i, _):
-        j, r = i // groups, i % groups
-        k, copy = small_hop(j, r)
+        k = (g // per) * groups + g % groups
+        return k, g % per, to_worker(chunk.at[j], p_ref.at[g % per], send_p.at[j], recv_p.at[g % per], k)
+
+    def send_small(j, _):
+        k, slot, copy = small_hop(j)
 
         @pl.when(k == me)
         def _():
-            slot = (index * mine + j) % per
             pltpu.make_async_copy(chunk.at[j], p_ref.at[slot], recv_p.at[slot]).start()
 
         @pl.when(k != me)
@@ -267,7 +286,7 @@
 
         return 0
 
-    lax.fori_loop(0, mine * groups, send_small, 0)
+    lax.fori_loop(0, mine, send_small, 0)
 
     lane = iota((rows, LANES), 1)
     place = lambda height, offset: (iota((height, LANES), 1) == iota((height, LANES), 0) + offset).astype(F32).astype(BF16)
@@ -334,109 +353,162 @@
 
     lax.fori_loop(0, groups, deal, 0)
 
-    def row_hop(k):
-        return to_worker(msg.at[k % groups], x_ref.at[index], send_x.at[k], recv_x.at[index], k)
+    def row_hop(i):
+        r = i % groups
+        k = (2 * (i // groups) + index % 2) * groups + r
+        return r, k, to_worker(msg.at[r], x_ref.at[index], send_x.at[i], recv_x.at[index], k)
+
+    hops = plan.sets * groups
 
     def send_rows(i, _):
-        k = (me + i) % workers
+        r, k, copy = row_hop((i + (critic // 2) * groups) % hops)
 
         @pl.when(k == me)
         def _():
-            pltpu.make_async_copy(msg.at[group], x_ref.at[index], recv_x.at[index]).start()
+            pltpu.make_async_copy(msg.at[r], x_ref.at[index], recv_x.at[index]).start()
 
         @pl.when(k != me)
         def _():
-            row_hop(k).start()
+            copy.start()
 
         return 0
 
-    lax.fori_loop(0, workers, send_rows, 0)
-
-    def pass_on(t, turn, i):
-        s = group + groups * turn
-        k = critic * groups + (group + 1 + i) % groups
-        return to_worker(w_slot(t, s), w_slot(t, s), pass_w.at[t, turn, i], recv_w.at[t, s], k)
-
-    def arrived_w(t, s):
-        pltpu.make_async_copy(low.at[t, 0], w_slot(t, s), recv_w.at[t, s]).wait()
+    lax.fori_loop(0, hops, send_rows, 0)
+    send_weights(1)
+
+    def peer(i):
+        return critic * groups + (group + 1 + i) % groups
+
+    def pass_weight(t, i):
+        s = group + groups * t
+        return to_worker(w_slot(s), w_slot(s), pass_w.at[t, i], recv_w.at[s], peer(i))
+
+    def pass_small(slot, i):
+        return to_worker(p_ref.at[slot], p_ref.at[slot], pass_p.at[slot // groups, i], recv_p.at[slot], peer(i))
+
+    extra = plan.extra(critic // 2, group)
+
+    def pass_rows(i, k, which):
+        s = 2 * i + critic % 2
+        return to_worker(x_ref.at[s], x_ref.at[s], pass_x.at[i, which], recv_x.at[s], k)
+
+    def other_rows(i):
+        return pass_rows(i, (critic + 1 - 2 * (critic % 2)) * groups + group, 0)
+
+    def extra_rows(i):
+        return pass_rows(i, extra * groups + group, 1)
+
+    def arrived_w(s):
+        pltpu.make_async_copy(low.at[0, 0], w_slot(s), recv_w.at[s]).wait()
+
+    def arrived_x(s):
+        pltpu.make_async_copy(msg.at[0], x_ref.at[s], recv_x.at[s]).wait()
+
+    def arrived_p(slot):
+        pltpu.make_async_copy(chunk.at[0], p_ref.at[slot], recv_p.at[slot]).wait()
 
     turns = (plan.n - group + groups - 1) // groups
+    passes_rows = critic < 2 * plan.sets
+
+    def peers(body):
+        lax.fori_loop(0, groups - 1, lambda i, _: (body(i), 0)[1], 0)
+
+    def each(count, body):
+        lax.fori_loop(0, count, lambda i, _: (body(i), 0)[1], 0)
 
     @pl.when(me < workers)
     def _():
+        def relay_weight(t):
+            arrived_w(group + groups * t)
+            peers(lambda i: pass_weight(t, i).start())
+
+        each(turns, relay_weight)
+
+        @pl.when(passes_rows)
+        def _():
+            def relay_rows(i):
+                arrived_x(2 * i + critic % 2)
+                other_rows(i).start()
+
+                @pl.when(extra >= 0)
+                def _():
+                    extra_rows(i).start()
+
+            each(plan.n // 2, relay_rows)
+
+        def relay_small(slot):
+            @pl.when((critic * per + slot) % groups == group)
+            def _():
+                arrived_p(slot)
+                peers(lambda i: pass_small(slot, i).start())
+
+        each(per, relay_small)
+
+        def arrived(s):
+            @pl.when(s % groups != group)
+            def _():
+                arrived_w(s)
+
+            @pl.when(jnp.logical_not(jnp.logical_and(passes_rows, s % 2 == critic % 2)))
+            def _():
+                arrived_x(s)
+
+        each(plan.n, arrived)
+
+        def arrived_small(slot):
+            @pl.when((critic * per + slot) % groups != group)
+            def _():
+                arrived_p(slot)
+
+        each(per, arrived_small)
+        each(turns, lambda t: pltpu.make_async_copy(low.at[1, 0], wc_ref.at[t], recv_c.at[t]).wait())
+        each(turns, lambda t: peers(lambda i: pass_weight(t, i).wait_send()))
+
+        @pl.when(passes_rows)
+        def _():
+            def passed_rows(i):
+                other_rows(i).wait_send()
+
+                @pl.when(extra >= 0)
+                def _():
+                    extra_rows(i).wait_send()
+
+            each(plan.n // 2, passed_rows)
+
+        def passed_small(slot):
+            @pl.when((critic * per + slot) % groups == group)
+            def _():
+                peers(lambda i: pass_small(slot, i).wait_send())
+
+        each(per, passed_small)
+
+    def sent_weights(c):
         for t in range(2):
-
-            def relay(turn, _):
-                arrived_w(t, group + groups * turn)
-
-                def one(i, _):
-                    pass_on(t, turn, i).start()
-                    return 0
-
-                lax.fori_loop(0, groups - 1, one, 0)
-                return 0
-
-            lax.fori_loop(0, turns, relay, 0)
-
-        def arrived(s, _):
-            @pl.when(s % groups != group)
-            def _():
-                arrived_w(0, s)
-                arrived_w(1, s)
-
-            pltpu.make_async_copy(msg.at[0], x_ref.at[s], recv_x.at[s]).wait()
-            return 0
-
-        lax.fori_loop(0, plan.n, arrived, 0)
-
-        def arrived_small(j, _):
-            pltpu.make_async_copy(chunk.at[0], p_ref.at[j], recv_p.at[j]).wait()
-            return 0
-
-        lax.fori_loop(0, per, arrived_small, 0)
-        for t in range(2):
-
-            def passed(turn, _):
-                def one(i, _):
-                    pass_on(t, turn, i).wait_send()
-                    return 0
-
-                lax.fori_loop(0, groups - 1, one, 0)
-                return 0
-
-            lax.fori_loop(0, turns, passed, 0)
-
-    def sent_weights(c, _):
-        for t in range(2):
-            k, copy = first_hop(t, c)
+            k, _dst, _recv, copy = first_hop(t, c)
 
             @pl.when(k != me)
             def _():
                 copy.wait_send()
 
-        return 0
-
-    lax.fori_loop(0, CRIT, sent_weights, 0)
-
-    def sent_small(i, _):
-        k, copy = small_hop(i // groups, i % groups)
+    each(CRIT, sent_weights)
+
+    def sent_small(j):
+        k, _slot, copy = small_hop(j)
 
         @pl.when(k != me)
         def _():
             copy.wait_send()
 
-        return 0
-
-    lax.fori_loop(0, mine * groups, sent_small, 0)
-
-    def sent_rows(k, _):
+    each(mine, sent_small)
+
+    def sent_rows(i):
+        _r, k, copy = row_hop(i)
+
         @pl.when(k != me)
         def _():
-            row_hop(k).wait_send()
-
-        return 0
-
-    lax.fori_loop(0, workers, sent_rows, 0)
+            copy.wait_send()
+
+    each(hops, sent_rows)
 
 
 def dispatch(plan, critic_hidden, target_hidden, critic_small, target_small, heads, rows_args, policy):
@@ -451,7 +523,7 @@
         functools.partial(dispatch_kernel, plan),
         out_shape=(
             jax.ShapeDtypeStruct((H, H), BF16),
-            jax.ShapeDtypeStruct((H, H), BF16),
+            jax.ShapeDtypeStruct((plan.turns,) + critic_hidden.shape[1:], BF16),
             jax.ShapeDtypeStruct((plan.n, pairs, LANES), BF16),
             jax.ShapeDtypeStruct((per, 32, LANES), F32),
         ),
@@ -463,12 +535,15 @@
             pltpu.VMEM((2, 32, -(-columns // LANES) * LANES), F32),
             pltpu.VMEM((mine, 32, LANES), F32),
             dma((2, CRIT)),
-            dma((2, plan.n)),
-            dma((2, plan.turns, plan.groups - 1)),
-            dma((plan.workers,)),
             dma((plan.n,)),
-            dma((mine, plan.groups)),
+            dma((plan.turns, plan.groups - 1)),
+            dma((plan.turns,)),
+            dma((plan.sets * plan.groups,)),
+            dma((plan.n,)),
+            dma((plan.n // 2, 2)),
+            dma((mine,)),
             dma((per,)),
+            dma((-(-per // plan.groups), plan.groups - 1)),
         ],
         compiler_params=pltpu.CompilerParams(collective_id=0, has_side_effects=True, vmem_limit_bytes=VMEM_LIMIT),
         name="dispatch",
@@ -680,11 +755,26 @@
 
 
 def critic_kernel(
-    plan, width, info_ref, xc_ref, q_ref, w_ref, p_ref, grad_ref, small_ref, sums_ref, z_one, slope, act, low, fact, par, win, picks, acc
+    plan, width, role_ref, info_ref, xc_ref, q_ref, shares, p_ref, grad_ref, small_ref, sums_ref, w_ref, z_one, slope, act, low, fact, par, win, picks, acc
 ):
     number = info_ref[0]
     scale = 2.0 / jnp.maximum(info_ref[1], 1).astype(F32)
     tiles = (number + TILE - 1) // TILE
+    rw, cw = shares[0].shape[1:]
+    for k, share in enumerate(shares):
+        owner = (role_ref[1] + plan.groups - k) % plan.groups
+
+        def gather(t, _):
+            s = owner + plan.groups * t
+
+            @pl.when(s < plan.n)
+            def _():
+                sdp, smp = plan.device(s)
+                w_ref[pl.ds(pl.multiple_of(smp * rw, rw), rw), pl.ds(pl.multiple_of(sdp * cw, cw), cw)] = share[t]
+
+            return 0
+
+        lax.fori_loop(0, plan.turns, gather, 0)
     par[...] = assemble(p_ref, width, HALF)
     win[...] = jnp.zeros_like(win)
     win[0:32, :] = low_input(par[...])
@@ -751,7 +841,7 @@
         small_ref[i] = pltpu.roll(block, LANES - offset, 1) if offset else block
 
 
-def critic_step(plan, width, info, xc, q_all, weights, params):
+def critic_step(plan, width, role, info, xc, q_all, shares, params):
     vmem = pl.BlockSpec(memory_space=pltpu.VMEM)
     smem = pl.BlockSpec(memory_space=pltpu.SMEM)
     return pl.pallas_call(
@@ -761,9 +851,10 @@
             jax.ShapeDtypeStruct((H // width, 32, LANES), F32),
             jax.ShapeDtypeStruct((8, LANES), F32),
         ),
-        in_specs=[smem] + [vmem] * 4,
+        in_specs=[smem, smem, vmem, vmem, (vmem,) * plan.groups, vmem],
         out_specs=(vmem,) * 3,
         scratch_shapes=[
+            pltpu.VMEM((H, H), BF16),
             pltpu.VMEM((TILE, H), F32),
             pltpu.VMEM((TILE, H), F32),
             pltpu.VMEM((TILE, H), BF16),
@@ -776,13 +867,13 @@
         ],
         compiler_params=pltpu.CompilerParams(vmem_limit_bytes=VMEM_LIMIT),
         name="critic_step",
-    )(info, xc, q_all, weights, params)
+    )(role, info, xc, q_all, shares, params)
 
 
 PRECISE = 2
 
 
-LAG = 2
+LAG = 3
 AHEAD = 3
 
 
@@ -928,21 +1019,43 @@
                 copy.start()
 
     width = min(256, cw)
-    many = width // BLK
+    halves = width // LANES
+    high_rows = halves * BLK
     nr, nc = rw // BLK, cw // width
     subs = [(i, j) for i in range(nr) for j in range(nc)]
-    mask = (iota((width, width), 0) // BLK == iota((width, width), 1) // BLK).astype(F32).astype(BF16)
-    eye = (iota((BLK, width), 0) == iota((BLK, width), 1) % BLK).astype(F32)
+    mask = (iota((LANES, LANES), 0) // BLK == iota((LANES, LANES), 1) // BLK).astype(F32).astype(BF16)
+    mask_wide = jnp.concatenate([mask] * halves, 1)
+    eye = (iota((high_rows, LANES), 0) % BLK == iota((high_rows, LANES), 1) % BLK).astype(F32)
     eye_low = eye.astype(BF16)
 
+    def packed(flat):
+        return jnp.concatenate([flat[:, k * LANES : (k + 1) * LANES] for k in range(halves)], 0)
+
+    def flat_of(x):
+        return jnp.concatenate([x[k * BLK : (k + 1) * BLK] for k in range(halves)], 1)
+
+    def tops(out, count):
+        return [
+            jnp.concatenate(
+                [out[(i * halves + k) * BLK : (i * halves + k + 1) * BLK, k * LANES : (k + 1) * LANES] for k in range(halves)], 0
+            )
+            for i in range(count)
+        ]
+
     def diag(x):
-        return jnp.concatenate([x] * many, 0) * mask
-
-    def precise(a, b):
-        ah, al = split2(a)
-        bh, bl = split2(b)
-        both = nn(jnp.concatenate([ah, al], 0), diag(bh))
-        return both[:BLK] + both[BLK:] + nn(ah, diag(bl))
+        return jnp.concatenate([flat_of(x)] * (LANES // BLK), 0) * mask_wide
+
+    def diag_rows(x):
+        tiled = [jnp.concatenate([x[k * BLK : (k + 1) * BLK]] * (LANES // BLK), 0) * mask for k in range(halves)]
+        return jnp.concatenate(tiled, 0)
+
+    def products(lhs, right):
+        return tops(nn(jnp.concatenate(lhs, 0), right), len(lhs))
+
+    def precise(parts, right, right_rest):
+        high, rest = parts
+        out = products([high, rest], right)
+        return out[0] + out[1] + products([high], right_rest)[0]
 
     def block_sums(s):
         high, rest = split2(s)
@@ -951,65 +1064,77 @@
     def place(c, i, j):
         return (c, slice(i * BLK, (i + 1) * BLK), slice(j * width, (j + 1) * width))
 
+    def column_sums(x):
+        return [jnp.sum(x[k * BLK : (k + 1) * BLK].reshape(BLK // 8, 8, LANES), 0) for k in range(halves)]
+
+    def over_blocks(total, spot):
+        rows = [jnp.sum(total[(spot + k) * 8 : (spot + k + 1) * 8], 0, keepdims=True) for k in range(halves)]
+        return jnp.concatenate([jnp.broadcast_to(row, (BLK, LANES)) for row in rows], 0)
+
     def blocked(c):
         pltpu.make_async_copy(pieces.at[0], given.at[c], recv_two.at[c]).wait()
-        sums = []
+        sums, stats = [], []
         for i, j in subs:
             at = place(c, i, j)
             grad = given[at]
             mo_ref[at] = MOMENTUM * mom_ref[at] + grad
-            low = grad.astype(BF16)
-            wide = diag(low)
-            left = STAT_DECAY * left_ref[at] + (1.0 - STAT_DECAY) * nt(low, wide)
-            flip = nt(eye_low, wide).astype(BF16)
-            right = STAT_DECAY * right_ref[at] + (1.0 - STAT_DECAY) * nn(flip, wide)
-            lo_ref[at] = left
-            ro_ref[at] = right
+            low = packed(grad.astype(BF16))
+            square, flip = tops(nt(jnp.concatenate([low, eye_low], 0), diag_rows(low)), 2)
+            left = STAT_DECAY * packed(left_ref[at]) + (1.0 - STAT_DECAY) * square
+            right = products([flip.astype(BF16)], diag(low))[0]
+            right = STAT_DECAY * packed(right_ref[at]) + (1.0 - STAT_DECAY) * right
+            lo_ref[at] = flat_of(left)
+            ro_ref[at] = flat_of(right)
             for stat in (left, right):
-                sums.append(jnp.sum((stat * stat).reshape(BLK // 8, 8, width), 0))
+                stats.append(stat)
+                sums += column_sums(stat * stat)
         total = block_sums(jnp.concatenate(sums, 0))
         chains = []
-        for k, (i, j) in enumerate(subs):
-            for side, ref in enumerate((lo_ref, ro_ref)):
-                spot = (2 * k + side) * 8
-                inv = lax.rsqrt(jnp.sum(total[spot : spot + 8], 0, keepdims=True))
-                rest = (eye - ref[place(c, i, j)] * inv) * 0.25
-                chains.append([rest, eye + rest, jnp.sqrt(jnp.sqrt(inv))])
+        for k, stat in enumerate(stats):
+            inv = lax.rsqrt(over_blocks(total, k * halves))
+            rest = (eye - stat * inv) * 0.25
+            chains.append([rest, eye + rest, jnp.sqrt(jnp.sqrt(inv))])
         for it in range(NEWTON - 1):
             full = it < PRECISE
-            work = []
+            squares = []
             for ch in chains:
                 high, rest = split2(ch[0])
-                wide = diag(high)
-                wide_rest = diag(rest) if full else None
                 lhs = [high] + ([rest] if full else []) + ([ch[1].astype(BF16)] if it > 0 else [])
-                out = nn(jnp.concatenate(lhs, 0), wide)
-                power = out[:BLK]
+                out = products(lhs, diag(high))
+                power = out[0]
                 if full:
-                    power = power + out[BLK : 2 * BLK] + nn(high, wide_rest)
+                    power = power + out[1] + products([high], diag(rest))[0]
                 if it > 0:
-                    ch[1] = ch[1] + out[-BLK:]
-                work.append([wide, wide_rest, power])
-            for factor in (3.75, 5.0, 2.5):
-                for ch, wk in zip(chains, work):
-                    high, rest = split2(factor * ch[0] + wk[2])
-                    if full:
-                        out = nn(jnp.concatenate([high, rest], 0), wk[0])
-                        wk[2] = out[:BLK] + out[BLK:] + nn(high, wk[1])
-                    else:
-                        wk[2] = nn(high, wk[0])
-            for ch, wk in zip(chains, work):
-                ch[0] = wk[2]
+                    ch[1] = ch[1] + out[-1]
+                squares.append(power)
+            factors = [[diag(v) for v in split2(power)[: 2 if full else 1]] for power in squares]
+
+            def times(x, right):
+                parts = split2(x)
+                return precise(parts, *right) if full else products([parts[0]], right[0])[0]
+
+            terms = [
+                5.0 * ch[0] + 3.75 * power + times(ch[0], right) for ch, power, right in zip(chains, squares, factors)
+            ]
+            for ch, power, right, term in zip(chains, squares, factors, terms):
+                ch[0] = 2.5 * power + times(term, right)
         for ch in chains:
-            ch[1] = ch[1] + nn(ch[1].astype(BF16), diag(ch[0].astype(BF16)))
+            ch[1] = ch[1] + products([ch[1].astype(BF16)], diag(ch[0].astype(BF16)))[0]
+        steps, sums = [], []
+        for k, (i, j) in enumerate(subs):
+            lc, rc = chains[2 * k], chains[2 * k + 1]
+            moment = split2(packed(mo_ref[place(c, i, j)]))
+            roots = split2(rc[1])
+            step = precise(split2(lc[1]), diag(moment[0]), diag(moment[1]))
+            step = precise(split2(step), diag(roots[0]), diag(roots[1])) * (lc[2] * rc[2])
+            steps.append(step)
+            sums += column_sums(step * step)
+        total = block_sums(jnp.concatenate(sums, 0)) * (1.0 / (BLK * BLK))
         for k, (i, j) in enumerate(subs):
             at = place(c, i, j)
-            lc, rc = chains[2 * k], chains[2 * k + 1]
-            step = precise(precise(lc[1], mo_ref[at]), rc[1]) * (lc[2] * rc[2])
-            squares = block_sums(jnp.sum((step * step).reshape(BLK // 8, 8, width), 0))
-            square = jnp.sum(squares, 0, keepdims=True) * (1.0 / (BLK * BLK))
             old = w_ref[at]
-            wo_ref[at] = old - RATE_HIDDEN * (step * lax.rsqrt(square + 1e-06) + WEIGHT_DECAY * old)
+            step = flat_of(steps[k] * lax.rsqrt(over_blocks(total, k * halves) + 1e-06))
+            wo_ref[at] = old - RATE_HIDDEN * (step + WEIGHT_DECAY * old)
 
     def round_(i, _):
         @pl.when(jnp.logical_and(me < workers, i < turns))
@@ -1183,7 +1308,7 @@
     facts = jnp.concatenate(
         [reward[None], jnp.stack([done_flags, noise_index, subsets[:, 0], subsets[:, 1]]).astype(F32), jnp.zeros((3, rows), F32)], 0
     )
-    w_target, w_critic, x, params = dispatch(
+    w_target, share, x, params = dispatch(
         plan,
         critic_hidden,
         target_hidden,
@@ -1193,9 +1318,10 @@
         (state_action.T, next_state.T, facts),
         (noise_table.T, policy_in, policy_mid, policy_out.T),
     )
+    shares = (share,) + tuple(lax.ppermute(share, ("dp", "mp"), plan.shift(k)) for k in range(1, plan.groups))
     xc, q, info = target_values(plan, rows, width, role, x, w_target, params)
     q_all = share_values(plan, q)
-    grad_hidden, grad_small, sums = critic_step(plan, width, info, xc, q_all, w_critic, params)
+    grad_hidden, grad_small, sums = critic_step(plan, width, role, info, xc, q_all, shares, params)
     hidden_momentum, left_renewed, right_renewed, hidden_updated, own, totals = shampoo(
         plan, columns, grad_hidden, grad_small, sums, hidden_moment, left_stats, right_stats, critic_hidden
     )

time: 286 us -> 257 us (0.90); the launches traced: 281 us -> 255 us
  Pallas kernels: 262 us -> 229 us
  starting transfers between devices: 0 us -> 5.56 us
    pallas_call x1, Pallas kernels: 96.8 us -> 83.5 us  [shampoo(): pl.pallas_call(functools.partial(shampoo_kernel, plan), out_shape=(shape,...]
    pallas_call x1, Pallas kernels: 22 us -> 10.8 us  [share_values(): pl.pallas_call(functools.partial(share_kernel, plan), out_shape=jax.Shape...]
    pallas_call x1, Pallas kernels: 71.1 us -> 62.3 us  [dispatch(): pl.pallas_call(functools.partial(dispatch_kernel, plan), out_shape=(jax.S...]
    ppermute x0 -> x2, starting transfers between devices: none -> 5.56 us  [local(): lax.ppermute(share, ('dp', 'mp'), plan.shift(k))]
    unnamed x28 -> x32, local copies, waits for them, and re-layouts: 7.25 us -> 8.33 us
  transfers between devices with their start and end apart: 0 -> 2, of which waited for: 0 -> 0; matrix products, arithmetic and copies ran while one was open for 0% -> 0% of each run, Pallas kernels for 0% -> 13%
where the time goes in v3:
time: 257 us; the launch traced here: 255 us
  Pallas kernels  229 us (89%)
  local copies, waits for them, and re-layouts  12.5 us (5%)
  other arithmetic  6.64 us (3%)
  starting transfers between devices  5.56 us (2%)
    pallas_call x1, Pallas kernels, shampoo(): pl.pallas_call(functools.partial(shampoo_kernel, plan), out_shape=(shape,...  83.5 us
    pallas_call x1, Pallas kernels, dispatch(): pl.pallas_call(functools.partial(dispatch_kernel, plan), out_shape=(jax.S...  62.3 us
    pallas_call x1, Pallas kernels, critic_step(): pl.pallas_call(functools.partial(critic_kernel, plan, width), out_shape=(...  50 us
    pallas_call x1, Pallas kernels, target_values(): pl.pallas_call(functools.partial(target_kernel, plan, width), out_shape=(...  22.3 us
    pallas_call x1, Pallas kernels, share_values(): pl.pallas_call(functools.partial(share_kernel, plan), out_shape=jax.Shape...  10.8 us
    unnamed x32, local copies, waits for them, and re-layouts  8.33 us
    ppermute x2, starting transfers between devices, local(): lax.ppermute(share, ('dp', 'mp'), plan.shift(k))  5.56 us
  transfers between devices with their start and end apart: 2, of which 0 were waited for; matrix products, arithmetic and copies ran while one was open for 0% of the time, Pallas kernels for 13%

profile of v3, /device:TPU:9, one launch (start us, length us, event | category | flops | bytes accessed | tf_op | source)
XLA Modules:
  0.0 254.5 jit_solution(7277833077070445411)
XLA Ops:
  0.6 0.7 stack.38
  1.3 0.7 stack.39
  2.0 0.8 slice_bitcast_fusion.1
  2.8 0.1 pad.2.clone
  2.9 0.6 pad_maximum_fusion.head_ref
  3.4 0.7 add_convert_fusion
  4.2 1.4 maximum_maximum_fusion.rows_ref
  5.5 62.3 %dispatch.1 = (bf16[1024,1024]{1,0:T(8,128)(2,1)}, bf16[11,64,512]{2,1,0:T(8,128)(2,1)}, bf16[32,96,128]{2,1,0:T(8,128)(2,1)}, f32[16,32,128]{2,1,0:T(8,128)}) custom-call(f32[10,64,512]{2,1,0:T(8,128)} %w_ref.1, f32[10,64,512]{2,1,0:T(8,128)} %targ_ref.1, f32[23,320]{1,0:T(8,128)} %crit_small_0_.1, f32[4,320]{1,0:T(4,128)} %crit_small_1_.1, ...), custom_call_target="tpu_custom_call" | custom-call | tf_op jit(solution)/shard_map/dispatch/pallas_call | solution.py:522
  67.8 2.3 collective-permute-start.1
  70.1 3.3 %collective-permute-start = (bf16[11,64,512]{2,1,0:T(8,128)(2,1)}, bf16[11,64,512]{2,1,0:T(8,128)(2,1)S(1)}, u32[]{:S(2)}, u32[]{:S(2)}) collective-permute-start(bf16[11,64,512]{2,1,0:T(8,128)(2,1)} %get-tuple-element.37.shares_0_), channel_id=1, source_target_pairs={{0,1},{1,2},{2,0},{3,18},{18,19},{19,3},{4,5},{5,6},{6,4},{7,22},{... | collective-permute-start | bytes 2162696 | tf_op jit(solution)/shard_map/ppermute | solution.py:1321
  73.5 0.6 pad_add_fusion.role_ref
  74.1 22.3 %target_values.1 = (bf16[5632,128]{1,0:T(8,128)(2,1)}, f32[44,128]{1,0:T(8,128)}, s32[2]{0:T(128)}) custom-call(s32[3]{0:T(128)} %pad_add_fusion.role_ref, bf16[32,96,128]{2,1,0:T(8,128)(2,1)} %get-tuple-element.31.x_ref, bf16[1024,1024]{1,0:T(8,128)(2,1)} %get-tuple-element.32.w_ref, f32[16,32,128]{2,1,0:T(8,128)} %get-tuple-element.33.p_ref), custom_call_target="tpu_custom_call" | custom-call | tf_op jit(solution)/shard_map/target_values/pallas_call | solution.py:671
  96.4 10.8 %share_values.1.q_ref = f32[10,44,128]{2,1,0:T(8,128)} custom-call(f32[44,128]{1,0:T(8,128)} %get-tuple-element.36.q_ref), custom_call_target="tpu_custom_call" | custom-call | tf_op jit(solution)/shard_map/share_values/pallas_call | solution.py:746
  107.2 0.0 copy-start.3
  107.2 0.8 copy-done.3
  108.1 0.2 copy-done.4
  108.3 50.0 %critic_step.1 = (f32[1024,1024]{1,0:T(8,128)}, f32[16,32,128]{2,1,0:T(8,128)}, f32[8,128]{1,0:T(8,128)}) custom-call(s32[3]{0:T(128)} %pad_add_fusion.role_ref, s32[2]{0:T(128)} %get-tuple-element.34.info_ref, bf16[5632,128]{1,0:T(8,128)(2,1)} %get-tuple-element.35.xc_ref, f32[10,44,128]{2,1,0:T(8,128)} %share_values.1.q_ref, ...), custom_call_target="tpu_custom_call" | custom-call | tf_op jit(solution)/shard_map/critic_step/pallas_call | solution.py:847
  158.3 0.0 copy-start.5
  158.3 0.0 copy-start.6
  158.4 0.0 copy-start.12
  158.4 83.5 %shampoo.1 = (f32[10,64,512]{2,1,0:T(8,128)}, f32[10,64,512]{2,1,0:T(8,128)}, f32[10,64,512]{2,1,0:T(8,128)}, f32[10,64,512]{2,1,0:T(8,128)}, f32[32,384]{1,0:T(8,128)}, /*index=5*/f32[8,128]{1,0:T(8,128)}) custom-call(f32[1024,1024]{1,0:T(8,128)} %get-tuple-element.38.g_ref, f32[16,32,128]{2,1,0:T(8,128)} %get-tuple-element.39.small_ref, ...), custom_call_target="tpu_custom_call" | custom-call | tf_op jit(solution)/shard_map/shampoo/pallas_call | solution.py:1238
  241.9 1.3 fusion.6
  243.2 0.7 slice_reduce_fusion
  243.9 1.4 multiply_subtract_fusion.1
  245.3 1.4 multiply_subtract_fusion
  246.7 0.6 multiply_subtract_fusion.2
  247.3 2.6 %copy.46 = f32[10,64,512]{2,1,0:T(8,128)} copy(f32[10,64,512]{2,1,0:T(8,128)} %get-tuple-element.86) | data formatting | bytes 2621440
  249.9 1.1 copy.47
  251.0 0.7 copy-done.1
  251.7 1.1 copy.48
  252.8 0.7 copy-done
  253.5 1.1 copy.49
  (23 shorter events, 0.1 us)
Async XLA Ops:
  67.8 39.4 %collective-permute-start.1 = (bf16[11,64,512]{2,1,0:T(8,128)(2,1)}, bf16[11,64,512]{2,1,0:T(8,128)(2,1)S(1)}, u32[]{:S(2)}, u32[]{:S(2)}) collective-permute-start(bf16[11,64,512]{2,1,0:T(8,128)(2,1)} %get-tuple-element.37.shares_0_), channel_id=1, source_target_pairs={{0,2},{1,0},{2,1},{3,19},{18,3},{19,18},{4,6},{5,4},{6,5},{7,23},{... | collective-permute-start | bytes 2162696 | tf_op jit(solution)/shard_map/ppermute | solution.py:1321
  70.1 37.1 %collective-permute-start = (bf16[11,64,512]{2,1,0:T(8,128)(2,1)}, bf16[11,64,512]{2,1,0:T(8,128)(2,1)S(1)}, u32[]{:S(2)}, u32[]{:S(2)}) collective-permute-start(bf16[11,64,512]{2,1,0:T(8,128)(2,1)} %get-tuple-element.37.shares_0_), channel_id=1, source_target_pairs={{0,1},{1,2},{2,0},{3,18},{18,19},{19,3},{4,5},{5,6},{6,4},{7,22},{... | collective-permute-start | bytes 2162696 | tf_op jit(solution)/shard_map/ppermute | solution.py:1321
  107.2 0.9 copy-start.3
  107.2 1.1 copy-start.4
  158.3 85.6 %copy-start.8 = (f32[4,320]{1,0:T(4,128)S(1)}, f32[4,320]{1,0:T(4,128)}, u32[]{:S(2)}) copy-start(f32[4,320]{1,0:T(4,128)} %crit_small_1_.1) | copy-start | bytes 15364
  158.3 85.6 %copy-start.10 = (f32[4,320]{1,0:T(4,128)S(1)}, f32[4,320]{1,0:T(4,128)}, u32[]{:S(2)}) copy-start(f32[4,320]{1,0:T(4,128)} %param.42) | copy-start | bytes 15364
  158.3 85.6 %copy-start.11 = (f32[4,320]{1,0:T(4,128)S(1)}, f32[4,320]{1,0:T(4,128)}, u32[]{:S(2)}) copy-start(f32[4,320]{1,0:T(4,128)} %param.41) | copy-start | bytes 15364
  158.3 86.9 %copy-start.5 = (f32[23,320]{1,0:T(8,128)S(1)}, f32[23,320]{1,0:T(8,128)}, u32[]{:S(2)}) copy-start(f32[23,320]{1,0:T(8,128)} %crit_small_0_.1) | copy-start | bytes 88324
  158.3 86.9 %copy-start.6 = (f32[23,320]{1,0:T(8,128)S(1)}, f32[23,320]{1,0:T(8,128)}, u32[]{:S(2)}) copy-start(f32[23,320]{1,0:T(8,128)} %param.39) | copy-start | bytes 88324
  158.4 86.9 %copy-start.7 = (f32[23,320]{1,0:T(8,128)S(1)}, f32[23,320]{1,0:T(8,128)}, u32[]{:S(2)}) copy-start(f32[23,320]{1,0:T(8,128)} %param.38) | copy-start | bytes 88324
  158.4 88.3 %copy-start.9 = (f32[320]{0:T(512)S(1)}, f32[320]{0:T(512)}, u32[]{:S(2)}) copy-start(f32[320]{0:T(512)} %param.43) | copy-start | bytes 3844
  158.4 88.3 %copy-start.12 = (f32[320]{0:T(512)S(1)}, f32[320]{0:T(512)}, u32[]{:S(2)}) copy-start(f32[320]{0:T(512)} %param.45) | copy-start | bytes 3844
  158.4 88.3 %copy-start.13 = (f32[320]{0:T(512)S(1)}, f32[320]{0:T(512)}, u32[]{:S(2)}) copy-start(f32[320]{0:T(512)} %param.44) | copy-start | bytes 3844
  247.3 2.6 %copy-start.2 = (f32[10,64,512]{2,1,0:T(8,128)S(1)}, f32[10,64,512]{2,1,0:T(8,128)}, u32[]{:S(2)}) copy-start(f32[10,64,512]{2,1,0:T(8,128)} %get-tuple-element.87) | copy-start | bytes 3932164
  249.9 1.8 copy-start.1
  251.7 1.8 copy-start

commit v4 on v3

--- a/solution.py
+++ b/solution.py
@@ -33,6 +33,7 @@
 LANES = 128
 HALF = 64
 TILE = 256
+AHEAD_TILES = 4
 L_TGT = 23
 L_BASE = 46
 L_BOOT = 49
@@ -40,7 +41,7 @@
 L_S1 = 51
 L_VALID = 52
 L_CNT = 53
-VMEM_LIMIT = 60 * 1024 * 1024
+MIB = 1024 * 1024
 
 
 def nn(a, b):
@@ -132,7 +133,7 @@
         return -(-per // 32) * 16
 
     def cap(self, rows):
-        return -(-(self.n * -(-rows // self.groups)) // TILE) * TILE
+        return -(-(self.n * -(-rows // self.groups)) // (TILE * AHEAD_TILES)) * TILE * AHEAD_TILES
 
 
 def chunks_of(columns):
@@ -172,18 +173,7 @@
 
 def dispatch_kernel(
     plan,
-    crit_ref,
-    targ_ref,
-    crit_small,
-    targ_small,
-    head_ref,
-    sa_ref,
-    ns_ref,
-    rows_ref,
-    table_ref,
-    pin_ref,
-    pmid_ref,
-    pout_ref,
+    inputs,
     wt_ref,
     wc_ref,
     x_ref,
@@ -202,7 +192,15 @@
     send_p,
     recv_p,
     pass_p,
+    stage,
+    stage_sem,
 ):
+    loads = [pltpu.make_async_copy(src, dst, stage_sem.at[k]) for k, (src, dst) in enumerate(zip(inputs, stage))]
+    for load in loads:
+        load.start()
+    crit_ref, targ_ref, crit_in, crit_norms, targ_in, targ_norms, head_ref = stage[:7]
+    sa_ref, ns_ref, rows_ref, table_ref, pin_ref, pmid_ref, pout_ref = stage[7:]
+    crit_small, targ_small = (crit_in, crit_norms), (targ_in, targ_norms)
     dp, mp = lax.axis_index("dp"), lax.axis_index("mp")
     me = plan.rank(dp, mp)
     index = dp * plan.n_mp + mp
@@ -213,6 +211,9 @@
     columns = crit_small[0].shape[1]
     width, mine, per = chunks_of(columns)
 
+    for load in loads[:2]:
+        load.wait()
+
     def to_low(c, _):
         low[0, c] = targ_ref[c].astype(BF16)
         low[1, c] = crit_ref[c].astype(BF16)
@@ -257,6 +258,8 @@
 
     send_weights(0)
 
+    for load in loads[2:]:
+        load.wait()
     wide[...] = jnp.zeros_like(wide)
     for t, parts in enumerate((targ_small, crit_small)):
         wide[t, 0:IN, 0:columns] = parts[0][...]
@@ -511,12 +514,12 @@
     each(hops, sent_rows)
 
 
-def dispatch(plan, critic_hidden, target_hidden, critic_small, target_small, heads, rows_args, policy):
-    rows = rows_args[0].shape[1]
+def dispatch(plan, inputs):
+    critic_hidden, critic_in, state_action = inputs[0], inputs[2], inputs[7]
+    rows = state_action.shape[1]
     pairs = plan.pairs(rows)
-    columns = critic_small[0].shape[1]
+    columns = critic_in.shape[1]
     _width, mine, per = chunks_of(columns)
-    vmem = pl.BlockSpec(memory_space=pltpu.VMEM)
     anywhere = pl.BlockSpec(memory_space=pl.ANY)
     dma = pltpu.SemaphoreType.DMA
     return pl.pallas_call(
@@ -527,7 +530,7 @@
             jax.ShapeDtypeStruct((plan.n, pairs, LANES), BF16),
             jax.ShapeDtypeStruct((per, 32, LANES), F32),
         ),
-        in_specs=[vmem, vmem, (vmem,) * 2, (vmem,) * 2] + [vmem] * 8,
+        in_specs=[(pl.BlockSpec(memory_space=pltpu.HBM),) * len(inputs)],
         out_specs=(anywhere,) * 4,
         scratch_shapes=[
             pltpu.VMEM((2,) + critic_hidden.shape, BF16),
@@ -544,10 +547,12 @@
             dma((mine,)),
             dma((per,)),
             dma((-(-per // plan.groups), plan.groups - 1)),
+            tuple(pltpu.VMEM(v.shape, v.dtype) for v in inputs),
+            dma((len(inputs),)),
         ],
-        compiler_params=pltpu.CompilerParams(collective_id=0, has_side_effects=True, vmem_limit_bytes=VMEM_LIMIT),
+        compiler_params=pltpu.CompilerParams(collective_id=0, has_side_effects=True, vmem_limit_bytes=20 * MIB),
         name="dispatch",
-    )(critic_hidden, target_hidden, critic_small, target_small, heads, *rows_args, *policy)
+    )(inputs)
 
 
 def norm_parts(pre):
@@ -564,6 +569,25 @@
 
 def low_input(params):
     return jnp.where(iota((32, H), 0) < IN, params, 0.0).astype(BF16)
+
+
+def input_layer(params, win_ref, gram_ref):
+    weight = low_input(params).astype(F32)
+    weight = weight - jnp.sum(weight, -1, keepdims=True) * (1.0 / H)
+    win_ref[...] = jnp.zeros_like(win_ref)
+    for k, part in enumerate(split3(weight)):
+        win_ref[k * 32 : (k + 1) * 32, :] = part
+    for k, part in enumerate(split3(nt(win_ref[...], win_ref[...]) * (1.0 / H))):
+        gram_ref[k] = part
+
+
+def input_norm(x, start, win_ref, gram_ref):
+    row, lane = iota((LANES, LANES), 0), iota((LANES, LANES), 1)
+    pick = jnp.logical_and(lane < 96, jnp.logical_and(lane % 32 < IN, row == lane % 32 + start))
+    thrice = nn(x, pick.astype(F32).astype(BF16)).astype(BF16)
+    image = sum(nn(thrice, gram_ref[k]) for k in range(3))
+    var = jnp.sum(image * thrice.astype(F32), -1, keepdims=True)
+    return nn(thrice, win_ref[...]), lax.rsqrt(jnp.maximum(var, 0.0) + 1e-05)
 
 
 def tile_span(t):
@@ -609,28 +633,36 @@
 
     @pl.when(active > 0)
     def _():
-        lax.fori_loop(0, n, compact, 0)
-
-    rows_f[pl.ds(number, TILE), :] = jnp.zeros((TILE, LANES), F32)
+        lax.fori_loop(0, n, compact, 0, unroll=4)
+
+    rows_f[pl.ds(number, AHEAD_TILES * TILE), :] = jnp.zeros((AHEAD_TILES * TILE, LANES), F32)
+    bundles = (tiles + AHEAD_TILES - 1) // AHEAD_TILES
 
     until = (iota((TILE, TILE), 1) < iota((TILE, TILE), 0)).astype(F32).astype(BF16)
     place = iota((TILE, TILE), 1).astype(F32)
     this = critic.astype(F32)
 
-    def choose(t, base):
-        wide = rows_f[tile_span(t), :]
-        x = wide.astype(BF16)
-        xc_ref[tile_span(t), :] = x
-        wanted = jnp.logical_or(wide[:, L_S0 : L_S0 + 1] == this, wide[:, L_S1 : L_S1 + 1] == this)
-        wanted = jnp.where(jnp.logical_and(wanted, wide[:, L_BOOT : L_BOOT + 1] > 0.0), 1.0, 0.0)
-        order = nn(until, jnp.broadcast_to(wanted, (TILE, LANES)).astype(BF16))[:, 0:1]
-        chosen = (jnp.where(wanted > 0.0, order, -1.0) == place).astype(F32).astype(BF16)
-        hot[t] = chosen
-        picked[pl.ds(base, TILE), :] = tn(chosen, x)
-        base_s[t] = base
-        return base + jnp.sum(wanted).astype(I32)
-
-    chosen_rows = lax.fori_loop(0, tiles, choose, 0)
+    def choose(b, base):
+        chosen, counts = [], []
+        for i in range(AHEAD_TILES):
+            t = b * AHEAD_TILES + i
+            wide = rows_f[tile_span(t), :]
+            x = wide.astype(BF16)
+            xc_ref[tile_span(t), :] = x
+            wanted = jnp.logical_or(wide[:, L_S0 : L_S0 + 1] == this, wide[:, L_S1 : L_S1 + 1] == this)
+            wanted = jnp.where(jnp.logical_and(wanted, wide[:, L_BOOT : L_BOOT + 1] > 0.0), 1.0, 0.0)
+            order = nn(until, jnp.broadcast_to(wanted, (TILE, LANES)).astype(BF16))[:, 0:1]
+            to = (jnp.where(wanted > 0.0, order, -1.0) == place).astype(F32).astype(BF16)
+            hot[t] = to
+            chosen.append(tn(to, x))
+            counts.append(jnp.sum(wanted).astype(I32))
+        for i in range(AHEAD_TILES):
+            picked[pl.ds(base, TILE), :] = chosen[i]
+            base_s[b * AHEAD_TILES + i] = base
+            base = base + counts[i]
+        return base
+
+    chosen_rows = lax.fori_loop(0, bundles, choose, 0)
     picked[pl.ds(chosen_rows, TILE), :] = jnp.zeros((TILE, LANES), F32)
     chosen_tiles = (chosen_rows + TILE - 1) // TILE
     half = jnp.where(iota((32, 1), 0) < IN + 4, 0.5, 1.0)
@@ -651,17 +683,19 @@
     lax.fori_loop(0, chosen_tiles, tile, 0)
     value[tile_span(chosen_tiles), :] = jnp.zeros((TILE, LANES), F32)
 
-    def spread(t, _):
+    def spread(b, _):
         lane = iota((TILE, LANES), 1)
-        high, mid, rest = (v.astype(F32) for v in split3(value[pl.ds(base_s[t], TILE), :]))
-        parts = jnp.where(lane == 0, high, jnp.where(lane == 1, mid, jnp.where(lane == 2, rest, 0.0)))
-        q = jnp.broadcast_to(jnp.sum(nn(hot[t], parts.astype(BF16)), -1, keepdims=True), (TILE, LANES))
-        for h in range(TILE // LANES):
-            flat = jnp.transpose(q[h * LANES : (h + 1) * LANES, :])
-            q_ref[pl.ds(t * (TILE // LANES) + h, 1), :] = flat[0:1, :]
+        for i in range(AHEAD_TILES):
+            t = b * AHEAD_TILES + i
+            high, mid, rest = (v.astype(F32) for v in split3(value[pl.ds(base_s[t], TILE), :]))
+            parts = jnp.where(lane == 0, high, jnp.where(lane == 1, mid, jnp.where(lane == 2, rest, 0.0)))
+            q = jnp.broadcast_to(jnp.sum(nn(hot[t], parts.astype(BF16)), -1, keepdims=True), (TILE, LANES))
+            for h in range(TILE // LANES):
+                flat = jnp.transpose(q[h * LANES : (h + 1) * LANES, :])
+                q_ref[pl.ds(t * (TILE // LANES) + h, 1), :] = flat[0:1, :]
         return 0
 
-    lax.fori_loop(0, tiles, spread, 0)
+    lax.fori_loop(0, bundles, spread, 0)
 
 
 def target_values(plan, rows, width, role, x, weights, params):
@@ -678,7 +712,7 @@
         in_specs=[smem, vmem, vmem, vmem],
         out_specs=(vmem, vmem, smem),
         scratch_shapes=[
-            pltpu.VMEM((capacity + TILE + x.shape[1], LANES), F32),
+            pltpu.VMEM((capacity + AHEAD_TILES * TILE + x.shape[1], LANES), F32),
             pltpu.VMEM((capacity + TILE, LANES), F32),
             pltpu.VMEM((capacity + TILE, LANES), F32),
             pltpu.VMEM((capacity // TILE, TILE, TILE), BF16),
@@ -689,7 +723,7 @@
             pltpu.SMEM((capacity // TILE,), I32),
             pltpu.SemaphoreType.DMA,
         ],
-        compiler_params=pltpu.CompilerParams(vmem_limit_bytes=VMEM_LIMIT),
+        compiler_params=pltpu.CompilerParams(vmem_limit_bytes=28 * MIB),
         name="target_values",
     )(role, x, weights, params)
 
@@ -749,13 +783,13 @@
         in_specs=[vmem],
         out_specs=vmem,
         scratch_shapes=[pltpu.SemaphoreType.DMA((CRIT,)), pltpu.SemaphoreType.DMA((CRIT,))],
-        compiler_params=pltpu.CompilerParams(collective_id=1, has_side_effects=True, vmem_limit_bytes=VMEM_LIMIT),
+        compiler_params=pltpu.CompilerParams(collective_id=1, has_side_effects=True, vmem_limit_bytes=8 * MIB),
         name="share_values",
     )(q)
 
 
 def critic_kernel(
-    plan, width, role_ref, info_ref, xc_ref, q_ref, shares, p_ref, grad_ref, small_ref, sums_ref, w_ref, z_one, slope, act, low, fact, par, win, picks, acc
+    plan, width, role_ref, info_ref, xc_ref, q_ref, shares, p_ref, grad_ref, lowered_ref, small_ref, sums_ref, w_ref, z_one, slope, act, low, fact, par, win, gram, picks, acc
 ):
     number = info_ref[0]
     scale = 2.0 / jnp.maximum(info_ref[1], 1).astype(F32)
@@ -776,20 +810,28 @@
 
         lax.fori_loop(0, plan.turns, gather, 0)
     par[...] = assemble(p_ref, width, HALF)
-    win[...] = jnp.zeros_like(win)
-    win[0:32, :] = low_input(par[...])
+    input_layer(par[...], win, gram)
     grad_ref[...] = jnp.zeros_like(grad_ref)
     acc[...] = jnp.zeros_like(acc)
     picks[...] = jnp.zeros_like(picks)
     sums_ref[...] = jnp.zeros_like(sums_ref)
     gain1, shift1, gain2, shift2, head = (par[IN + k : IN + k + 1, :] for k in range(5))
 
+    hg = (0.5 * head) * gain2
+
     def fold(k, value):
         acc[32 + k * 8 : 40 + k * 8, :] += jnp.sum(value.reshape(TILE // 8, 8, H), 0)
 
     def tile(t, _):
         x = xc_ref[tile_span(t), :]
         wide = x.astype(F32)
+        pre, inv_one = input_norm(x, 0, win, gram)
+        z = pre * inv_one
+        z_one[...] = z
+        value, twice = swish_parts(z * (0.5 * gain1) + 0.5 * shift1)
+        slope[...] = 0.5 * twice
+        act[...] = value.astype(BF16)
+        pre = nn(act[...], w_ref[...])
         for h in range(TILE // LANES):
             picks[0:CRIT, :] = q_ref[:, pl.ds(t * (TILE // LANES) + h, 1), :].reshape(CRIT, LANES)
             table = jnp.transpose(picks[...])
@@ -800,25 +842,22 @@
             base = part[:, L_BASE : L_BASE + 1] + part[:, L_BASE + 1 : L_BASE + 2] + part[:, L_BASE + 2 : L_BASE + 3]
             goal = base + jnp.where(part[:, L_BOOT : L_BOOT + 1] > 0.0, REWARD_DISCOUNT * jnp.minimum(one, two), 0.0)
             fact[h * LANES : (h + 1) * LANES, 0:1] = goal
-        z, inv_one = norm_parts(nn(x, win[...]))
-        z_one[...] = z
-        value, twice = swish_parts(z * (0.5 * gain1) + 0.5 * shift1)
-        slope[...] = 0.5 * twice
-        act[...] = value.astype(BF16)
-        z, inv = norm_parts(nn(act[...], w_ref[...]))
+        z, inv = norm_parts(pre)
         value, twice = swish_parts(z * (0.5 * gain2) + 0.5 * shift2)
         q = jnp.sum(value * head, -1, keepdims=True)
         error = (q - fact[:, 0:1]) * wide[:, L_VALID : L_VALID + 1]
         sums_ref[0:1, :] += jnp.broadcast_to(jnp.sum(error * error, 0, keepdims=True), (1, LANES))
         dq = error * scale
-        fold(4, dq * value)
-        dy = dq * (twice * (0.5 * head))
-        fold(3, dy)
-        fold(2, dy * z)
-        dz = dy * gain2
+        flat = jnp.transpose(jnp.broadcast_to(dq, (TILE, LANES)))[0:8, :]
+        high, rest = split2(flat)
+        weigh = jnp.concatenate([high, rest], 0)
+        tz = twice * z
+        for k, v in ((4, value), (3, twice), (2, tz)):
+            acc[32 + k * 8 : 40 + k * 8, :] += nn(weigh, v.astype(BF16))[4:12]
+        dz = twice * hg
         mean = jnp.sum(dz, -1, keepdims=True) * (1.0 / H)
-        along = jnp.sum(dz * z, -1, keepdims=True) * (1.0 / H)
-        low[...] = (inv * (dz - mean - z * along)).astype(BF16)
+        along = jnp.sum(tz * hg, -1, keepdims=True) * (1.0 / H)
+        low[...] = ((inv * dq) * (dz - mean - z * along)).astype(BF16)
         down = nt(low[...], w_ref[...])
         grad_ref[...] += tn(act[...], low[...])
         z = z_one[...]
@@ -832,7 +871,12 @@
         return 0
 
     lax.fori_loop(0, tiles, tile, 0)
+    lowered_ref[...] = grad_ref[...].astype(BF16)
     sums_ref[1:2, :] = jnp.broadcast_to(info_ref[1].astype(F32), (1, LANES))
+    for k in range(2, 5):
+        total = jnp.sum(acc[32 + k * 8 : 40 + k * 8, :], 0, keepdims=True) * 0.25
+        acc[32 + k * 8 : 40 + k * 8, :] = jnp.zeros((8, H), F32)
+        acc[32 + k * 8 : 33 + k * 8, :] = total if k == 4 else total * (0.5 * head)
     for k in range(5):
         acc[IN + k : IN + k + 1, :] = jnp.sum(acc[32 + k * 8 : 40 + k * 8, :], 0, keepdims=True)
     for i in range(H // width):
@@ -848,11 +892,12 @@
         functools.partial(critic_kernel, plan, width),
         out_shape=(
             jax.ShapeDtypeStruct((H, H), F32),
+            jax.ShapeDtypeStruct((H, H), BF16),
             jax.ShapeDtypeStruct((H // width, 32, LANES), F32),
             jax.ShapeDtypeStruct((8, LANES), F32),
         ),
         in_specs=[smem, smem, vmem, vmem, (vmem,) * plan.groups, vmem],
-        out_specs=(vmem,) * 3,
+        out_specs=(vmem,) * 4,
         scratch_shapes=[
             pltpu.VMEM((H, H), BF16),
             pltpu.VMEM((TILE, H), F32),
@@ -862,10 +907,11 @@
             pltpu.VMEM((TILE, LANES), F32),
             pltpu.VMEM((32, H), F32),
             pltpu.VMEM((LANES, H), BF16),
+            pltpu.VMEM((3, LANES, LANES), BF16),
             pltpu.VMEM((16, LANES), F32),
             pltpu.VMEM((72, H), F32),
         ],
-        compiler_params=pltpu.CompilerParams(vmem_limit_bytes=VMEM_LIMIT),
+        compiler_params=pltpu.CompilerParams(vmem_limit_bytes=36 * MIB),
         name="critic_step",
     )(role, info, xc, q_all, shares, params)
 
@@ -880,6 +926,7 @@
 def shampoo_kernel(
     plan,
     g_ref,
+    lowered_ref,
     small_ref,
     sums_ref,
     mom_ref,
@@ -934,7 +981,7 @@
         turn = turn_of(step)
         s = other + groups * turn
         copy = to_device(
-            g_ref.at[block(s)],
+            lowered_ref.at[block(s)],
             parts.at[groups - 2 - i, turn],
             send_one.at[step, i],
             recv_one.at[groups - 2 - i, turn],
@@ -1004,11 +1051,11 @@
         @pl.when(s < n)
         def _():
             for i in range(groups - 1):
-                pltpu.make_async_copy(pieces.at[0], parts.at[i, turn], recv_one.at[i, turn]).wait()
+                pltpu.make_async_copy(parts.at[0, 0], parts.at[i, turn], recv_one.at[i, turn]).wait()
             value = g_ref[block(s)]
             for i in range(groups - 1):
-                value = value + parts[i, turn]
-            pieces[turn] = value
+                value = value + parts[i, turn].astype(F32)
+            pieces[turn] = value.astype(BF16)
 
             @pl.when(s == index)
             def _():
@@ -1076,7 +1123,7 @@
         sums, stats = [], []
         for i, j in subs:
             at = place(c, i, j)
-            grad = given[at]
+            grad = given[at].astype(F32)
             mo_ref[at] = MOMENTUM * mom_ref[at] + grad
             low = packed(grad.astype(BF16))
             square, flip = tops(nt(jnp.concatenate([low, eye_low], 0), diag_rows(low)), 2)
@@ -1229,7 +1276,7 @@
         lax.fori_loop(1, n, finish_total, 0)
 
 
-def shampoo(plan, columns, grad, small, sums, moment, left, right, weight):
+def shampoo(plan, columns, grad, lowered, small, sums, moment, left, right, weight):
     vmem = pl.BlockSpec(memory_space=pltpu.VMEM)
     shape = jax.ShapeDtypeStruct(moment.shape, F32)
     _width, mine, per = chunks_of(columns)
@@ -1239,12 +1286,12 @@
         functools.partial(shampoo_kernel, plan),
         out_shape=(shape,) * 4
         + (jax.ShapeDtypeStruct((32, -(-columns // LANES) * LANES), F32), jax.ShapeDtypeStruct((8, LANES), F32)),
-        in_specs=[vmem] * 7,
+        in_specs=[vmem] * 8,
         out_specs=(vmem,) * 6,
         scratch_shapes=[
-            pltpu.VMEM((plan.groups - 1, plan.turns) + piece, F32),
-            pltpu.VMEM((plan.turns,) + piece, F32),
-            pltpu.VMEM((CRIT,) + piece, F32),
+            pltpu.VMEM((plan.groups - 1, plan.turns) + piece, BF16),
+            pltpu.VMEM((plan.turns,) + piece, BF16),
+            pltpu.VMEM((CRIT,) + piece, BF16),
             pltpu.VMEM((plan.groups, mine, 32, LANES), F32),
             pltpu.VMEM((plan.workers, 8, LANES), F32),
             dma((plan.turns, plan.groups - 1)),
@@ -1256,9 +1303,9 @@
             dma((plan.n,)),
             dma((plan.workers,)),
         ],
-        compiler_params=pltpu.CompilerParams(collective_id=2, has_side_effects=True, vmem_limit_bytes=VMEM_LIMIT),
+        compiler_params=pltpu.CompilerParams(collective_id=2, has_side_effects=True, vmem_limit_bytes=24 * MIB),
         name="shampoo",
-    )(grad, small, sums, moment, left, right, weight)
+    )(grad, lowered, small, sums, moment, left, right, weight)
 
 
 def adamw(grad, moment, square, weight, rate):
@@ -1310,20 +1357,15 @@
     )
     w_target, share, x, params = dispatch(
         plan,
-        critic_hidden,
-        target_hidden,
-        (critic_in, critic_norms),
-        (target_in, target_norms),
-        jnp.stack([target_head, critic_head]),
-        (state_action.T, next_state.T, facts),
-        (noise_table.T, policy_in, policy_mid, policy_out.T),
+        (critic_hidden, target_hidden, critic_in, critic_norms, target_in, target_norms, jnp.stack([target_head, critic_head]))
+        + (state_action.T, next_state.T, facts, noise_table.T, policy_in, policy_mid, policy_out.T),
     )
     shares = (share,) + tuple(lax.ppermute(share, ("dp", "mp"), plan.shift(k)) for k in range(1, plan.groups))
     xc, q, info = target_values(plan, rows, width, role, x, w_target, params)
     q_all = share_values(plan, q)
-    grad_hidden, grad_small, sums = critic_step(plan, width, role, info, xc, q_all, shares, params)
+    grad_hidden, lowered, grad_small, sums = critic_step(plan, width, role, info, xc, q_all, shares, params)
     hidden_momentum, left_renewed, right_renewed, hidden_updated, own, totals = shampoo(
-        plan, columns, grad_hidden, grad_small, sums, hidden_moment, left_stats, right_stats, critic_hidden
+        plan, columns, grad_hidden, lowered, grad_small, sums, hidden_moment, left_stats, right_stats, critic_hidden
     )
     own = own[:, :columns]
     loss_total, counted = totals[0, 0], totals[1, 0]

time: 257 us -> 221 us (0.86)
  Pallas kernels: 229 us -> 193 us
  local copies, waits for them, and re-layouts: 12.5 us -> 17.1 us
  other arithmetic: 6.64 us -> 3.45 us
    pallas_call x1, Pallas kernels: 83.5 us -> 61.9 us  [shampoo(): pl.pallas_call(functools.partial(shampoo_kernel, plan), out_shape=(shape,...]
    pallas_call x1, Pallas kernels: 22.3 us -> 14.1 us  [target_values(): pl.pallas_call(functools.partial(target_kernel, plan, width), out_shape=(...]
    unnamed x32 -> x54, local copies, waits for them, and re-layouts: 8.33 us -> 14.3 us
    pallas_call x1, Pallas kernels: 50 us -> 46.7 us  [critic_step(): pl.pallas_call(functools.partial(critic_kernel, plan, width), out_shape=(...]
  transfers between devices with their start and end apart: 2 -> 2, of which waited for: 0 -> 0; matrix products, arithmetic and copies ran while one was open for 0% -> 0% of each run, Pallas kernels for 13% -> 11%
where the time goes in v4:
time: 221 us; the launch traced here: 220 us
  Pallas kernels  193 us (87%)
  local copies, waits for them, and re-layouts  17.1 us (8%)
  starting transfers between devices  5.56 us (3%)
  other arithmetic  3.45 us (2%)
    pallas_call x1, Pallas kernels, shampoo(): pl.pallas_call(functools.partial(shampoo_kernel, plan), out_shape=(shape,...  61.9 us
    pallas_call x1, Pallas kernels, dispatch(): pl.pallas_call(functools.partial(dispatch_kernel, plan), out_shape=(jax.S...  60.7 us
    pallas_call x1, Pallas kernels, critic_step(): pl.pallas_call(functools.partial(critic_kernel, plan, width), out_shape=(...  46.7 us
    unnamed x54, local copies, waits for them, and re-layouts  14.3 us
    pallas_call x1, Pallas kernels, target_values(): pl.pallas_call(functools.partial(target_kernel, plan, width), out_shape=(...  14.1 us
    pallas_call x1, Pallas kernels, share_values(): pl.pallas_call(functools.partial(share_kernel, plan), out_shape=jax.Shape...  9.95 us
    ppermute x2, starting transfers between devices, local(): lax.ppermute(share, ('dp', 'mp'), plan.shift(k))  5.56 us
  transfers between devices with their start and end apart: 2, of which 0 were waited for; matrix products, arithmetic and copies ran while one was open for 0% of the time, Pallas kernels for 11%

profile of v4, /device:TPU:9, one launch (start us, length us, event | category | flops | bytes accessed | tf_op | source)
XLA Modules:
  0.0 220.4 jit_solution(3697839569098456094)
XLA Ops:
  0.6 0.7 stack.38
  1.3 0.7 stack.39
  2.0 0.8 slice_bitcast_fusion.1
  2.9 0.7 add_convert_fusion
  3.6 0.8 maximum_maximum_fusion.inputs_9_
  4.3 1.3 copy-done
  5.7 1.3 copy-done.2
  7.0 0.8 copy-done.6
  7.7 0.9 copy-done.8
  8.7 0.8 copy-done.9
  9.4 0.7 copy-done.10
  10.2 0.7 copy-done.11
  10.9 0.7 copy-done.12
  11.6 0.7 copy-done.14
  12.3 0.7 copy-done.15
  13.0 0.7 copy-done.16
  13.7 0.7 copy-done.17
  14.4 60.7 %dispatch.1 = (bf16[1024,1024]{1,0:T(8,128)(2,1)S(1)}, bf16[11,64,512]{2,1,0:T(8,128)(2,1)}, bf16[32,96,128]{2,1,0:T(8,128)(2,1)S(1)}, f32[16,32,128]{2,1,0:T(8,128)S(1)}) custom-call(f32[10,64,512]{2,1,0:T(8,128)S(1)} %copy-done, f32[10,64,512]{2,1,0:T(8,128)S(1)} %copy-done.2, f32[23,320]{1,0:T(8,128)S(1)} %copy-done.6, f32[4,320]{1,0:T(4,128)S(1)} %copy-done.12, ...), custom_call_target="tpu_custom_call" | custom-call | tf_op jit(solution)/shard_map/dispatch/pallas_call | solution.py:525
  75.1 2.3 %collective-permute-start.1 = (bf16[11,64,512]{2,1,0:T(8,128)(2,1)}, bf16[11,64,512]{2,1,0:T(8,128)(2,1)}, u32[]{:S(2)}, u32[]{:S(2)}) collective-permute-start(bf16[11,64,512]{2,1,0:T(8,128)(2,1)} %get-tuple-element.38.shares_0_), channel_id=1, source_target_pairs={{0,2},{1,0},{2,1},{3,19},{18,3},{19,18},{4,6},{5,4},{6,5},{7,23},{... | collective-permute-start | bytes 2162696 | tf_op jit(solution)/shard_map/ppermute | solution.py:1363
  77.4 3.3 %collective-permute-start = (bf16[11,64,512]{2,1,0:T(8,128)(2,1)}, bf16[11,64,512]{2,1,0:T(8,128)(2,1)}, u32[]{:S(2)}, u32[]{:S(2)}) collective-permute-start(bf16[11,64,512]{2,1,0:T(8,128)(2,1)} %get-tuple-element.38.shares_0_), channel_id=1, source_target_pairs={{0,1},{1,2},{2,0},{3,18},{18,19},{19,3},{4,5},{5,6},{6,4},{7,22},{... | collective-permute-start | bytes 2162696 | tf_op jit(solution)/shard_map/ppermute | solution.py:1363
  80.9 14.1 %target_values.1 = (bf16[6144,128]{1,0:T(8,128)(2,1)S(1)}, f32[48,128]{1,0:T(8,128)S(1)}, s32[2]{0:T(128)S(1)}) custom-call(s32[3]{0:T(128)S(1)} %pad_add_fusion.role_ref, bf16[32,96,128]{2,1,0:T(8,128)(2,1)S(1)} %get-tuple-element.32.x_ref, bf16[1024,1024]{1,0:T(8,128)(2,1)S(1)} %get-tuple-element.33.w_ref, f32[16,32,128]{2,1,0:T(8,128)S(1)} %get-tuple-element.34.p_ref), custom_call_target="tpu_custom_call" | custom-call | tf_op jit(solution)/shard_map/target_values/pallas_call | solution.py:705
  95.0 10.0 %share_values.1.q_ref = f32[10,48,128]{2,1,0:T(8,128)S(1)} custom-call(f32[48,128]{1,0:T(8,128)S(1)} %get-tuple-element.37.q_ref), custom_call_target="tpu_custom_call" | custom-call | tf_op jit(solution)/shard_map/share_values/pallas_call | solution.py:780
  105.0 46.7 %critic_step.1 = (f32[1024,1024]{1,0:T(8,128)S(1)}, bf16[1024,1024]{1,0:T(8,128)(2,1)S(1)}, f32[16,32,128]{2,1,0:T(8,128)S(1)}, f32[8,128]{1,0:T(8,128)S(1)}) custom-call(s32[3]{0:T(128)S(1)} %pad_add_fusion.role_ref, s32[2]{0:T(128)S(1)} %get-tuple-element.35.info_ref, bf16[6144,128]{1,0:T(8,128)(2,1)S(1)} %get-tuple-element.36.xc_ref, ...), custom_call_target="tpu_custom_call" | custom-call | tf_op jit(solution)/shard_map/critic_step/pallas_call | solution.py:891
  151.9 61.9 %shampoo.1 = (f32[10,64,512]{2,1,0:T(8,128)S(1)}, f32[10,64,512]{2,1,0:T(8,128)S(1)}, f32[10,64,512]{2,1,0:T(8,128)S(1)}, f32[10,64,512]{2,1,0:T(8,128)S(1)}, f3...) custom-call(f32[1024,1024]{1,0:T(8,128)S(1)} %get-tuple-element.39.g_ref, ...), custom_call_target="tpu_custom_call" | custom-call | tf_op jit(solution)/shard_map/shampoo/pallas_call | solution.py:1285
  213.7 0.5 fusion.6
  214.3 0.6 multiply_subtract_fusion.1
  214.9 0.7 multiply_subtract_fusion
  215.6 0.6 multiply_subtract_fusion.2
  216.2 1.1 copy.46
  217.3 1.1 copy.47
  218.3 1.1 copy.48
  219.4 1.1 copy.49
  (45 shorter events, 0.3 us)
Async XLA Ops:
  4.3 1.3 copy-start
  5.7 1.3 copy-start.2
  7.0 0.8 copy-start.6
  7.7 0.9 copy-start.8
  8.7 0.8 copy-start.9
  9.4 0.7 copy-start.10
  10.2 0.7 copy-start.11
  10.9 0.7 copy-start.12
  11.6 0.7 copy-start.14
  12.3 0.7 copy-start.15
  13.0 0.7 copy-start.16
  13.7 0.7 copy-start.17
  75.1 29.8 %collective-permute-start.1 = (bf16[11,64,512]{2,1,0:T(8,128)(2,1)}, bf16[11,64,512]{2,1,0:T(8,128)(2,1)}, u32[]{:S(2)}, u32[]{:S(2)}) collective-permute-start(bf16[11,64,512]{2,1,0:T(8,128)(2,1)} %get-tuple-element.38.shares_0_), channel_id=1, source_target_pairs={{0,2},{1,0},{2,1},{3,19},{18,3},{19,18},{4,6},{5,4},{6,5},{7,23},{... | collective-permute-start | bytes 2162696 | tf_op jit(solution)/shard_map/ppermute | solution.py:1363
  77.4 27.5 %collective-permute-start = (bf16[11,64,512]{2,1,0:T(8,128)(2,1)}, bf16[11,64,512]{2,1,0:T(8,128)(2,1)}, u32[]{:S(2)}, u32[]{:S(2)}) collective-permute-start(bf16[11,64,512]{2,1,0:T(8,128)(2,1)} %get-tuple-element.38.shares_0_), channel_id=1, source_target_pairs={{0,1},{1,2},{2,0},{3,18},{18,19},{19,3},{4,5},{5,6},{6,4},{7,22},{... | collective-permute-start | bytes 2162696 | tf_op jit(solution)/shard_map/ppermute | solution.py:1363
  80.9 70.8 %copy-start.5 = (f32[10,64,512]{2,1,0:T(8,128)S(1)}, f32[10,64,512]{2,1,0:T(8,128)}, u32[]{:S(2)}) copy-start(f32[10,64,512]{2,1,0:T(8,128)} %right_ref.1) | copy-start | bytes 3932164
  105.0 46.8 %copy-start.1 = (f32[10,64,512]{2,1,0:T(8,128)S(1)}, f32[10,64,512]{2,1,0:T(8,128)}, u32[]{:S(2)}) copy-start(f32[10,64,512]{2,1,0:T(8,128)} %w_ref.1) | copy-start | bytes 3932164
  105.0 46.8 %copy-start.3 = (f32[10,64,512]{2,1,0:T(8,128)S(1)}, f32[10,64,512]{2,1,0:T(8,128)}, u32[]{:S(2)}) copy-start(f32[10,64,512]{2,1,0:T(8,128)} %mom_ref.1) | copy-start | bytes 3932164
  105.0 46.8 %copy-start.4 = (f32[10,64,512]{2,1,0:T(8,128)S(1)}, f32[10,64,512]{2,1,0:T(8,128)}, u32[]{:S(2)}) copy-start(f32[10,64,512]{2,1,0:T(8,128)} %left_ref.1) | copy-start | bytes 3932164
  151.8 62.5 %copy-start.13 = (f32[4,320]{1,0:T(4,128)S(1)}, f32[4,320]{1,0:T(4,128)}, u32[]{:S(2)}) copy-start(f32[4,320]{1,0:T(4,128)} %inputs_3_.1) | copy-start | bytes 15364
  151.8 62.5 %copy-start.21 = (f32[4,320]{1,0:T(4,128)S(1)}, f32[4,320]{1,0:T(4,128)}, u32[]{:S(2)}) copy-start(f32[4,320]{1,0:T(4,128)} %param.42) | copy-start | bytes 15364
  151.8 62.5 %copy-start.22 = (f32[4,320]{1,0:T(4,128)S(1)}, f32[4,320]{1,0:T(4,128)}, u32[]{:S(2)}) copy-start(f32[4,320]{1,0:T(4,128)} %param.41) | copy-start | bytes 15364
  151.8 63.1 %copy-start.7 = (f32[23,320]{1,0:T(8,128)S(1)}, f32[23,320]{1,0:T(8,128)}, u32[]{:S(2)}) copy-start(f32[23,320]{1,0:T(8,128)} %inputs_2_.1) | copy-start | bytes 88324
  151.8 63.1 %copy-start.18 = (f32[23,320]{1,0:T(8,128)S(1)}, f32[23,320]{1,0:T(8,128)}, u32[]{:S(2)}) copy-start(f32[23,320]{1,0:T(8,128)} %param.39) | copy-start | bytes 88324
  151.8 63.1 %copy-start.19 = (f32[23,320]{1,0:T(8,128)S(1)}, f32[23,320]{1,0:T(8,128)}, u32[]{:S(2)}) copy-start(f32[23,320]{1,0:T(8,128)} %param.38) | copy-start | bytes 88324
  151.8 63.8 %copy-start.20 = (f32[320]{0:T(512)S(1)}, f32[320]{0:T(512)}, u32[]{:S(2)}) copy-start(f32[320]{0:T(512)} %param.43) | copy-start | bytes 3844
  151.8 63.8 %copy-start.23 = (f32[320]{0:T(512)S(1)}, f32[320]{0:T(512)}, u32[]{:S(2)}) copy-start(f32[320]{0:T(512)} %param.45) | copy-start | bytes 3844
  151.9 63.8 %copy-start.24 = (f32[320]{0:T(512)S(1)}, f32[320]{0:T(512)}, u32[]{:S(2)}) copy-start(f32[320]{0:T(512)} %param.44) | copy-start | bytes 3844

commit v5 on v4

--- a/solution.py
+++ b/solution.py
@@ -155,7 +155,7 @@
     return jnp.concatenate(groups, 1)
 
 
-def all_barrier(plan, dp, mp):
+def greet_all(plan, dp, mp):
     barrier = pltpu.get_barrier_semaphore()
 
     def tell(s, _):
@@ -168,7 +168,10 @@
         return 0
 
     lax.fori_loop(0, plan.n, tell, 0)
-    pl.semaphore_wait(barrier, plan.n - 1)
+
+
+def await_all(plan):
+    pl.semaphore_wait(pltpu.get_barrier_semaphore(), plan.n - 1)
 
 
 def dispatch_kernel(
@@ -198,10 +201,11 @@
     loads = [pltpu.make_async_copy(src, dst, stage_sem.at[k]) for k, (src, dst) in enumerate(zip(inputs, stage))]
     for load in loads:
         load.start()
+    dp, mp = lax.axis_index("dp"), lax.axis_index("mp")
+    greet_all(plan, dp, mp)
     crit_ref, targ_ref, crit_in, crit_norms, targ_in, targ_norms, head_ref = stage[:7]
-    sa_ref, ns_ref, rows_ref, table_ref, pin_ref, pmid_ref, pout_ref = stage[7:]
+    sa_ref, ns_ref, reward_ref, done_ref, index_ref, subs_ref, table_ref, pin_ref, pmid_ref, pout_ref = stage[7:]
     crit_small, targ_small = (crit_in, crit_norms), (targ_in, targ_norms)
-    dp, mp = lax.axis_index("dp"), lax.axis_index("mp")
     me = plan.rank(dp, mp)
     index = dp * plan.n_mp + mp
     groups, workers = plan.groups, plan.workers
@@ -220,7 +224,7 @@
         return 0
 
     lax.fori_loop(0, CRIT, to_low, 0)
-    all_barrier(plan, dp, mp)
+    await_all(plan)
 
     def w_slot(s):
         sdp, smp = plan.device(s)
@@ -241,7 +245,7 @@
 
     def send_weights(t):
         def one(i, _):
-            c = (critic + i) % CRIT
+            c = (critic + 2 * CRIT + i * (1 - 2 * (index % 2))) % CRIT
             k, dst, recv, copy = first_hop(t, c)
 
             @pl.when(k == me)
@@ -302,8 +306,12 @@
     keep = lane < ACT
     means = nn(hidden, spread(0))
     raw = nn(hidden, spread(ACT))
-    facts = rows_ref[...]
-    across = jnp.transpose(facts)
+    across = []
+    for i in range(rows // LANES):
+        lines = [reward_ref[i : i + 1, :], done_ref[i : i + 1, :].astype(F32), index_ref[i : i + 1, :].astype(F32)]
+        lines += [subs_ref[:, i * LANES : (i + 1) * LANES].astype(F32), jnp.zeros((3, LANES), F32)]
+        across.append(jnp.transpose(jnp.concatenate(lines, 0)))
+    across = jnp.concatenate(across, 0)
     picked = (iota((rows, table_ref.shape[1]), 1) == across[:, 2:3].astype(I32)).astype(F32).astype(BF16)
     noise = jnp.zeros((rows, LANES), F32)
     for part in split3(table_ref[...]):
@@ -336,7 +344,8 @@
     ).astype(BF16)
 
     pairs = msg.shape[1]
-    valid = (facts[1:2, :] != 2.0).astype(F32)
+    done_row = jnp.concatenate([done_ref[i : i + 1, :] for i in range(rows // LANES)], 1)
+    valid = (done_row != 2).astype(F32)
     before = (iota((rows, rows), 0) < iota((rows, rows), 1)).astype(F32).astype(BF16)
     order = nn(jnp.broadcast_to(valid, (8, rows)).astype(BF16), before)[0:1, :]
     order = jnp.where(valid > 0.0, order, -1.0)
@@ -421,11 +430,19 @@
 
     @pl.when(me < workers)
     def _():
-        def relay_weight(t):
-            arrived_w(group + groups * t)
-            peers(lambda i: pass_weight(t, i).start())
-
-        each(turns, relay_weight)
+        def relay_weight(j):
+            t = j
+            if plan.turns == 11:
+                step = j // 2
+                away = jnp.where(step == 5, -3, ((step + 1) // 2) * (2 * (step % 2) - 1))
+                t = (turn + 5 * (j % 2) + away + 2 * plan.turns) % plan.turns
+
+            @pl.when(t < turns)
+            def _():
+                arrived_w(group + groups * t)
+                peers(lambda i: pass_weight(t, i).start())
+
+        each(plan.turns, relay_weight)
 
         @pl.when(passes_rows)
         def _():
@@ -550,7 +567,7 @@
             tuple(pltpu.VMEM(v.shape, v.dtype) for v in inputs),
             dma((len(inputs),)),
         ],
-        compiler_params=pltpu.CompilerParams(collective_id=0, has_side_effects=True, vmem_limit_bytes=20 * MIB),
+        compiler_params=pltpu.CompilerParams(collective_id=0, has_side_effects=True, vmem_limit_bytes=60 * MIB),
         name="dispatch",
     )(inputs)
 
@@ -595,9 +612,10 @@
 
 
 def target_kernel(
-    plan, width, role_ref, x_ref, w_ref, p_ref, xc_ref, q_ref, info_ref, rows_f, picked, value, hot, win, par, cnt_v, cnt_s, base_s, sem
+    plan, width, x_ref, w_ref, p_ref, xc_ref, q_ref, info_ref, rows_f, picked, value, hot, win, par, flat_q, cnt_v, cnt_s, base_s, sem
 ):
-    critic, group, active = role_ref[0], role_ref[1], role_ref[2]
+    me = plan.rank(lax.axis_index("dp"), lax.axis_index("mp"))
+    critic, group, active = me // plan.groups, me % plan.groups, (me < plan.workers).astype(I32)
     groups, n = plan.groups, plan.n
     pairs = x_ref.shape[1]
     first = x_ref[:, 0, :].astype(F32)
@@ -692,13 +710,14 @@
             q = jnp.broadcast_to(jnp.sum(nn(hot[t], parts.astype(BF16)), -1, keepdims=True), (TILE, LANES))
             for h in range(TILE // LANES):
                 flat = jnp.transpose(q[h * LANES : (h + 1) * LANES, :])
-                q_ref[pl.ds(t * (TILE // LANES) + h, 1), :] = flat[0:1, :]
+                flat_q[pl.ds(t * (TILE // LANES) + h, 1), :] = flat[0:1, :]
         return 0
 
     lax.fori_loop(0, bundles, spread, 0)
-
-
-def target_values(plan, rows, width, role, x, weights, params):
+    q_ref[...] = flat_q[...].astype(BF16)
+
+
+def target_values(plan, rows, width, x, weights, params):
     capacity = plan.cap(rows)
     vmem = pl.BlockSpec(memory_space=pltpu.VMEM)
     smem = pl.BlockSpec(memory_space=pltpu.SMEM)
@@ -706,10 +725,10 @@
         functools.partial(target_kernel, plan, width),
         out_shape=(
             jax.ShapeDtypeStruct((capacity, LANES), BF16),
-            jax.ShapeDtypeStruct((capacity // LANES, LANES), F32),
+            jax.ShapeDtypeStruct((capacity // LANES, LANES), BF16),
             jax.ShapeDtypeStruct((2,), I32),
         ),
-        in_specs=[smem, vmem, vmem, vmem],
+        in_specs=[vmem, vmem, vmem],
         out_specs=(vmem, vmem, smem),
         scratch_shapes=[
             pltpu.VMEM((capacity + AHEAD_TILES * TILE + x.shape[1], LANES), F32),
@@ -718,6 +737,7 @@
             pltpu.VMEM((capacity // TILE, TILE, TILE), BF16),
             pltpu.VMEM((LANES, H), BF16),
             pltpu.VMEM((32, H), F32),
+            pltpu.VMEM((capacity // LANES, LANES), F32),
             pltpu.VMEM((2 * plan.n + 8, LANES), I32),
             pltpu.SMEM((2 * plan.n + 8, LANES), I32),
             pltpu.SMEM((capacity // TILE,), I32),
@@ -725,7 +745,7 @@
         ],
         compiler_params=pltpu.CompilerParams(vmem_limit_bytes=28 * MIB),
         name="target_values",
-    )(role, x, weights, params)
+    )(x, weights, params)
 
 
 def share_kernel(plan, q_ref, all_ref, send, recv):
@@ -779,7 +799,7 @@
     vmem = pl.BlockSpec(memory_space=pltpu.VMEM)
     return pl.pallas_call(
         functools.partial(share_kernel, plan),
-        out_shape=jax.ShapeDtypeStruct((CRIT,) + q.shape, F32),
+        out_shape=jax.ShapeDtypeStruct((CRIT,) + q.shape, BF16),
         in_specs=[vmem],
         out_specs=vmem,
         scratch_shapes=[pltpu.SemaphoreType.DMA((CRIT,)), pltpu.SemaphoreType.DMA((CRIT,))],
@@ -789,14 +809,15 @@
 
 
 def critic_kernel(
-    plan, width, role_ref, info_ref, xc_ref, q_ref, shares, p_ref, grad_ref, lowered_ref, small_ref, sums_ref, w_ref, z_one, slope, act, low, fact, par, win, gram, picks, acc
+    plan, width, info_ref, xc_ref, q_ref, shares, p_ref, grad_ref, lowered_ref, small_ref, sums_ref, w_ref, z_one, slope, act, low, fact, par, win, gram, picks, acc, q_all
 ):
     number = info_ref[0]
     scale = 2.0 / jnp.maximum(info_ref[1], 1).astype(F32)
     tiles = (number + TILE - 1) // TILE
     rw, cw = shares[0].shape[1:]
+    me = plan.rank(lax.axis_index("dp"), lax.axis_index("mp"))
     for k, share in enumerate(shares):
-        owner = (role_ref[1] + plan.groups - k) % plan.groups
+        owner = (me % plan.groups + plan.groups - k) % plan.groups
 
         def gather(t, _):
             s = owner + plan.groups * t
@@ -814,6 +835,7 @@
     grad_ref[...] = jnp.zeros_like(grad_ref)
     acc[...] = jnp.zeros_like(acc)
     picks[...] = jnp.zeros_like(picks)
+    q_all[...] = q_ref[...].astype(F32)
     sums_ref[...] = jnp.zeros_like(sums_ref)
     gain1, shift1, gain2, shift2, head = (par[IN + k : IN + k + 1, :] for k in range(5))
 
@@ -833,7 +855,7 @@
         act[...] = value.astype(BF16)
         pre = nn(act[...], w_ref[...])
         for h in range(TILE // LANES):
-            picks[0:CRIT, :] = q_ref[:, pl.ds(t * (TILE // LANES) + h, 1), :].reshape(CRIT, LANES)
+            picks[0:CRIT, :] = q_all[:, pl.ds(t * (TILE // LANES) + h, 1), :].reshape(CRIT, LANES)
             table = jnp.transpose(picks[...])
             part = wide[h * LANES : (h + 1) * LANES, :]
             critic = iota(table.shape, 1).astype(F32)
@@ -885,7 +907,7 @@
         small_ref[i] = pltpu.roll(block, LANES - offset, 1) if offset else block
 
 
-def critic_step(plan, width, role, info, xc, q_all, shares, params):
+def critic_step(plan, width, info, xc, q_all, shares, params):
     vmem = pl.BlockSpec(memory_space=pltpu.VMEM)
     smem = pl.BlockSpec(memory_space=pltpu.SMEM)
     return pl.pallas_call(
@@ -896,7 +918,7 @@
             jax.ShapeDtypeStruct((H // width, 32, LANES), F32),
             jax.ShapeDtypeStruct((8, LANES), F32),
         ),
-        in_specs=[smem, smem, vmem, vmem, (vmem,) * plan.groups, vmem],
+        in_specs=[smem, vmem, vmem, (vmem,) * plan.groups, vmem],
         out_specs=(vmem,) * 4,
         scratch_shapes=[
             pltpu.VMEM((H, H), BF16),
@@ -910,10 +932,11 @@
             pltpu.VMEM((3, LANES, LANES), BF16),
             pltpu.VMEM((16, LANES), F32),
             pltpu.VMEM((72, H), F32),
+            pltpu.VMEM(q_all.shape, F32),
         ],
         compiler_params=pltpu.CompilerParams(vmem_limit_bytes=36 * MIB),
         name="critic_step",
-    )(role, info, xc, q_all, shares, params)
+    )(info, xc, q_all, shares, params)
 
 
 PRECISE = 2
@@ -962,7 +985,8 @@
     mine, per = shares.shape[1], small_ref.shape[0]
     columns = own_ref.shape[1]
     chunk_width = H // per
-    all_barrier(plan, dp, mp)
+    greet_all(plan, dp, mp)
+    await_all(plan)
 
     def to_device(src, dst, send, recv, device):
         return pltpu.make_async_remote_copy(
@@ -1347,23 +1371,19 @@
     target_head,
     target_hidden,
 ):
-    me = plan.rank(lax.axis_index("dp"), lax.axis_index("mp"))
-    critic, group = me // plan.groups, me % plan.groups
-    role = jnp.stack([critic, group, (me < plan.workers).astype(I32)])
     rows, columns = state_action.shape[0], critic_in.shape[1]
     width = chunks_of(columns)[0]
-    facts = jnp.concatenate(
-        [reward[None], jnp.stack([done_flags, noise_index, subsets[:, 0], subsets[:, 1]]).astype(F32), jnp.zeros((3, rows), F32)], 0
-    )
+    lines = lambda v: v.reshape(rows // LANES, LANES)
     w_target, share, x, params = dispatch(
         plan,
         (critic_hidden, target_hidden, critic_in, critic_norms, target_in, target_norms, jnp.stack([target_head, critic_head]))
-        + (state_action.T, next_state.T, facts, noise_table.T, policy_in, policy_mid, policy_out.T),
+        + (state_action.T, next_state.T, lines(reward), lines(done_flags), lines(noise_index), subsets.T)
+        + (noise_table.T, policy_in, policy_mid, policy_out.T),
     )
     shares = (share,) + tuple(lax.ppermute(share, ("dp", "mp"), plan.shift(k)) for k in range(1, plan.groups))
-    xc, q, info = target_values(plan, rows, width, role, x, w_target, params)
+    xc, q, info = target_values(plan, rows, width, x, w_target, params)
     q_all = share_values(plan, q)
-    grad_hidden, lowered, grad_small, sums = critic_step(plan, width, role, info, xc, q_all, shares, params)
+    grad_hidden, lowered, grad_small, sums = critic_step(plan, width, info, xc, q_all, shares, params)
     hidden_momentum, left_renewed, right_renewed, hidden_updated, own, totals = shampoo(
         plan, columns, grad_hidden, lowered, grad_small, sums, hidden_moment, left_stats, right_stats, critic_hidden
     )

time: 221 us -> 202 us (0.914)
  Pallas kernels: 193 us -> 184 us
  local copies, waits for them, and re-layouts: 17.1 us -> 9.88 us
    unnamed x54 -> x40, local copies, waits for them, and re-layouts: 14.3 us -> 7.98 us
    pallas_call x1, Pallas kernels: 9.95 us -> 6.82 us  [share_values(): pl.pallas_call(functools.partial(share_kernel, plan), out_shape=jax.Shape...]
    pallas_call x1, Pallas kernels: 46.7 us -> 44.3 us  [critic_step(): pl.pallas_call(functools.partial(critic_kernel, plan, width), out_shape=(...]
    pallas_call x1, Pallas kernels: 60.7 us -> 58.4 us  [dispatch(): pl.pallas_call(functools.partial(dispatch_kernel, plan), out_shape=(jax.S...]
  transfers between devices with their start and end apart: 2 -> 2, of which waited for: 0 -> 0; matrix products, arithmetic and copies ran while one was open for 0% -> 0% of each run, Pallas kernels for 11% -> 10%
where the time goes in v5:
time: 202 us; the launch traced here: 203 us
  Pallas kernels  184 us (91%)
  local copies, waits for them, and re-layouts  9.88 us (5%)
  starting transfers between devices  5.56 us (3%)
  other arithmetic  2.48 us (1%)
    pallas_call x1, Pallas kernels, shampoo(): pl.pallas_call(functools.partial(shampoo_kernel, plan), out_shape=(shape,...  61.2 us
    pallas_call x1, Pallas kernels, dispatch(): pl.pallas_call(functools.partial(dispatch_kernel, plan), out_shape=(jax.S...  58.4 us
    pallas_call x1, Pallas kernels, critic_step(): pl.pallas_call(functools.partial(critic_kernel, plan, width), out_shape=(...  44.3 us
    pallas_call x1, Pallas kernels, target_values(): pl.pallas_call(functools.partial(target_kernel, plan, width), out_shape=(...  13.5 us
    unnamed x40, local copies, waits for them, and re-layouts  7.98 us
    pallas_call x1, Pallas kernels, share_values(): pl.pallas_call(functools.partial(share_kernel, plan), out_shape=jax.Shape...  6.82 us
    ppermute x2, starting transfers between devices, local(): lax.ppermute(share, ('dp', 'mp'), plan.shift(k))  5.56 us
  transfers between devices with their start and end apart: 2, of which 0 were waited for; matrix products, arithmetic and copies ran while one was open for 0% of the time, Pallas kernels for 10%

profile of v5, /device:TPU:9, one launch (start us, length us, event | category | flops | bytes accessed | tf_op | source)
XLA Modules:
  0.0 203.1 jit_solution(2946760847480434379)
XLA Ops:
  0.6 0.7 stack.9
  1.3 0.7 stack.10
  2.0 0.6 pad_maximum_fusion.inputs_6_
  2.6 58.4 %dispatch.1 = (bf16[1024,1024]{1,0:T(8,128)(2,1)}, bf16[11,64,512]{2,1,0:T(8,128)(2,1)}, bf16[32,96,128]{2,1,0:T(8,128)(2,1)}, f32[16,32,128]{2,1,0:T(8,128)}) custom-call(f32[10,64,512]{2,1,0:T(8,128)} %w_ref.1, f32[10,64,512]{2,1,0:T(8,128)} %inputs_1_.1, f32[23,320]{1,0:T(8,128)} %inputs_2_.1, f32[4,320]{1,0:T(4,128)} %inputs_3_.1, f32[23,320]{1,0:T(8,128)} %inputs_4_.1, ...), custom_call_target="tpu_custom_call" | custom-call | tf_op jit(solution)/shard_map/dispatch/pallas_call | solution.py:542
  61.0 2.3 %collective-permute-start.1 = (bf16[11,64,512]{2,1,0:T(8,128)(2,1)}, bf16[11,64,512]{2,1,0:T(8,128)(2,1)S(1)}, u32[]{:S(2)}, u32[]{:S(2)}) collective-permute-start(bf16[11,64,512]{2,1,0:T(8,128)(2,1)} %get-tuple-element.38.shares_0_), channel_id=1, source_target_pairs={{0,2},{1,0},{2,1},{3,19},{18,3},{19,18},{4,6},{5,4},{6,5},{7,23},{... | collective-permute-start | bytes 2162696 | tf_op jit(solution)/shard_map/ppermute | solution.py:1383
  63.3 3.3 %collective-permute-start = (bf16[11,64,512]{2,1,0:T(8,128)(2,1)}, bf16[11,64,512]{2,1,0:T(8,128)(2,1)S(1)}, u32[]{:S(2)}, u32[]{:S(2)}) collective-permute-start(bf16[11,64,512]{2,1,0:T(8,128)(2,1)} %get-tuple-element.38.shares_0_), channel_id=1, source_target_pairs={{0,1},{1,2},{2,0},{3,18},{18,19},{19,3},{4,5},{5,6},{6,4},{7,22},{... | collective-permute-start | bytes 2162696 | tf_op jit(solution)/shard_map/ppermute | solution.py:1383
  66.6 1.6 copy-done.1
  68.2 0.9 copy-done.5
  69.1 1.1 copy-done.7
  70.3 13.5 %target_values.1 = (bf16[6144,128]{1,0:T(8,128)(2,1)S(1)}, bf16[48,128]{1,0:T(8,128)(2,1)S(1)}, s32[2]{0:T(128)S(1)}) custom-call(bf16[32,96,128]{2,1,0:T(8,128)(2,1)S(1)} %copy-done.7, bf16[1024,1024]{1,0:T(8,128)(2,1)S(1)} %copy-done.1, f32[16,32,128]{2,1,0:T(8,128)S(1)} %copy-done.5), custom_call_target="tpu_custom_call" | custom-call | tf_op jit(solution)/shard_map/target_values/pallas_call | solution.py:724
  83.8 6.8 %share_values.1.q_ref = bf16[10,48,128]{2,1,0:T(8,128)(2,1)S(1)} custom-call(bf16[48,128]{1,0:T(8,128)(2,1)S(1)} %get-tuple-element.37.q_ref), custom_call_target="tpu_custom_call" | custom-call | tf_op jit(solution)/shard_map/share_values/pallas_call | solution.py:800
  90.7 0.0 copy-start
  90.7 0.0 copy-start.2
  90.7 0.0 copy-start.3
  90.7 44.3 %critic_step.1 = (f32[1024,1024]{1,0:T(8,128)S(1)}, bf16[1024,1024]{1,0:T(8,128)(2,1)S(1)}, f32[16,32,128]{2,1,0:T(8,128)S(1)}, f32[8,128]{1,0:T(8,128)S(1)}) custom-call(s32[2]{0:T(128)S(1)} %get-tuple-element.35.info_ref, bf16[6144,128]{1,0:T(8,128)(2,1)S(1)} %get-tuple-element.36.xc_ref, bf16[10,48,128]{2,1,0:T(8,128)(2,1)S(1)} %share_values.1.q_ref, ...), custom_call_target="tpu_custom_call" | custom-call | tf_op jit(solution)/shard_map/critic_step/pallas_call | solution.py:913
  135.1 0.0 copy-start.12
  135.1 0.0 copy-start.14
  135.1 0.0 copy-start.15
  135.1 0.0 copy-start.9
  135.1 0.0 copy-start.10
  135.1 0.0 copy-start.11
  135.1 0.0 copy-start.13
  135.1 0.0 copy-start.16
  135.2 61.2 %shampoo.1 = (f32[10,64,512]{2,1,0:T(8,128)S(1)}, f32[10,64,512]{2,1,0:T(8,128)S(1)}, f32[10,64,512]{2,1,0:T(8,128)S(1)}, f32[10,64,512]{2,1,0:T(8,128)S(1)}, f3...) custom-call(f32[1024,1024]{1,0:T(8,128)S(1)} %get-tuple-element.39.g_ref, ...), custom_call_target="tpu_custom_call" | custom-call | tf_op jit(solution)/shard_map/shampoo/pallas_call | solution.py:1309
  196.4 0.5 fusion.6
  196.9 0.6 multiply_subtract_fusion.1
  197.6 0.7 multiply_subtract_fusion
  198.2 0.6 multiply_subtract_fusion.2
  198.8 1.1 copy.46
  199.9 1.1 copy.47
  201.0 1.1 copy.48
  202.0 1.1 copy.49
  (25 shorter events, 0.1 us)
Async XLA Ops:
  61.0 29.6 %collective-permute-start.1 = (bf16[11,64,512]{2,1,0:T(8,128)(2,1)}, bf16[11,64,512]{2,1,0:T(8,128)(2,1)S(1)}, u32[]{:S(2)}, u32[]{:S(2)}) collective-permute-start(bf16[11,64,512]{2,1,0:T(8,128)(2,1)} %get-tuple-element.38.shares_0_), channel_id=1, source_target_pairs={{0,2},{1,0},{2,1},{3,19},{18,3},{19,18},{4,6},{5,4},{6,5},{7,23},{... | collective-permute-start | bytes 2162696 | tf_op jit(solution)/shard_map/ppermute | solution.py:1383
  63.3 27.3 %collective-permute-start = (bf16[11,64,512]{2,1,0:T(8,128)(2,1)}, bf16[11,64,512]{2,1,0:T(8,128)(2,1)S(1)}, u32[]{:S(2)}, u32[]{:S(2)}) collective-permute-start(bf16[11,64,512]{2,1,0:T(8,128)(2,1)} %get-tuple-element.38.shares_0_), channel_id=1, source_target_pairs={{0,1},{1,2},{2,0},{3,18},{18,19},{19,3},{4,5},{5,6},{6,4},{7,22},{... | collective-permute-start | bytes 2162696 | tf_op jit(solution)/shard_map/ppermute | solution.py:1383
  66.6 1.6 copy-start.1
  68.2 0.9 copy-start.5
  69.1 1.1 copy-start.7
  70.2 20.4 %copy-start.6 = (f32[16,32,128]{2,1,0:T(8,128)S(1)}, f32[16,32,128]{2,1,0:T(8,128)}, u32[]{:S(2)}) copy-start(f32[16,32,128]{2,1,0:T(8,128)} %get-tuple-element.34.p_ref) | copy-start | bytes 786436
  70.2 20.4 %copy-start.8 = (bf16[11,64,512]{2,1,0:T(8,128)(2,1)S(1)}, bf16[11,64,512]{2,1,0:T(8,128)(2,1)}, u32[]{:S(2)}) copy-start(bf16[11,64,512]{2,1,0:T(8,128)(2,1)} %get-tuple-element.38.shares_0_) | copy-start | bytes 2162692
  70.2 64.8 %copy-start.4 = (f32[10,64,512]{2,1,0:T(8,128)S(1)}, f32[10,64,512]{2,1,0:T(8,128)}, u32[]{:S(2)}) copy-start(f32[10,64,512]{2,1,0:T(8,128)} %right_ref.1) | copy-start | bytes 3932164
  90.7 44.4 %copy-start = (f32[10,64,512]{2,1,0:T(8,128)S(1)}, f32[10,64,512]{2,1,0:T(8,128)}, u32[]{:S(2)}) copy-start(f32[10,64,512]{2,1,0:T(8,128)} %w_ref.1) | copy-start | bytes 3932164
  90.7 44.4 %copy-start.2 = (f32[10,64,512]{2,1,0:T(8,128)S(1)}, f32[10,64,512]{2,1,0:T(8,128)}, u32[]{:S(2)}) copy-start(f32[10,64,512]{2,1,0:T(8,128)} %mom_ref.1) | copy-start | bytes 3932164
  90.7 44.4 %copy-start.3 = (f32[10,64,512]{2,1,0:T(8,128)S(1)}, f32[10,64,512]{2,1,0:T(8,128)}, u32[]{:S(2)}) copy-start(f32[10,64,512]{2,1,0:T(8,128)} %left_ref.1) | copy-start | bytes 3932164
  135.1 61.8 %copy-start.12 = (f32[4,320]{1,0:T(4,128)S(1)}, f32[4,320]{1,0:T(4,128)}, u32[]{:S(2)}) copy-start(f32[4,320]{1,0:T(4,128)} %inputs_3_.1) | copy-start | bytes 15364
  135.1 61.8 %copy-start.14 = (f32[4,320]{1,0:T(4,128)S(1)}, f32[4,320]{1,0:T(4,128)}, u32[]{:S(2)}) copy-start(f32[4,320]{1,0:T(4,128)} %param.42) | copy-start | bytes 15364
  135.1 61.8 %copy-start.15 = (f32[4,320]{1,0:T(4,128)S(1)}, f32[4,320]{1,0:T(4,128)}, u32[]{:S(2)}) copy-start(f32[4,320]{1,0:T(4,128)} %param.41) | copy-start | bytes 15364
  135.1 62.5 %copy-start.9 = (f32[23,320]{1,0:T(8,128)S(1)}, f32[23,320]{1,0:T(8,128)}, u32[]{:S(2)}) copy-start(f32[23,320]{1,0:T(8,128)} %inputs_2_.1) | copy-start | bytes 88324
  135.1 62.5 %copy-start.10 = (f32[23,320]{1,0:T(8,128)S(1)}, f32[23,320]{1,0:T(8,128)}, u32[]{:S(2)}) copy-start(f32[23,320]{1,0:T(8,128)} %param.39) | copy-start | bytes 88324
  135.1 62.4 %copy-start.11 = (f32[23,320]{1,0:T(8,128)S(1)}, f32[23,320]{1,0:T(8,128)}, u32[]{:S(2)}) copy-start(f32[23,320]{1,0:T(8,128)} %param.38) | copy-start | bytes 88324
  135.1 63.1 %copy-start.13 = (f32[320]{0:T(512)S(1)}, f32[320]{0:T(512)}, u32[]{:S(2)}) copy-start(f32[320]{0:T(512)} %param.43) | copy-start | bytes 3844
  135.1 63.1 %copy-start.16 = (f32[320]{0:T(512)S(1)}, f32[320]{0:T(512)}, u32[]{:S(2)}) copy-start(f32[320]{0:T(512)} %param.45) | copy-start | bytes 3844
  135.2 63.1 %copy-start.17 = (f32[320]{0:T(512)S(1)}, f32[320]{0:T(512)}, u32[]{:S(2)}) copy-start(f32[320]{0:T(512)} %param.44) | copy-start | bytes 3844

commit v6 on v5

--- a/solution.py
+++ b/solution.py
@@ -42,6 +42,7 @@
 L_VALID = 52
 L_CNT = 53
 MIB = 1024 * 1024
+TARGET_MIB = 28
 
 
 def nn(a, b):
@@ -240,8 +241,8 @@
     def first_hop(t, c):
         k = c * groups + index % groups
         dst = w_slot(index) if t == 0 else wc_ref.at[turn]
-        recv = recv_w.at[index] if t == 0 else recv_c.at[turn]
-        return k, dst, recv, to_worker(low.at[t, c], dst, send_w.at[t, c], recv, k)
+        recv = recv_w.at[turn] if t == 0 else recv_c.at[0]
+        return k, dst, recv, to_worker(low.at[t, c], dst, send_w.at[0], recv, k)
 
     def send_weights(t):
         def one(i, _):
@@ -368,7 +369,7 @@
     def row_hop(i):
         r = i % groups
         k = (2 * (i // groups) + index % 2) * groups + r
-        return r, k, to_worker(msg.at[r], x_ref.at[index], send_x.at[i], recv_x.at[index], k)
+        return r, k, to_worker(msg.at[r], x_ref.at[index], send_x.at[0], recv_x.at[index], k)
 
     hops = plan.sets * groups
 
@@ -393,7 +394,7 @@
 
     def pass_weight(t, i):
         s = group + groups * t
-        return to_worker(w_slot(s), w_slot(s), pass_w.at[t, i], recv_w.at[s], peer(i))
+        return to_worker(w_slot(s), w_slot(s), pass_w.at[i], recv_w.at[plan.turns + groups - 2 - i], peer(i))
 
     def pass_small(slot, i):
         return to_worker(p_ref.at[slot], p_ref.at[slot], pass_p.at[slot // groups, i], recv_p.at[slot], peer(i))
@@ -402,7 +403,7 @@
 
     def pass_rows(i, k, which):
         s = 2 * i + critic % 2
-        return to_worker(x_ref.at[s], x_ref.at[s], pass_x.at[i, which], recv_x.at[s], k)
+        return to_worker(x_ref.at[s], x_ref.at[s], pass_x.at[which], recv_x.at[plan.n], k)
 
     def other_rows(i):
         return pass_rows(i, (critic + 1 - 2 * (critic % 2)) * groups + group, 0)
@@ -410,8 +411,24 @@
     def extra_rows(i):
         return pass_rows(i, extra * groups + group, 1)
 
-    def arrived_w(s):
-        pltpu.make_async_copy(low.at[0, 0], w_slot(s), recv_w.at[s]).wait()
+    def arrived_w(t):
+        pltpu.make_async_copy(low.at[0, 0], w_slot(group + groups * t), recv_w.at[t]).wait()
+
+    def blocks_done(sem, number):
+        some = (plan.n - number + groups - 1) // groups
+
+        @pl.when(some == plan.turns)
+        def _():
+            pltpu.make_async_copy(wc_ref, wc_ref, sem).wait()
+
+        @pl.when(some != plan.turns)
+        def _():
+            fewer = wc_ref.at[pl.ds(0, plan.turns - 1)]
+            pltpu.make_async_copy(fewer, fewer, sem).wait()
+
+    def rows_done(sem, count):
+        some = x_ref.at[pl.ds(0, count)]
+        pltpu.make_async_copy(some, some, sem).wait()
 
     def arrived_x(s):
         pltpu.make_async_copy(msg.at[0], x_ref.at[s], recv_x.at[s]).wait()
@@ -439,7 +456,7 @@
 
             @pl.when(t < turns)
             def _():
-                arrived_w(group + groups * t)
+                arrived_w(t)
                 peers(lambda i: pass_weight(t, i).start())
 
         each(plan.turns, relay_weight)
@@ -464,16 +481,15 @@
 
         each(per, relay_small)
 
-        def arrived(s):
-            @pl.when(s % groups != group)
-            def _():
-                arrived_w(s)
-
-            @pl.when(jnp.logical_not(jnp.logical_and(passes_rows, s % 2 == critic % 2)))
-            def _():
-                arrived_x(s)
-
-        each(plan.n, arrived)
+        peers(lambda i: blocks_done(recv_w.at[plan.turns + i], (group + 1 + i) % groups))
+
+        @pl.when(passes_rows)
+        def _():
+            rows_done(recv_x.at[plan.n], plan.n // 2)
+
+        @pl.when(jnp.logical_not(passes_rows))
+        def _():
+            rows_done(recv_x.at[plan.n], plan.n)
 
         def arrived_small(slot):
             @pl.when((critic * per + slot) % groups != group)
@@ -481,19 +497,16 @@
                 arrived_p(slot)
 
         each(per, arrived_small)
-        each(turns, lambda t: pltpu.make_async_copy(low.at[1, 0], wc_ref.at[t], recv_c.at[t]).wait())
-        each(turns, lambda t: peers(lambda i: pass_weight(t, i).wait_send()))
+        blocks_done(recv_c.at[0], group)
+        peers(lambda i: blocks_done(pass_w.at[i], group))
 
         @pl.when(passes_rows)
         def _():
-            def passed_rows(i):
-                other_rows(i).wait_send()
-
-                @pl.when(extra >= 0)
-                def _():
-                    extra_rows(i).wait_send()
-
-            each(plan.n // 2, passed_rows)
+            rows_done(pass_x.at[0], plan.n // 2)
+
+            @pl.when(extra >= 0)
+            def _():
+                rows_done(pass_x.at[1], plan.n // 2)
 
         def passed_small(slot):
             @pl.when((critic * per + slot) % groups == group)
@@ -502,15 +515,16 @@
 
         each(per, passed_small)
 
-    def sent_weights(c):
-        for t in range(2):
-            k, _dst, _recv, copy = first_hop(t, c)
-
-            @pl.when(k != me)
-            def _():
-                copy.wait_send()
-
-    each(CRIT, sent_weights)
+    at_home = jnp.logical_and(me < workers, index % groups == group)
+
+    @pl.when(at_home)
+    def _():
+        sent = low.at[:, pl.ds(0, CRIT - 1)]
+        pltpu.make_async_copy(sent, sent, send_w.at[0]).wait()
+
+    @pl.when(jnp.logical_not(at_home))
+    def _():
+        pltpu.make_async_copy(low, low, send_w.at[0]).wait()
 
     def sent_small(j):
         k, _slot, copy = small_hop(j)
@@ -521,14 +535,15 @@
 
     each(mine, sent_small)
 
-    def sent_rows(i):
-        _r, k, copy = row_hop(i)
-
-        @pl.when(k != me)
-        def _():
-            copy.wait_send()
-
-    each(hops, sent_rows)
+    at_home_rows = jnp.logical_and(jnp.logical_and(me < workers, passes_rows), index % 2 == critic % 2)
+
+    @pl.when(at_home_rows)
+    def _():
+        rows_done(send_x.at[0], hops - 1)
+
+    @pl.when(jnp.logical_not(at_home_rows))
+    def _():
+        rows_done(send_x.at[0], hops)
 
 
 def dispatch(plan, inputs):
@@ -554,13 +569,13 @@
             pltpu.VMEM((plan.groups, pairs, LANES), BF16),
             pltpu.VMEM((2, 32, -(-columns // LANES) * LANES), F32),
             pltpu.VMEM((mine, 32, LANES), F32),
-            dma((2, CRIT)),
-            dma((plan.n,)),
-            dma((plan.turns, plan.groups - 1)),
-            dma((plan.turns,)),
-            dma((plan.sets * plan.groups,)),
-            dma((plan.n,)),
-            dma((plan.n // 2, 2)),
+            dma((1,)),
+            dma((plan.turns + plan.groups - 1,)),
+            dma((plan.groups - 1,)),
+            dma((1,)),
+            dma((1,)),
+            dma((plan.n + 1,)),
+            dma((2,)),
             dma((mine,)),
             dma((per,)),
             dma((-(-per // plan.groups), plan.groups - 1)),
@@ -743,7 +758,7 @@
             pltpu.SMEM((capacity // TILE,), I32),
             pltpu.SemaphoreType.DMA,
         ],
-        compiler_params=pltpu.CompilerParams(vmem_limit_bytes=28 * MIB),
+        compiler_params=pltpu.CompilerParams(vmem_limit_bytes=TARGET_MIB * MIB),
         name="target_values",
     )(x, weights, params)
 
@@ -967,6 +982,8 @@
     given,
     shares,
     totals,
+    sums_in,
+    sums_all,
     send_one,
     recv_one,
     send_two,
@@ -1024,8 +1041,15 @@
             small_ref.at[q], shares.at[group, g % mine], send_s.at[q], recv_s.at[group, g % mine], plan.device(s)
         )
 
-    def total_hop(s):
-        return to_device(sums_ref, totals.at[me], send_t.at[s], recv_t.at[me], plan.device(s))
+    def total_first(i):
+        k = critic * groups + (group + 1 + i) % groups
+        return to_device(sums_ref, sums_in.at[groups - 2 - i], send_t.at[i], recv_t.at[groups - 2 - i], plan.place(k))
+
+    def total_second(turn):
+        s = group + groups * turn
+        return s, to_device(
+            sums_all, totals.at[critic], send_t.at[groups - 1 + turn], recv_t.at[groups - 1 + critic], plan.device(s)
+        )
 
     def start_first(step):
         def one(i, _):
@@ -1055,18 +1079,34 @@
             return 0
 
         lax.fori_loop(0, per, start_small, 0)
-        totals[me] = sums_ref[...]
-
-        def start_total(i, _):
-            total_hop((index + i) % n).start()
+        for i in range(groups - 1):
+            pltpu.make_async_copy(sums_ref, sums_in.at[i], recv_t.at[i]).wait()
+        value = sums_ref[...]
+        for i in range(groups - 1):
+            value = value + jnp.where(iota((8, LANES), 0) == 0, sums_in[i], 0.0)
+        sums_all[...] = value
+
+        def start_total(turn, _):
+            s, copy = total_second(turn)
+
+            @pl.when(s == index)
+            def _():
+                totals[critic] = sums_all[...]
+
+            @pl.when(jnp.logical_and(s < n, s != index))
+            def _():
+                copy.start()
+
             return 0
 
-        lax.fori_loop(1, n, start_total, 0)
+        lax.fori_loop(0, turns, start_total, 0)
 
     @pl.when(me < workers)
     def _():
         for step in range(AHEAD):
             start_first(step)
+        for i in range(groups - 1):
+            total_first(i).start()
 
     def add_up(step):
         turn = turn_of(step)
@@ -1214,7 +1254,7 @@
             def _():
                 start_first(i + AHEAD)
 
-            @pl.when(i == LAG)
+            @pl.when(i == turns - 2)
             def _():
                 start_rest()
 
@@ -1247,14 +1287,14 @@
                 part = jnp.where(iota((32, LANES), 1) // chunk_width == turn // chunk_width, moved, part)
         own_ref[:, g * LANES : (g + 1) * LANES] = part
 
-    def arrived_total(k, _):
-        @pl.when(k != me)
+    def arrived_total(c, _):
+        @pl.when(c * groups + index % groups != me)
         def _():
-            pltpu.make_async_copy(sums_ref, totals.at[k], recv_t.at[k]).wait()
+            pltpu.make_async_copy(sums_ref, totals.at[c], recv_t.at[groups - 1 + c]).wait()
 
         return 0
 
-    lax.fori_loop(0, workers, arrived_total, 0)
+    lax.fori_loop(0, CRIT, arrived_total, 0)
     out_ref[0:1, :] = jnp.sum(totals[:, 0, :], 0, keepdims=True)
     out_ref[1:2, :] = totals[0, 1:2, :]
     out_ref[2:8, :] = jnp.zeros((6, LANES), F32)
@@ -1293,11 +1333,19 @@
 
         lax.fori_loop(0, per, finish_small, 0)
 
-        def finish_total(i, _):
-            total_hop((index + i) % n).wait_send()
+        for i in range(groups - 1):
+            total_first(i).wait_send()
+
+        def finish_total(turn, _):
+            s, copy = total_second(turn)
+
+            @pl.when(jnp.logical_and(s < n, s != index))
+            def _():
+                copy.wait_send()
+
             return 0
 
-        lax.fori_loop(1, n, finish_total, 0)
+        lax.fori_loop(0, turns, finish_total, 0)
 
 
 def shampoo(plan, columns, grad, lowered, small, sums, moment, left, right, weight):
@@ -1317,15 +1365,17 @@
             pltpu.VMEM((plan.turns,) + piece, BF16),
             pltpu.VMEM((CRIT,) + piece, BF16),
             pltpu.VMEM((plan.groups, mine, 32, LANES), F32),
-            pltpu.VMEM((plan.workers, 8, LANES), F32),
+            pltpu.VMEM((CRIT, 8, LANES), F32),
+            pltpu.VMEM((plan.groups - 1, 8, LANES), F32),
+            pltpu.VMEM((8, LANES), F32),
             dma((plan.turns, plan.groups - 1)),
             dma((plan.groups - 1, plan.turns)),
             dma((plan.turns,)),
             dma((CRIT,)),
             dma((per,)),
             dma((plan.groups, mine)),
-            dma((plan.n,)),
-            dma((plan.workers,)),
+            dma((plan.groups - 1 + plan.turns,)),
+            dma((plan.groups - 1 + CRIT,)),
         ],
         compiler_params=pltpu.CompilerParams(collective_id=2, has_side_effects=True, vmem_limit_bytes=24 * MIB),
         name="shampoo",
@@ -1339,6 +1389,35 @@
     square_hat = square_new / (1.0 - SECOND_DECAY**STEP)
     weight_new = weight - rate * (moment_hat / (jnp.sqrt(square_hat) + 1e-08) + WEIGHT_DECAY * weight)
     return (moment_new, square_new, weight_new)
+
+
+def finish_kernel(own_ref, weights, hidden, updated, stored, sems):
+    copies = [pltpu.make_async_copy(src, dst, sems.at[k]) for k, (src, dst) in enumerate(zip(hidden, stored))]
+    for copy in copies:
+        copy.start()
+    columns = weights[0].shape[1]
+    for k, (first, last, rate) in enumerate(((0, IN, RATE_INPUT), (IN, IN + 4, RATE_NORMS))):
+        grad = own_ref[first:last, 0:columns]
+        moment, square, weight = (weights[3 * k + j][...] for j in range(3))
+        for ref, value in zip(updated[3 * k : 3 * k + 3], adamw(grad, moment, square, weight, rate)):
+            ref[...] = value
+    for copy in copies:
+        copy.wait()
+
+
+def finish(own, weights, hidden):
+    vmem = pl.BlockSpec(memory_space=pltpu.VMEM)
+    anywhere = pl.BlockSpec(memory_space=pl.ANY)
+    shapes = lambda arrays: tuple(jax.ShapeDtypeStruct(v.shape, F32) for v in arrays)
+    return pl.pallas_call(
+        finish_kernel,
+        out_shape=(shapes(weights), shapes(hidden)),
+        in_specs=[vmem, (vmem,) * len(weights), (anywhere,) * len(hidden)],
+        out_specs=((vmem,) * len(weights), (anywhere,) * len(hidden)),
+        scratch_shapes=[pltpu.SemaphoreType.DMA((len(hidden),))],
+        compiler_params=pltpu.CompilerParams(vmem_limit_bytes=8 * MIB),
+        name="finish",
+    )(own, weights, hidden)
 
 
 def local(
@@ -1384,14 +1463,15 @@
     xc, q, info = target_values(plan, rows, width, x, w_target, params)
     q_all = share_values(plan, q)
     grad_hidden, lowered, grad_small, sums = critic_step(plan, width, info, xc, q_all, shares, params)
-    hidden_momentum, left_renewed, right_renewed, hidden_updated, own, totals = shampoo(
+    *hidden, own, totals = shampoo(
         plan, columns, grad_hidden, lowered, grad_small, sums, hidden_moment, left_stats, right_stats, critic_hidden
     )
-    own = own[:, :columns]
     loss_total, counted = totals[0, 0], totals[1, 0]
-    in_moment, in_square, in_updated = adamw(own[:IN], in_first, in_second, critic_in, RATE_INPUT)
-    norm_moment, norm_square, norm_updated = adamw(own[IN : IN + 4], norm_first, norm_second, critic_norms, RATE_NORMS)
-    head_moment, head_square, head_updated = adamw(own[IN + 4], head_first, head_second, critic_head, RATE_HEAD)
+    weights = (in_first, in_second, critic_in, norm_first, norm_second, critic_norms)
+    small, hidden = finish(own, weights, tuple(hidden))
+    in_moment, in_square, in_updated, norm_moment, norm_square, norm_updated = small
+    hidden_momentum, left_renewed, right_renewed, hidden_updated = hidden
+    head_moment, head_square, head_updated = adamw(own[IN + 4, :columns], head_first, head_second, critic_head, RATE_HEAD)
     return (
         loss_total,
         counted,

time: 202 us -> 196 us (0.970); the launches traced: 203 us -> 193 us
  local copies, waits for them, and re-layouts: 9.88 us -> 5.66 us
  Pallas kernels: 184 us -> 180 us
    pallas_call x1, Pallas kernels: 61.2 us -> 55.8 us  [shampoo(): pl.pallas_call(functools.partial(shampoo_kernel, plan), out_shape=(shape,...]
    unnamed x40 -> x36, local copies, waits for them, and re-layouts: 7.98 us -> 3.75 us
    pallas_call x0 -> x1, Pallas kernels: none -> 3.04 us  [finish(): pl.pallas_call(finish_kernel, out_shape=(shapes(weights), shapes(hidden))...]
  transfers between devices with their start and end apart: 2 -> 2, of which waited for: 0 -> 0; matrix products, arithmetic and copies ran while one was open for 0% -> 0% of each run, Pallas kernels for 10% -> 11%
where the time goes in v6:
time: 196 us; the launch traced here: 193 us
  Pallas kernels  180 us (92%)
  local copies, waits for them, and re-layouts  5.66 us (3%)
  starting transfers between devices  5.56 us (3%)
    pallas_call x1, Pallas kernels, dispatch(): pl.pallas_call(functools.partial(dispatch_kernel, plan), out_shape=(jax.S...  56.5 us
    pallas_call x1, Pallas kernels, shampoo(): pl.pallas_call(functools.partial(shampoo_kernel, plan), out_shape=(shape,...  55.8 us
    pallas_call x1, Pallas kernels, critic_step(): pl.pallas_call(functools.partial(critic_kernel, plan, width), out_shape=(...  44.2 us
    pallas_call x1, Pallas kernels, target_values(): pl.pallas_call(functools.partial(target_kernel, plan, width), out_shape=(...  13.5 us
    pallas_call x1, Pallas kernels, share_values(): pl.pallas_call(functools.partial(share_kernel, plan), out_shape=jax.Shape...  6.8 us
    ppermute x2, starting transfers between devices, local(): lax.ppermute(share, ('dp', 'mp'), plan.shift(k))  5.56 us
  transfers between devices with their start and end apart: 2, of which 0 were waited for; matrix products, arithmetic and copies ran while one was open for 0% of the time, Pallas kernels for 11%

profile of v6, /device:TPU:9, one launch (start us, length us, event | category | flops | bytes accessed | tf_op | source)
XLA Modules:
  0.0 193.4 jit_solution(17269792500877832772)
XLA Ops:
  0.6 0.7 stack.9
  1.3 0.7 stack.10
  2.0 0.6 pad_maximum_fusion.inputs_6_
  2.6 56.5 %dispatch.1 = (bf16[1024,1024]{1,0:T(8,128)(2,1)}, bf16[11,64,512]{2,1,0:T(8,128)(2,1)}, bf16[32,96,128]{2,1,0:T(8,128)(2,1)}, f32[16,32,128]{2,1,0:T(8,128)}) custom-call(f32[10,64,512]{2,1,0:T(8,128)} %w_ref.1, f32[10,64,512]{2,1,0:T(8,128)} %inputs_1_.1, f32[23,320]{1,0:T(8,128)} %weights_2_.1, f32[4,320]{1,0:T(4,128)} %weights_5_.1, ...), custom_call_target="tpu_custom_call" | custom-call | tf_op jit(solution)/shard_map/dispatch/pallas_call | solution.py:557
  59.1 2.3 %collective-permute-start.1 = (bf16[11,64,512]{2,1,0:T(8,128)(2,1)}, bf16[11,64,512]{2,1,0:T(8,128)(2,1)S(1)}, u32[]{:S(2)}, u32[]{:S(2)}) collective-permute-start(bf16[11,64,512]{2,1,0:T(8,128)(2,1)} %get-tuple-element.48.shares_0_), channel_id=1, source_target_pairs={{0,2},{1,0},{2,1},{3,19},{18,3},{19,18},{4,6},{5,4},{6,5},{7,23},{... | collective-permute-start | bytes 2162696 | tf_op jit(solution)/shard_map/ppermute | solution.py:1462
  61.5 3.2 %collective-permute-start = (bf16[11,64,512]{2,1,0:T(8,128)(2,1)}, bf16[11,64,512]{2,1,0:T(8,128)(2,1)S(1)}, u32[]{:S(2)}, u32[]{:S(2)}) collective-permute-start(bf16[11,64,512]{2,1,0:T(8,128)(2,1)} %get-tuple-element.48.shares_0_), channel_id=1, source_target_pairs={{0,1},{1,2},{2,0},{3,18},{18,19},{19,3},{4,5},{5,6},{6,4},{7,22},{... | collective-permute-start | bytes 2162696 | tf_op jit(solution)/shard_map/ppermute | solution.py:1462
  64.7 0.0 copy-start.1
  64.7 1.6 copy-done.1
  66.3 0.9 copy-done.5
  67.2 1.1 copy-done.7
  68.4 13.5 %target_values.1 = (bf16[6144,128]{1,0:T(8,128)(2,1)S(1)}, bf16[48,128]{1,0:T(8,128)(2,1)S(1)}, s32[2]{0:T(128)S(1)}) custom-call(bf16[32,96,128]{2,1,0:T(8,128)(2,1)S(1)} %copy-done.7, bf16[1024,1024]{1,0:T(8,128)(2,1)S(1)} %copy-done.1, f32[16,32,128]{2,1,0:T(8,128)S(1)} %copy-done.5), custom_call_target="tpu_custom_call" | custom-call | tf_op jit(solution)/shard_map/target_values/pallas_call | solution.py:739
  81.9 6.8 %share_values.1.q_ref = bf16[10,48,128]{2,1,0:T(8,128)(2,1)S(1)} custom-call(bf16[48,128]{1,0:T(8,128)(2,1)S(1)} %get-tuple-element.47.q_ref), custom_call_target="tpu_custom_call" | custom-call | tf_op jit(solution)/shard_map/share_values/pallas_call | solution.py:815
  88.7 0.0 collective-permute-done.1.shares_2_
  88.8 0.0 collective-permute-done.shares_1_
  88.8 0.0 copy-start
  88.8 0.0 copy-start.2
  88.8 0.0 copy-start.3
  88.8 44.2 %critic_step.1 = (f32[1024,1024]{1,0:T(8,128)S(1)}, bf16[1024,1024]{1,0:T(8,128)(2,1)S(1)}, f32[16,32,128]{2,1,0:T(8,128)S(1)}, f32[8,128]{1,0:T(8,128)S(1)}) custom-call(s32[2]{0:T(128)S(1)} %get-tuple-element.45.info_ref, bf16[6144,128]{1,0:T(8,128)(2,1)S(1)} %get-tuple-element.46.xc_ref, bf16[10,48,128]{2,1,0:T(8,128)(2,1)S(1)} %share_values.1.q_ref, ...), custom_call_target="tpu_custom_call" | custom-call | tf_op jit(solution)/shard_map/critic_step/pallas_call | solution.py:928
  133.1 0.0 copy-start.15
  133.1 0.0 copy-start.16
  133.1 0.0 copy-start.17
  133.1 0.0 copy-start.9
  133.2 0.0 copy-start.10
  133.2 0.0 copy-start.11
  133.2 0.0 copy-start.12
  133.2 0.0 copy-start.13
  133.2 0.0 copy-start.14
  133.2 55.8 %shampoo.1 = (f32[10,64,512]{2,1,0:T(8,128)S(1)}, f32[10,64,512]{2,1,0:T(8,128)S(1)}, f32[10,64,512]{2,1,0:T(8,128)S(1)}, f32[10,64,512]{2,1,0:T(8,128)S(1)}, f3...) custom-call(f32[1024,1024]{1,0:T(8,128)S(1)} %get-tuple-element.49.g_ref, ...), custom_call_target="tpu_custom_call" | custom-call | tf_op jit(solution)/shard_map/shampoo/pallas_call | solution.py:1357
  189.0 0.5 fusion.2
  189.6 0.6 multiply_subtract_fusion
  190.2 0.0 copy-done.10
  190.2 3.0 %finish.1 = (f32[23,320]{1,0:T(8,128)}, f32[23,320]{1,0:T(8,128)}, f32[23,320]{1,0:T(8,128)}, f32[4,320]{1,0:T(4,128)}, f32[4,320]{1,0:T(4,128)}, /*index=5*/f32...) custom-call(f32[32,384]{1,0:T(8,128)S(1)} %get-tuple-element.54.own_, ...), custom_call_target="tpu_custom_call" | custom-call | tf_op jit(solution)/shard_map/finish/pallas_call | solution.py:1412
  (20 shorter events, 0.1 us)
Async XLA Ops:
  59.1 29.6 %collective-permute-start.1 = (bf16[11,64,512]{2,1,0:T(8,128)(2,1)}, bf16[11,64,512]{2,1,0:T(8,128)(2,1)S(1)}, u32[]{:S(2)}, u32[]{:S(2)}) collective-permute-start(bf16[11,64,512]{2,1,0:T(8,128)(2,1)} %get-tuple-element.48.shares_0_), channel_id=1, source_target_pairs={{0,2},{1,0},{2,1},{3,19},{18,3},{19,18},{4,6},{5,4},{6,5},{7,23},{... | collective-permute-start | bytes 2162696 | tf_op jit(solution)/shard_map/ppermute | solution.py:1462
  61.5 27.3 %collective-permute-start = (bf16[11,64,512]{2,1,0:T(8,128)(2,1)}, bf16[11,64,512]{2,1,0:T(8,128)(2,1)S(1)}, u32[]{:S(2)}, u32[]{:S(2)}) collective-permute-start(bf16[11,64,512]{2,1,0:T(8,128)(2,1)} %get-tuple-element.48.shares_0_), channel_id=1, source_target_pairs={{0,1},{1,2},{2,0},{3,18},{18,19},{19,3},{4,5},{5,6},{6,4},{7,22},{... | collective-permute-start | bytes 2162696 | tf_op jit(solution)/shard_map/ppermute | solution.py:1462
  64.7 1.6 copy-start.1
  66.3 0.9 copy-start.5
  67.2 1.1 copy-start.7
  68.4 20.4 %copy-start.6 = (f32[16,32,128]{2,1,0:T(8,128)S(1)}, f32[16,32,128]{2,1,0:T(8,128)}, u32[]{:S(2)}) copy-start(f32[16,32,128]{2,1,0:T(8,128)} %get-tuple-element.44.p_ref) | copy-start | bytes 786436
  68.4 20.4 %copy-start.8 = (bf16[11,64,512]{2,1,0:T(8,128)(2,1)S(1)}, bf16[11,64,512]{2,1,0:T(8,128)(2,1)}, u32[]{:S(2)}) copy-start(bf16[11,64,512]{2,1,0:T(8,128)(2,1)} %get-tuple-element.48.shares_0_) | copy-start | bytes 2162692
  68.4 64.7 %copy-start.4 = (f32[10,64,512]{2,1,0:T(8,128)S(1)}, f32[10,64,512]{2,1,0:T(8,128)}, u32[]{:S(2)}) copy-start(f32[10,64,512]{2,1,0:T(8,128)} %right_ref.1) | copy-start | bytes 3932164
  88.8 44.3 %copy-start = (f32[10,64,512]{2,1,0:T(8,128)S(1)}, f32[10,64,512]{2,1,0:T(8,128)}, u32[]{:S(2)}) copy-start(f32[10,64,512]{2,1,0:T(8,128)} %w_ref.1) | copy-start | bytes 3932164
  88.8 44.3 %copy-start.2 = (f32[10,64,512]{2,1,0:T(8,128)S(1)}, f32[10,64,512]{2,1,0:T(8,128)}, u32[]{:S(2)}) copy-start(f32[10,64,512]{2,1,0:T(8,128)} %mom_ref.1) | copy-start | bytes 3932164
  88.8 44.3 %copy-start.3 = (f32[10,64,512]{2,1,0:T(8,128)S(1)}, f32[10,64,512]{2,1,0:T(8,128)}, u32[]{:S(2)}) copy-start(f32[10,64,512]{2,1,0:T(8,128)} %left_ref.1) | copy-start | bytes 3932164
  133.1 56.4 %copy-start.15 = (f32[320]{0:T(512)S(1)}, f32[320]{0:T(512)}, u32[]{:S(2)}) copy-start(f32[320]{0:T(512)} %param.43) | copy-start | bytes 3844
  133.1 56.4 %copy-start.16 = (f32[320]{0:T(512)S(1)}, f32[320]{0:T(512)}, u32[]{:S(2)}) copy-start(f32[320]{0:T(512)} %param.45) | copy-start | bytes 3844
  133.1 56.4 %copy-start.17 = (f32[320]{0:T(512)S(1)}, f32[320]{0:T(512)}, u32[]{:S(2)}) copy-start(f32[320]{0:T(512)} %param.44) | copy-start | bytes 3844
  133.1 57.0 %copy-start.9 = (f32[23,320]{1,0:T(8,128)S(1)}, f32[23,320]{1,0:T(8,128)}, u32[]{:S(2)}) copy-start(f32[23,320]{1,0:T(8,128)} %weights_2_.1) | copy-start | bytes 88324
  133.2 57.0 %copy-start.10 = (f32[23,320]{1,0:T(8,128)S(1)}, f32[23,320]{1,0:T(8,128)}, u32[]{:S(2)}) copy-start(f32[23,320]{1,0:T(8,128)} %weights_0_.1) | copy-start | bytes 88324
  133.2 57.0 %copy-start.11 = (f32[23,320]{1,0:T(8,128)S(1)}, f32[23,320]{1,0:T(8,128)}, u32[]{:S(2)}) copy-start(f32[23,320]{1,0:T(8,128)} %weights_1_.1) | copy-start | bytes 88324
  133.2 57.0 %copy-start.12 = (f32[4,320]{1,0:T(4,128)S(1)}, f32[4,320]{1,0:T(4,128)}, u32[]{:S(2)}) copy-start(f32[4,320]{1,0:T(4,128)} %weights_5_.1) | copy-start | bytes 15364
  133.2 57.0 %copy-start.13 = (f32[4,320]{1,0:T(4,128)S(1)}, f32[4,320]{1,0:T(4,128)}, u32[]{:S(2)}) copy-start(f32[4,320]{1,0:T(4,128)} %weights_3_.1) | copy-start | bytes 15364
  133.2 57.0 %copy-start.14 = (f32[4,320]{1,0:T(4,128)S(1)}, f32[4,320]{1,0:T(4,128)}, u32[]{:S(2)}) copy-start(f32[4,320]{1,0:T(4,128)} %weights_4_.1) | copy-start | bytes 15364

commit v7 on v6

--- a/solution.py
+++ b/solution.py
@@ -773,11 +773,10 @@
     @pl.when(me < plan.workers)
     def _():
         def peer(i):
-            other = (critic + i) % CRIT
-            return other, plan.place(other * groups + group)
+            return plan.place((critic + i) % CRIT * groups + group)
 
         def tell(i, _):
-            pl.semaphore_signal(barrier, inc=1, device_id=peer(i)[1], device_id_type=MESH)
+            pl.semaphore_signal(barrier, inc=1, device_id=peer(i), device_id_type=MESH)
             return 0
 
         lax.fori_loop(1, CRIT, tell, 0)
@@ -785,12 +784,12 @@
         all_ref[critic] = q_ref[...]
 
         def copy(i):
-            other, device = peer(i)
+            device = peer(i)
             return pltpu.make_async_remote_copy(
                 src_ref=q_ref,
                 dst_ref=all_ref.at[critic],
-                send_sem=send.at[other],
-                recv_sem=recv.at[critic],
+                send_sem=send,
+                recv_sem=recv,
                 device_id=device,
                 device_id_type=MESH,
             )
@@ -801,13 +800,9 @@
 
         lax.fori_loop(1, CRIT, start, 0)
 
-        def finish(i, _):
-            copy(i).wait_send()
-            other = peer(i)[0]
-            pltpu.make_async_copy(q_ref, all_ref.at[other], recv.at[other]).wait()
-            return 0
-
-        lax.fori_loop(1, CRIT, finish, 0)
+        others = all_ref.at[pl.ds(0, CRIT - 1)]
+        pltpu.make_async_copy(others, others, recv).wait()
+        pltpu.make_async_copy(others, others, send).wait()
 
 
 def share_values(plan, q):
@@ -817,7 +812,7 @@
         out_shape=jax.ShapeDtypeStruct((CRIT,) + q.shape, BF16),
         in_specs=[vmem],
         out_specs=vmem,
-        scratch_shapes=[pltpu.SemaphoreType.DMA((CRIT,)), pltpu.SemaphoreType.DMA((CRIT,))],
+        scratch_shapes=[pltpu.SemaphoreType.DMA, pltpu.SemaphoreType.DMA],
         compiler_params=pltpu.CompilerParams(collective_id=1, has_side_effects=True, vmem_limit_bytes=8 * MIB),
         name="share_values",
     )(q)
@@ -1024,7 +1019,7 @@
         copy = to_device(
             lowered_ref.at[block(s)],
             parts.at[groups - 2 - i, turn],
-            send_one.at[step, i],
+            send_one.at[i],
             recv_one.at[groups - 2 - i, turn],
             plan.place(critic * groups + other),
         )
@@ -1037,9 +1032,7 @@
     def small_hop(q):
         g = critic * per + q
         s = g // mine
-        return s, to_device(
-            small_ref.at[q], shares.at[group, g % mine], send_s.at[q], recv_s.at[group, g % mine], plan.device(s)
-        )
+        return s, to_device(small_ref.at[q], shares.at[group, g % mine], send_s.at[q], recv_s.at[0], plan.device(s))
 
     def total_first(i):
         k = critic * groups + (group + 1 + i) % groups
@@ -1070,7 +1063,7 @@
             @pl.when(s == index)
             def _():
                 slot = (critic * per + q) % mine
-                pltpu.make_async_copy(small_ref.at[q], shares.at[group, slot], recv_s.at[group, slot]).start()
+                pltpu.make_async_copy(small_ref.at[q], shares.at[group, slot], recv_s.at[0]).start()
 
             @pl.when(s != index)
             def _():
@@ -1270,11 +1263,7 @@
 
     lax.fori_loop(0, turns + LAG, round_, 0)
 
-    def arrived_small(i, _):
-        pltpu.make_async_copy(small_ref.at[0], shares.at[i // mine, i % mine], recv_s.at[i // mine, i % mine]).wait()
-        return 0
-
-    lax.fori_loop(0, groups * mine, arrived_small, 0)
+    pltpu.make_async_copy(shares, shares, recv_s.at[0]).wait()
     for g in range(columns // LANES):
         part = jnp.zeros((32, LANES), F32)
         for j in range(mine):
@@ -1301,18 +1290,20 @@
 
     @pl.when(me < workers)
     def _():
-        def finish(step, _):
-            def one(i, _):
-                s, copy = first_hop(step, i)
-
-                @pl.when(s < n)
-                def _():
-                    copy.wait_send()
-
-                return 0
-
-            lax.fori_loop(0, groups - 1, one, 0)
-            s, copy = second_hop(step)
+        for i in range(groups - 1):
+            some = (n - (group + 1 + i) % groups + groups - 1) // groups
+
+            @pl.when(some == turns)
+            def _():
+                pltpu.make_async_copy(parts.at[0], parts.at[0], send_one.at[i]).wait()
+
+            @pl.when(some != turns)
+            def _():
+                fewer = parts.at[0, pl.ds(0, turns - 1)]
+                pltpu.make_async_copy(fewer, fewer, send_one.at[i]).wait()
+
+        def finish(turn, _):
+            s, copy = second_hop(turn)
 
             @pl.when(jnp.logical_and(s < n, s != index))
             def _():
@@ -1368,12 +1359,12 @@
             pltpu.VMEM((CRIT, 8, LANES), F32),
             pltpu.VMEM((plan.groups - 1, 8, LANES), F32),
             pltpu.VMEM((8, LANES), F32),
-            dma((plan.turns, plan.groups - 1)),
+            dma((plan.groups - 1,)),
             dma((plan.groups - 1, plan.turns)),
             dma((plan.turns,)),
             dma((CRIT,)),
             dma((per,)),
-            dma((plan.groups, mine)),
+            dma((1,)),
             dma((plan.groups - 1 + plan.turns,)),
             dma((plan.groups - 1 + CRIT,)),
         ],

time: 196 us -> 194 us (0.990)
  transfers between devices with their start and end apart: 2 -> 2, of which waited for: 0 -> 0; matrix products, arithmetic and copies ran while one was open for 0% -> 0% of each run, Pallas kernels for 11% -> 10%
where the time goes in v7:
time: 194 us; the launch traced here: 192 us
  Pallas kernels  179 us (92%)
  local copies, waits for them, and re-layouts  5.66 us (3%)
  starting transfers between devices  5.56 us (3%)
    pallas_call x1, Pallas kernels, dispatch(): pl.pallas_call(functools.partial(dispatch_kernel, plan), out_shape=(jax.S...  56.5 us
    pallas_call x1, Pallas kernels, shampoo(): pl.pallas_call(functools.partial(shampoo_kernel, plan), out_shape=(shape,...  54.8 us
    pallas_call x1, Pallas kernels, critic_step(): pl.pallas_call(functools.partial(critic_kernel, plan, width), out_shape=(...  44.2 us
    pallas_call x1, Pallas kernels, target_values(): pl.pallas_call(functools.partial(target_kernel, plan, width), out_shape=(...  13.5 us
    pallas_call x1, Pallas kernels, share_values(): pl.pallas_call(functools.partial(share_kernel, plan), out_shape=jax.Shape...  6.62 us
    ppermute x2, starting transfers between devices, local(): lax.ppermute(share, ('dp', 'mp'), plan.shift(k))  5.56 us
  transfers between devices with their start and end apart: 2, of which 0 were waited for; matrix products, arithmetic and copies ran while one was open for 0% of the time, Pallas kernels for 10%

profile of v7, /device:TPU:9, one launch (start us, length us, event | category | flops | bytes accessed | tf_op | source)
XLA Modules:
  0.0 192.3 jit_solution(12299061203521955369)
XLA Ops:
  0.6 0.7 stack.9
  1.3 0.7 stack.10
  2.0 0.6 pad_maximum_fusion.inputs_6_
  2.6 56.5 %dispatch.1 = (bf16[1024,1024]{1,0:T(8,128)(2,1)}, bf16[11,64,512]{2,1,0:T(8,128)(2,1)}, bf16[32,96,128]{2,1,0:T(8,128)(2,1)}, f32[16,32,128]{2,1,0:T(8,128)}) custom-call(f32[10,64,512]{2,1,0:T(8,128)} %w_ref.1, f32[10,64,512]{2,1,0:T(8,128)} %inputs_1_.1, f32[23,320]{1,0:T(8,128)} %weights_2_.1, f32[4,320]{1,0:T(4,128)} %weights_5_.1, ...), custom_call_target="tpu_custom_call" | custom-call | tf_op jit(solution)/shard_map/dispatch/pallas_call | solution.py:557
  59.1 2.3 %collective-permute-start.1 = (bf16[11,64,512]{2,1,0:T(8,128)(2,1)}, bf16[11,64,512]{2,1,0:T(8,128)(2,1)S(1)}, u32[]{:S(2)}, u32[]{:S(2)}) collective-permute-start(bf16[11,64,512]{2,1,0:T(8,128)(2,1)} %get-tuple-element.48.shares_0_), channel_id=1, source_target_pairs={{0,2},{1,0},{2,1},{3,19},{18,3},{19,18},{4,6},{5,4},{6,5},{7,23},{... | collective-permute-start | bytes 2162696 | tf_op jit(solution)/shard_map/ppermute | solution.py:1453
  61.5 3.2 %collective-permute-start = (bf16[11,64,512]{2,1,0:T(8,128)(2,1)}, bf16[11,64,512]{2,1,0:T(8,128)(2,1)S(1)}, u32[]{:S(2)}, u32[]{:S(2)}) collective-permute-start(bf16[11,64,512]{2,1,0:T(8,128)(2,1)} %get-tuple-element.48.shares_0_), channel_id=1, source_target_pairs={{0,1},{1,2},{2,0},{3,18},{18,19},{19,3},{4,5},{5,6},{6,4},{7,22},{... | collective-permute-start | bytes 2162696 | tf_op jit(solution)/shard_map/ppermute | solution.py:1453
  64.7 1.6 copy-done.1
  66.3 0.9 copy-done.5
  67.2 1.1 copy-done.7
  68.4 13.5 %target_values.1 = (bf16[6144,128]{1,0:T(8,128)(2,1)S(1)}, bf16[48,128]{1,0:T(8,128)(2,1)S(1)}, s32[2]{0:T(128)S(1)}) custom-call(bf16[32,96,128]{2,1,0:T(8,128)(2,1)S(1)} %copy-done.7, bf16[1024,1024]{1,0:T(8,128)(2,1)S(1)} %copy-done.1, f32[16,32,128]{2,1,0:T(8,128)S(1)} %copy-done.5), custom_call_target="tpu_custom_call" | custom-call | tf_op jit(solution)/shard_map/target_values/pallas_call | solution.py:739
  81.9 6.6 %share_values.1.q_ref = bf16[10,48,128]{2,1,0:T(8,128)(2,1)S(1)} custom-call(bf16[48,128]{1,0:T(8,128)(2,1)S(1)} %get-tuple-element.47.q_ref), custom_call_target="tpu_custom_call" | custom-call | tf_op jit(solution)/shard_map/share_values/pallas_call | solution.py:810
  88.6 0.0 collective-permute-done.1.shares_2_
  88.6 0.0 collective-permute-done.shares_1_
  88.6 0.0 copy-start
  88.6 0.0 copy-start.2
  88.6 0.0 copy-start.3
  88.7 44.2 %critic_step.1 = (f32[1024,1024]{1,0:T(8,128)S(1)}, bf16[1024,1024]{1,0:T(8,128)(2,1)S(1)}, f32[16,32,128]{2,1,0:T(8,128)S(1)}, f32[8,128]{1,0:T(8,128)S(1)}) custom-call(s32[2]{0:T(128)S(1)} %get-tuple-element.45.info_ref, bf16[6144,128]{1,0:T(8,128)(2,1)S(1)} %get-tuple-element.46.xc_ref, bf16[10,48,128]{2,1,0:T(8,128)(2,1)S(1)} %share_values.1.q_ref, ...), custom_call_target="tpu_custom_call" | custom-call | tf_op jit(solution)/shard_map/critic_step/pallas_call | solution.py:923
  132.9 0.0 copy-start.15
  133.0 0.0 copy-start.16
  133.0 0.0 copy-start.17
  133.0 0.0 copy-start.9
  133.0 0.0 copy-start.10
  133.0 0.0 copy-start.11
  133.0 0.0 copy-start.12
  133.0 0.0 copy-start.13
  133.0 0.0 copy-start.14
  133.1 54.8 %shampoo.1 = (f32[10,64,512]{2,1,0:T(8,128)S(1)}, f32[10,64,512]{2,1,0:T(8,128)S(1)}, f32[10,64,512]{2,1,0:T(8,128)S(1)}, f32[10,64,512]{2,1,0:T(8,128)S(1)}, f3...) custom-call(f32[1024,1024]{1,0:T(8,128)S(1)} %get-tuple-element.49.g_ref, ...), custom_call_target="tpu_custom_call" | custom-call | tf_op jit(solution)/shard_map/shampoo/pallas_call | solution.py:1348
  187.9 0.5 fusion.2
  188.4 0.0 copy-done.15
  188.4 0.6 multiply_subtract_fusion
  189.0 0.0 copy-done.10
  189.1 3.0 %finish.1 = (f32[23,320]{1,0:T(8,128)}, f32[23,320]{1,0:T(8,128)}, f32[23,320]{1,0:T(8,128)}, f32[4,320]{1,0:T(4,128)}, f32[4,320]{1,0:T(4,128)}, /*index=5*/f32...) custom-call(f32[32,384]{1,0:T(8,128)S(1)} %get-tuple-element.54.own_, ...), custom_call_target="tpu_custom_call" | custom-call | tf_op jit(solution)/shard_map/finish/pallas_call | solution.py:1403
  (20 shorter events, 0.1 us)
Async XLA Ops:
  59.1 29.5 %collective-permute-start.1 = (bf16[11,64,512]{2,1,0:T(8,128)(2,1)}, bf16[11,64,512]{2,1,0:T(8,128)(2,1)S(1)}, u32[]{:S(2)}, u32[]{:S(2)}) collective-permute-start(bf16[11,64,512]{2,1,0:T(8,128)(2,1)} %get-tuple-element.48.shares_0_), channel_id=1, source_target_pairs={{0,2},{1,0},{2,1},{3,19},{18,3},{19,18},{4,6},{5,4},{6,5},{7,23},{... | collective-permute-start | bytes 2162696 | tf_op jit(solution)/shard_map/ppermute | solution.py:1453
  61.5 27.1 %collective-permute-start = (bf16[11,64,512]{2,1,0:T(8,128)(2,1)}, bf16[11,64,512]{2,1,0:T(8,128)(2,1)S(1)}, u32[]{:S(2)}, u32[]{:S(2)}) collective-permute-start(bf16[11,64,512]{2,1,0:T(8,128)(2,1)} %get-tuple-element.48.shares_0_), channel_id=1, source_target_pairs={{0,1},{1,2},{2,0},{3,18},{18,19},{19,3},{4,5},{5,6},{6,4},{7,22},{... | collective-permute-start | bytes 2162696 | tf_op jit(solution)/shard_map/ppermute | solution.py:1453
  64.7 1.6 copy-start.1
  66.3 0.9 copy-start.5
  67.2 1.1 copy-start.7
  68.4 20.2 %copy-start.6 = (f32[16,32,128]{2,1,0:T(8,128)S(1)}, f32[16,32,128]{2,1,0:T(8,128)}, u32[]{:S(2)}) copy-start(f32[16,32,128]{2,1,0:T(8,128)} %get-tuple-element.44.p_ref) | copy-start | bytes 786436
  68.4 20.2 %copy-start.8 = (bf16[11,64,512]{2,1,0:T(8,128)(2,1)S(1)}, bf16[11,64,512]{2,1,0:T(8,128)(2,1)}, u32[]{:S(2)}) copy-start(bf16[11,64,512]{2,1,0:T(8,128)(2,1)} %get-tuple-element.48.shares_0_) | copy-start | bytes 2162692
  68.4 64.5 %copy-start.4 = (f32[10,64,512]{2,1,0:T(8,128)S(1)}, f32[10,64,512]{2,1,0:T(8,128)}, u32[]{:S(2)}) copy-start(f32[10,64,512]{2,1,0:T(8,128)} %right_ref.1) | copy-start | bytes 3932164
  88.6 44.3 %copy-start = (f32[10,64,512]{2,1,0:T(8,128)S(1)}, f32[10,64,512]{2,1,0:T(8,128)}, u32[]{:S(2)}) copy-start(f32[10,64,512]{2,1,0:T(8,128)} %w_ref.1) | copy-start | bytes 3932164
  88.6 44.3 %copy-start.2 = (f32[10,64,512]{2,1,0:T(8,128)S(1)}, f32[10,64,512]{2,1,0:T(8,128)}, u32[]{:S(2)}) copy-start(f32[10,64,512]{2,1,0:T(8,128)} %mom_ref.1) | copy-start | bytes 3932164
  88.6 44.3 %copy-start.3 = (f32[10,64,512]{2,1,0:T(8,128)S(1)}, f32[10,64,512]{2,1,0:T(8,128)}, u32[]{:S(2)}) copy-start(f32[10,64,512]{2,1,0:T(8,128)} %left_ref.1) | copy-start | bytes 3932164
  132.9 55.5 %copy-start.15 = (f32[320]{0:T(512)S(1)}, f32[320]{0:T(512)}, u32[]{:S(2)}) copy-start(f32[320]{0:T(512)} %param.43) | copy-start | bytes 3844
  133.0 55.5 %copy-start.16 = (f32[320]{0:T(512)S(1)}, f32[320]{0:T(512)}, u32[]{:S(2)}) copy-start(f32[320]{0:T(512)} %param.45) | copy-start | bytes 3844
  133.0 55.5 %copy-start.17 = (f32[320]{0:T(512)S(1)}, f32[320]{0:T(512)}, u32[]{:S(2)}) copy-start(f32[320]{0:T(512)} %param.44) | copy-start | bytes 3844
  133.0 56.1 %copy-start.9 = (f32[23,320]{1,0:T(8,128)S(1)}, f32[23,320]{1,0:T(8,128)}, u32[]{:S(2)}) copy-start(f32[23,320]{1,0:T(8,128)} %weights_2_.1) | copy-start | bytes 88324
  133.0 56.0 %copy-start.10 = (f32[23,320]{1,0:T(8,128)S(1)}, f32[23,320]{1,0:T(8,128)}, u32[]{:S(2)}) copy-start(f32[23,320]{1,0:T(8,128)} %weights_0_.1) | copy-start | bytes 88324
  133.0 56.0 %copy-start.11 = (f32[23,320]{1,0:T(8,128)S(1)}, f32[23,320]{1,0:T(8,128)}, u32[]{:S(2)}) copy-start(f32[23,320]{1,0:T(8,128)} %weights_1_.1) | copy-start | bytes 88324
  133.0 56.0 %copy-start.12 = (f32[4,320]{1,0:T(4,128)S(1)}, f32[4,320]{1,0:T(4,128)}, u32[]{:S(2)}) copy-start(f32[4,320]{1,0:T(4,128)} %weights_5_.1) | copy-start | bytes 15364
  133.0 56.0 %copy-start.13 = (f32[4,320]{1,0:T(4,128)S(1)}, f32[4,320]{1,0:T(4,128)}, u32[]{:S(2)}) copy-start(f32[4,320]{1,0:T(4,128)} %weights_3_.1) | copy-start | bytes 15364
  133.0 56.0 %copy-start.14 = (f32[4,320]{1,0:T(4,128)S(1)}, f32[4,320]{1,0:T(4,128)}, u32[]{:S(2)}) copy-start(f32[4,320]{1,0:T(4,128)} %weights_4_.1) | copy-start | bytes 15364

commit v8 on v7

--- a/solution.py
+++ b/solution.py
@@ -949,7 +949,7 @@
     )(info, xc, q_all, shares, params)
 
 
-PRECISE = 2
+PRECISE = 1
 
 
 LAG = 3

time: 194 us -> 192 us (0.990)
  Pallas kernels: 179 us -> 176 us
    pallas_call x1, Pallas kernels: 54.8 us -> 52.3 us  [shampoo(): pl.pallas_call(functools.partial(shampoo_kernel, plan), out_shape=(shape,...]
  transfers between devices with their start and end apart: 2 -> 2, of which waited for: 0 -> 0; matrix products, arithmetic and copies ran while one was open for 0% -> 0% of each run, Pallas kernels for 10% -> 11%
where the time goes in v8:
time: 192 us; the launch traced here: 190 us
  Pallas kernels  176 us (92%)
  local copies, waits for them, and re-layouts  5.66 us (3%)
  starting transfers between devices  5.56 us (3%)
    pallas_call x1, Pallas kernels, dispatch(): pl.pallas_call(functools.partial(dispatch_kernel, plan), out_shape=(jax.S...  56.5 us
    pallas_call x1, Pallas kernels, shampoo(): pl.pallas_call(functools.partial(shampoo_kernel, plan), out_shape=(shape,...  52.3 us
    pallas_call x1, Pallas kernels, critic_step(): pl.pallas_call(functools.partial(critic_kernel, plan, width), out_shape=(...  44.2 us
    pallas_call x1, Pallas kernels, target_values(): pl.pallas_call(functools.partial(target_kernel, plan, width), out_shape=(...  13.5 us
    pallas_call x1, Pallas kernels, share_values(): pl.pallas_call(functools.partial(share_kernel, plan), out_shape=jax.Shape...  6.62 us
    ppermute x2, starting transfers between devices, local(): lax.ppermute(share, ('dp', 'mp'), plan.shift(k))  5.56 us
  transfers between devices with their start and end apart: 2, of which 0 were waited for; matrix products, arithmetic and copies ran while one was open for 0% of the time, Pallas kernels for 11%

profile of v8, /device:TPU:9, one launch (start us, length us, event | category | flops | bytes accessed | tf_op | source)
XLA Modules:
  0.0 189.8 jit_solution(4446039352453861208)
XLA Ops:
  0.6 0.7 stack.9
  1.3 0.7 stack.10
  2.0 0.6 pad_maximum_fusion.inputs_6_
  2.6 56.5 %dispatch.1 = (bf16[1024,1024]{1,0:T(8,128)(2,1)}, bf16[11,64,512]{2,1,0:T(8,128)(2,1)}, bf16[32,96,128]{2,1,0:T(8,128)(2,1)}, f32[16,32,128]{2,1,0:T(8,128)}) custom-call(f32[10,64,512]{2,1,0:T(8,128)} %w_ref.1, f32[10,64,512]{2,1,0:T(8,128)} %inputs_1_.1, f32[23,320]{1,0:T(8,128)} %weights_2_.1, f32[4,320]{1,0:T(4,128)} %weights_5_.1, ...), custom_call_target="tpu_custom_call" | custom-call | tf_op jit(solution)/shard_map/dispatch/pallas_call | solution.py:557
  59.1 2.3 %collective-permute-start.1 = (bf16[11,64,512]{2,1,0:T(8,128)(2,1)}, bf16[11,64,512]{2,1,0:T(8,128)(2,1)S(1)}, u32[]{:S(2)}, u32[]{:S(2)}) collective-permute-start(bf16[11,64,512]{2,1,0:T(8,128)(2,1)} %get-tuple-element.48.shares_0_), channel_id=1, source_target_pairs={{0,2},{1,0},{2,1},{3,19},{18,3},{19,18},{4,6},{5,4},{6,5},{7,23},{... | collective-permute-start | bytes 2162696 | tf_op jit(solution)/shard_map/ppermute | solution.py:1453
  61.5 3.2 %collective-permute-start = (bf16[11,64,512]{2,1,0:T(8,128)(2,1)}, bf16[11,64,512]{2,1,0:T(8,128)(2,1)S(1)}, u32[]{:S(2)}, u32[]{:S(2)}) collective-permute-start(bf16[11,64,512]{2,1,0:T(8,128)(2,1)} %get-tuple-element.48.shares_0_), channel_id=1, source_target_pairs={{0,1},{1,2},{2,0},{3,18},{18,19},{19,3},{4,5},{5,6},{6,4},{7,22},{... | collective-permute-start | bytes 2162696 | tf_op jit(solution)/shard_map/ppermute | solution.py:1453
  64.7 1.6 copy-done.1
  66.3 0.9 copy-done.5
  67.2 1.1 copy-done.7
  68.4 13.5 %target_values.1 = (bf16[6144,128]{1,0:T(8,128)(2,1)S(1)}, bf16[48,128]{1,0:T(8,128)(2,1)S(1)}, s32[2]{0:T(128)S(1)}) custom-call(bf16[32,96,128]{2,1,0:T(8,128)(2,1)S(1)} %copy-done.7, bf16[1024,1024]{1,0:T(8,128)(2,1)S(1)} %copy-done.1, f32[16,32,128]{2,1,0:T(8,128)S(1)} %copy-done.5), custom_call_target="tpu_custom_call" | custom-call | tf_op jit(solution)/shard_map/target_values/pallas_call | solution.py:739
  81.9 6.6 %share_values.1.q_ref = bf16[10,48,128]{2,1,0:T(8,128)(2,1)S(1)} custom-call(bf16[48,128]{1,0:T(8,128)(2,1)S(1)} %get-tuple-element.47.q_ref), custom_call_target="tpu_custom_call" | custom-call | tf_op jit(solution)/shard_map/share_values/pallas_call | solution.py:810
  88.6 0.0 collective-permute-done.1.shares_2_
  88.6 0.0 collective-permute-done.shares_1_
  88.6 0.0 copy-start
  88.6 0.0 copy-start.2
  88.6 0.0 copy-start.3
  88.7 44.2 %critic_step.1 = (f32[1024,1024]{1,0:T(8,128)S(1)}, bf16[1024,1024]{1,0:T(8,128)(2,1)S(1)}, f32[16,32,128]{2,1,0:T(8,128)S(1)}, f32[8,128]{1,0:T(8,128)S(1)}) custom-call(s32[2]{0:T(128)S(1)} %get-tuple-element.45.info_ref, bf16[6144,128]{1,0:T(8,128)(2,1)S(1)} %get-tuple-element.46.xc_ref, bf16[10,48,128]{2,1,0:T(8,128)(2,1)S(1)} %share_values.1.q_ref, ...), custom_call_target="tpu_custom_call" | custom-call | tf_op jit(solution)/shard_map/critic_step/pallas_call | solution.py:923
  132.9 0.0 copy-done.4
  132.9 0.0 copy-done
  132.9 0.0 copy-start.15
  133.0 0.0 copy-start.16
  133.0 0.0 copy-start.17
  133.0 0.0 copy-start.9
  133.0 0.0 copy-start.10
  133.0 0.0 copy-start.11
  133.0 0.0 copy-start.12
  133.0 0.0 copy-start.13
  133.0 0.0 copy-start.14
  133.0 52.3 %shampoo.1 = (f32[10,64,512]{2,1,0:T(8,128)S(1)}, f32[10,64,512]{2,1,0:T(8,128)S(1)}, f32[10,64,512]{2,1,0:T(8,128)S(1)}, f32[10,64,512]{2,1,0:T(8,128)S(1)}, f3...) custom-call(f32[1024,1024]{1,0:T(8,128)S(1)} %get-tuple-element.49.g_ref, ...), custom_call_target="tpu_custom_call" | custom-call | tf_op jit(solution)/shard_map/shampoo/pallas_call | solution.py:1348
  185.4 0.5 fusion.2
  186.0 0.6 multiply_subtract_fusion
  186.6 3.0 %finish.1 = (f32[23,320]{1,0:T(8,128)}, f32[23,320]{1,0:T(8,128)}, f32[23,320]{1,0:T(8,128)}, f32[4,320]{1,0:T(4,128)}, f32[4,320]{1,0:T(4,128)}, /*index=5*/f32...) custom-call(f32[32,384]{1,0:T(8,128)S(1)} %get-tuple-element.54.own_, ...), custom_call_target="tpu_custom_call" | custom-call | tf_op jit(solution)/shard_map/finish/pallas_call | solution.py:1403
  (20 shorter events, 0.1 us)
Async XLA Ops:
  59.1 29.5 %collective-permute-start.1 = (bf16[11,64,512]{2,1,0:T(8,128)(2,1)}, bf16[11,64,512]{2,1,0:T(8,128)(2,1)S(1)}, u32[]{:S(2)}, u32[]{:S(2)}) collective-permute-start(bf16[11,64,512]{2,1,0:T(8,128)(2,1)} %get-tuple-element.48.shares_0_), channel_id=1, source_target_pairs={{0,2},{1,0},{2,1},{3,19},{18,3},{19,18},{4,6},{5,4},{6,5},{7,23},{... | collective-permute-start | bytes 2162696 | tf_op jit(solution)/shard_map/ppermute | solution.py:1453
  61.5 27.1 %collective-permute-start = (bf16[11,64,512]{2,1,0:T(8,128)(2,1)}, bf16[11,64,512]{2,1,0:T(8,128)(2,1)S(1)}, u32[]{:S(2)}, u32[]{:S(2)}) collective-permute-start(bf16[11,64,512]{2,1,0:T(8,128)(2,1)} %get-tuple-element.48.shares_0_), channel_id=1, source_target_pairs={{0,1},{1,2},{2,0},{3,18},{18,19},{19,3},{4,5},{5,6},{6,4},{7,22},{... | collective-permute-start | bytes 2162696 | tf_op jit(solution)/shard_map/ppermute | solution.py:1453
  64.7 1.6 copy-start.1
  66.3 0.9 copy-start.5
  67.2 1.1 copy-start.7
  68.4 20.2 %copy-start.6 = (f32[16,32,128]{2,1,0:T(8,128)S(1)}, f32[16,32,128]{2,1,0:T(8,128)}, u32[]{:S(2)}) copy-start(f32[16,32,128]{2,1,0:T(8,128)} %get-tuple-element.44.p_ref) | copy-start | bytes 786436
  68.4 20.2 %copy-start.8 = (bf16[11,64,512]{2,1,0:T(8,128)(2,1)S(1)}, bf16[11,64,512]{2,1,0:T(8,128)(2,1)}, u32[]{:S(2)}) copy-start(bf16[11,64,512]{2,1,0:T(8,128)(2,1)} %get-tuple-element.48.shares_0_) | copy-start | bytes 2162692
  68.4 64.5 %copy-start.4 = (f32[10,64,512]{2,1,0:T(8,128)S(1)}, f32[10,64,512]{2,1,0:T(8,128)}, u32[]{:S(2)}) copy-start(f32[10,64,512]{2,1,0:T(8,128)} %right_ref.1) | copy-start | bytes 3932164
  88.6 44.3 %copy-start = (f32[10,64,512]{2,1,0:T(8,128)S(1)}, f32[10,64,512]{2,1,0:T(8,128)}, u32[]{:S(2)}) copy-start(f32[10,64,512]{2,1,0:T(8,128)} %w_ref.1) | copy-start | bytes 3932164
  88.6 44.3 %copy-start.2 = (f32[10,64,512]{2,1,0:T(8,128)S(1)}, f32[10,64,512]{2,1,0:T(8,128)}, u32[]{:S(2)}) copy-start(f32[10,64,512]{2,1,0:T(8,128)} %mom_ref.1) | copy-start | bytes 3932164
  88.6 44.3 %copy-start.3 = (f32[10,64,512]{2,1,0:T(8,128)S(1)}, f32[10,64,512]{2,1,0:T(8,128)}, u32[]{:S(2)}) copy-start(f32[10,64,512]{2,1,0:T(8,128)} %left_ref.1) | copy-start | bytes 3932164
  132.9 53.0 %copy-start.15 = (f32[320]{0:T(512)S(1)}, f32[320]{0:T(512)}, u32[]{:S(2)}) copy-start(f32[320]{0:T(512)} %param.43) | copy-start | bytes 3844
  133.0 53.0 %copy-start.16 = (f32[320]{0:T(512)S(1)}, f32[320]{0:T(512)}, u32[]{:S(2)}) copy-start(f32[320]{0:T(512)} %param.45) | copy-start | bytes 3844
  133.0 53.0 %copy-start.17 = (f32[320]{0:T(512)S(1)}, f32[320]{0:T(512)}, u32[]{:S(2)}) copy-start(f32[320]{0:T(512)} %param.44) | copy-start | bytes 3844
  133.0 53.6 %copy-start.9 = (f32[23,320]{1,0:T(8,128)S(1)}, f32[23,320]{1,0:T(8,128)}, u32[]{:S(2)}) copy-start(f32[23,320]{1,0:T(8,128)} %weights_2_.1) | copy-start | bytes 88324
  133.0 53.6 %copy-start.10 = (f32[23,320]{1,0:T(8,128)S(1)}, f32[23,320]{1,0:T(8,128)}, u32[]{:S(2)}) copy-start(f32[23,320]{1,0:T(8,128)} %weights_0_.1) | copy-start | bytes 88324
  133.0 53.6 %copy-start.11 = (f32[23,320]{1,0:T(8,128)S(1)}, f32[23,320]{1,0:T(8,128)}, u32[]{:S(2)}) copy-start(f32[23,320]{1,0:T(8,128)} %weights_1_.1) | copy-start | bytes 88324
  133.0 53.6 %copy-start.12 = (f32[4,320]{1,0:T(4,128)S(1)}, f32[4,320]{1,0:T(4,128)}, u32[]{:S(2)}) copy-start(f32[4,320]{1,0:T(4,128)} %weights_5_.1) | copy-start | bytes 15364
  133.0 53.6 %copy-start.13 = (f32[4,320]{1,0:T(4,128)S(1)}, f32[4,320]{1,0:T(4,128)}, u32[]{:S(2)}) copy-start(f32[4,320]{1,0:T(4,128)} %weights_3_.1) | copy-start | bytes 15364
  133.0 53.6 %copy-start.14 = (f32[4,320]{1,0:T(4,128)S(1)}, f32[4,320]{1,0:T(4,128)}, u32[]{:S(2)}) copy-start(f32[4,320]{1,0:T(4,128)} %weights_4_.1) | copy-start | bytes 15364
